TPU v7x, 32 devices: a whole 2x2x4 slice. The times are simulated.
32 devices in a mesh: section: 2 (over x), stream: 16 (over z, y, core).
Axes of the slice: x: 2, y: 2, z: 4, core: 2. Of those that a mesh axis runs over, the one named last changes fastest.
Arguments:
- tokens: bfloat16 [32, 64, 1024], P('stream'), may hold values from -6 to 6
- doc_ids: int32 [32, 448], P('stream'), may hold values from 0 to 3, never falling along the last dimension, each value on 1 to 224 neighbouring positions
- memory: bfloat16 [2, 32, 256, 1024], P('section', 'stream'), may hold values from -6 to 6
- compressed: bfloat16 [2, 32, 128, 1024], P('section', 'stream'), may hold values from -6 to 6
- cot_out: bfloat16 [32, 64, 1024], P('stream'), may hold values from -6 to 6
- cot_comp: bfloat16 [2, 32, 21, 1024], P('section', 'stream'), may hold values from -6 to 6
- attn_in: float32 [2, 1024, 3072], P('section', 'stream'), may hold values from -0.1875 to 0.1875
- attn_out: float32 [2, 1024, 1024], P('section', 'stream'), may hold values from -0.5 to 0.5
- rel_proj: float32 [2, 1024, 1024], P('section', 'stream'), may hold values from -0.1875 to 0.1875
- ff_in: float32 [2, 1024, 4096], P('section', 'stream'), may hold values from -0.1875 to 0.1875
- ff_out: float32 [2, 4096, 1024], P('section', 'stream'), may hold values from -0.09375 to 0.09375
- compress: float32 [2, 3072, 1024], P('section', 'stream'), may hold values from -0.109375 to 0.109375
- gains: float32 [2, 1024, 2], P('section', 'stream'), may hold values from 0.25 to 1.75
- biases: float32 [2, 1024, 4], P('section', 'stream'), may hold values from -3 to 3
- pos_bias: float32 [2, 1024, 2], P('section', 'stream'), may hold values from -3 to 3
- ff_bias: float32 [2, 4096], P('section', 'stream'), may hold values from -3 to 3
Outputs:
- activations: bfloat16 [2, 32, 64, 1024], P('section', 'stream')
- new_memory: bfloat16 [2, 32, 256, 1024], P('section', 'stream')
- new_compressed: bfloat16 [2, 32, 128, 1024], P('section', 'stream')
- input_grad: float32 [2, 32, 64, 1024], P('section', 'stream')
- grad_attn_in: float32 [2, 1024, 3072], P('section', 'stream')
- grad_attn_out: float32 [2, 1024, 1024], P('section', 'stream')
- grad_rel_proj: float32 [2, 1024, 1024], P('section', 'stream')
- grad_ff_in: float32 [2, 1024, 4096], P('section', 'stream')
- grad_ff_out: float32 [2, 4096, 1024], P('section', 'stream')
- grad_compress: float32 [2, 3072, 1024], P('section', 'stream')
- grad_gains: float32 [2, 1024, 2], P('section', 'stream')
- grad_biases: float32 [2, 1024, 4], P('section', 'stream')
- grad_pos_bias: float32 [2, 1024, 2], P('section', 'stream')
- grad_ff_bias: float32 [2, 4096], P('section', 'stream')
Inputs may be any that keep to these rules, and one draw needn't show every extreme that they name: `doc_ids`: along each row the document numbers never fall; positions 0 to 127 are the compressed slots, then 256 memory slots, then the 64 tokens of the segment.
All inputs are finite; a program needn't handle non-finite values.
Results may differ from a plain program's by a relative error of at most 0.028.
Values may be sent and summed in bfloat16 or wider, within the bound.
No kernel may reach another device: no remote copies, remote signals or barrier semaphores. Data moves between devices by JAX's collectives and lax.ppermute only.
A program may use at most 448 MiB of HBM per device.

v0:
```python
import math

import jax
import jax.numpy as jnp
from jax import lax
from jax.sharding import PartitionSpec as P

HEADS = 8
CNEW = 21


def as_sent(shard):
    return jax.tree.map(lambda a: a.astype(jnp.bfloat16) if a.dtype == jnp.float32 else a, shard)


def from_behind(shard, axis, by):
    size = lax.axis_size(axis)
    pairs = [(i, i + by) for i in range(size) if 0 <= i + by < size]
    return lax.ppermute(shard, axis, pairs)


def value_plain(value):
    return lax.optimization_barrier(value.astype(jnp.bfloat16)).astype(jnp.float32)


def make_rounders():
    round_value = jax.custom_vjp(value_plain)

    def value_keep(value):
        return (value_plain(value), None)

    def value_pass(kept, grad):
        return (grad,)

    round_value.defvjp(value_keep, value_pass)

    def grad_plain(value):
        return value

    round_grad = jax.custom_vjp(grad_plain)

    def grad_keep(value):
        return (value, None)

    def grad_round(kept, grad):
        return (value_plain(grad),)

    round_grad.defvjp(grad_keep, grad_round)
    return (round_value, round_grad)


def matmul(first_op, second_op):
    if second_op.dtype == jnp.bfloat16:
        return jnp.dot(first_op.astype(jnp.bfloat16), second_op, preferred_element_type=jnp.float32)
    return jnp.dot(first_op, second_op, preferred_element_type=jnp.float32)


def layer_norm(values, gain_vec, bias_vec):
    mean_value = jnp.mean(values, -1, keepdims=True)
    centred = values - mean_value
    spread = jnp.mean(centred * centred, -1, keepdims=True)
    return centred * lax.rsqrt(spread + 1e-05) * gain_vec + bias_vec


def gelu_tanh(values):
    return (
        0.5
        * values
        * (1.0 + jnp.tanh(0.7978845608028654 * (values + 0.044715 * values * values * values)))
    )


def sinusoid(key_count, model_width):
    offsets = jnp.arange(key_count, dtype=jnp.float32)[:, None]
    inverse_rate = jnp.exp(
        jnp.arange(model_width // 2, dtype=jnp.float32) * (-2.0 * math.log(10000.0) / model_width)
    )
    angles = offsets * inverse_rate[None, :]
    return jnp.concatenate([jnp.sin(angles), jnp.cos(angles)], 1)


def skew_rows(reversed_scores):
    head_count, seg_len, key_len = reversed_scores.shape
    padded = jnp.pad(reversed_scores, ((0, 0), (0, 0), (0, 1))).reshape(
        head_count, seg_len * (key_len + 1)
    )
    return padded[:, seg_len - 1 : seg_len - 1 + seg_len * key_len].reshape(
        head_count, seg_len, key_len
    )


def layer(weights, hidden, mem_rows, comp_rows, doc_row):
    round_value, round_grad = make_rounders()
    attn_in, attn_out, rel_proj, ff_in, ff_out, compress, gains, biases, pos_bias, ff_bias = weights
    gains = gains.astype(jnp.float32)
    biases = biases.astype(jnp.float32)
    pos_bias = pos_bias.astype(jnp.float32)
    ff_bias = ff_bias.astype(jnp.float32)
    model_width = hidden.shape[1]
    head_count = HEADS
    head_dim = model_width // head_count
    seg_len = hidden.shape[0]
    past_len = comp_rows.shape[0] + mem_rows.shape[0]
    key_len = past_len + seg_len
    joined = jnp.concatenate([comp_rows, mem_rows, hidden], 0)
    normed = round_value(layer_norm(joined, gains[:, 0], biases[:, 0]))
    queries = matmul(normed[past_len:], attn_in[:, :model_width])
    keyval = round_grad(round_value(matmul(normed, attn_in[:, model_width:])))
    key_heads = keyval[:, :model_width].reshape(key_len, head_count, head_dim)
    value_heads = keyval[:, model_width:].reshape(key_len, head_count, head_dim)
    q_content = round_grad(round_value(queries + pos_bias[:, 0])).reshape(
        seg_len, head_count, head_dim
    )
    q_position = round_grad(round_value(queries + pos_bias[:, 1])).reshape(
        seg_len, head_count, head_dim
    )
    sinus_table = round_value(sinusoid(key_len, model_width))
    relative = round_grad(round_value(matmul(sinus_table, rel_proj))).reshape(
        key_len, head_count, head_dim
    )
    content = jnp.einsum("shd,khd->hsk", q_content, key_heads)
    reversed_full = jnp.einsum("shd,khd->hsk", q_position, relative[::-1])
    position = skew_rows(reversed_full)
    query_pos = jnp.arange(seg_len)[:, None] + past_len
    key_pos = jnp.arange(key_len)[None, :]
    raw_scores = round_grad(content + position)
    scores = raw_scores * (1.0 / math.sqrt(head_dim))
    query_doc = doc_row[past_len:]
    allowed = (key_pos <= query_pos) & (doc_row[None, :] == query_doc[:, None])
    scores = jnp.where(allowed[None], scores, -1e30)
    peak = jnp.max(scores, 2, keepdims=True)
    exponent = jnp.exp(scores - peak)
    attn_probs = round_grad(round_value(exponent / jnp.sum(exponent, 2, keepdims=True)))
    mixed = jnp.einsum("hsk,khd->shd", attn_probs, value_heads).reshape(seg_len, model_width)
    mixed = round_grad(round_value(mixed))
    branch = round_grad(matmul(mixed, attn_out))
    middle = hidden + branch
    normed_two = round_value(layer_norm(middle, gains[:, 1], biases[:, 1]))
    ff_pre = round_grad(matmul(normed_two, ff_in) + ff_bias)
    activated = round_value(gelu_tanh(ff_pre))
    output = middle + matmul(activated, ff_out) + biases[:, 2]
    windows = mem_rows[: 3 * CNEW].reshape(CNEW, 3 * model_width)
    squeezed = matmul(windows, compress) + biases[:, 3]
    return (output, squeezed)


def forward_run(operands):
    weights_low, entry, mem_rows, comp_rows, doc_row = operands
    return layer(weights_low, entry, mem_rows, comp_rows, doc_row)


def forward_skip(operands):
    entry = operands[1]
    return (jnp.zeros_like(entry), jnp.zeros((CNEW, entry.shape[1]), jnp.float32))


def backward_run(operands):
    weights_float, entry, mem_rows, comp_rows, doc_row, cot_main, cot_side = operands

    def local_layer(weights_in, entry_float):
        return layer(weights_in, entry_float, mem_rows, comp_rows, doc_row)

    primal, pullback = jax.vjp(local_layer, weights_float, entry)
    weight_grads, entry_grad = pullback((cot_main, cot_side))
    return (weight_grads, entry_grad)


def backward_skip(operands):
    zero_grads = tuple((jnp.zeros(weight.shape, jnp.float32) for weight in operands[0]))
    return (zero_grads, jnp.zeros_like(operands[1]))


def per_device(
    tokens,
    doc_ids,
    memory,
    compressed,
    cot_out,
    cot_comp,
    attn_in,
    attn_out,
    rel_proj,
    ff_in,
    ff_out,
    compress,
    gains,
    biases,
    pos_bias,
    ff_bias,
):
    masters = (
        attn_in,
        attn_out,
        rel_proj,
        ff_in,
        ff_out,
        compress,
        gains,
        biases,
        pos_bias,
        ff_bias,
    )
    micro = tokens.shape[0]
    first = lax.axis_index("section") == 0
    shards = tuple((master[0].astype(jnp.bfloat16) for master in masters))
    gathered = jax.tree.map(
        lambda part, own: part.astype(own.dtype),
        lax.all_gather(as_sent(shards), "stream", axis=0, tiled=True),
        shards,
    )
    mem_float = memory[0].astype(jnp.float32)
    comp_float = compressed[0].astype(jnp.float32)
    side_cots = cot_comp[0].astype(jnp.float32)

    def pick(stacked, index_first, index_second):
        return jnp.where(first, stacked[index_first], stacked[index_second])

    received = jnp.zeros((tokens.shape[1], tokens.shape[2]), jnp.float32)
    tick_inputs = []
    tick_outputs = []
    tick_squeezed = []
    for tick in range(micro + 1):
        lower = min(tick, micro - 1)
        upper = max(tick - 1, 0)
        entry = jnp.where(first, tokens[lower].astype(jnp.float32), received)
        active = jnp.where(first, tick < micro, tick >= 1)
        operands = (
            gathered,
            entry,
            pick(mem_float, lower, upper),
            pick(comp_float, lower, upper),
            pick(doc_ids, lower, upper),
        )
        output, squeezed = lax.cond(active, forward_run, forward_skip, operands)
        tick_inputs.append(entry)
        tick_outputs.append(output)
        tick_squeezed.append(squeezed)
        if tick < micro:
            received = from_behind(output.astype(jnp.bfloat16), "section", 1).astype(jnp.float32)
    entries = jnp.stack(
        [jnp.where(first, tick_inputs[index], tick_inputs[index + 1]) for index in range(micro)]
    )
    outputs = jnp.stack(
        [jnp.where(first, tick_outputs[index], tick_outputs[index + 1]) for index in range(micro)]
    )
    squeezes = jnp.stack(
        [jnp.where(first, tick_squeezed[index], tick_squeezed[index + 1]) for index in range(micro)]
    )
    gathered = jax.tree.map(
        lambda part, own: part.astype(own.dtype),
        lax.all_gather(as_sent(shards), "stream", axis=0, tiled=True),
        shards,
    )
    weights_float = tuple((weight.astype(jnp.float32) for weight in gathered))
    totals = tuple((jnp.zeros(weight.shape, jnp.float32) for weight in gathered))
    returned = jnp.zeros((tokens.shape[1], tokens.shape[2]), jnp.float32)
    tick_grads = []
    for tick in range(micro + 1):
        upper = max(micro - 1 - tick, 0)
        lower = min(micro - tick, micro - 1)
        active = jnp.where(first, tick >= 1, tick < micro)
        cot_main = jnp.where(first, returned, cot_out[upper].astype(jnp.float32))
        operands = (
            weights_float,
            pick(entries, lower, upper),
            pick(mem_float, lower, upper),
            pick(comp_float, lower, upper),
            pick(doc_ids, lower, upper),
            cot_main,
            pick(side_cots, lower, upper),
        )
        weight_grads, entry_grad = lax.cond(active, backward_run, backward_skip, operands)
        tick_grads.append(entry_grad)
        totals = tuple((total + grad_term for total, grad_term in zip(totals, weight_grads)))
        if tick < micro:
            returned = from_behind(entry_grad.astype(jnp.bfloat16), "section", -1).astype(
                jnp.float32
            )
    totals = lax.psum_scatter(totals, "stream", scatter_dimension=0, tiled=True)
    input_grad = jnp.stack(
        [
            jnp.where(first, tick_grads[micro - index], tick_grads[micro - 1 - index])
            for index in range(micro)
        ]
    )
    seg_len = tokens.shape[1]
    activations = outputs.astype(jnp.bfloat16)[None]
    new_memory = jnp.concatenate([memory[0][:, seg_len:], entries.astype(jnp.bfloat16)], 1)[None]
    new_compressed = jnp.concatenate([compressed[0][:, CNEW:], squeezes.astype(jnp.bfloat16)], 1)[
        None
    ]
    (
        grad_one,
        grad_two,
        grad_three,
        grad_four,
        grad_five,
        grad_six,
        grad_seven,
        grad_eight,
        grad_nine,
        grad_ten,
    ) = totals
    return (
        activations,
        new_memory,
        new_compressed,
        input_grad[None],
        grad_one[None],
        grad_two[None],
        grad_three[None],
        grad_four[None],
        grad_five[None],
        grad_six[None],
        grad_seven[None],
        grad_eight[None],
        grad_nine[None],
        grad_ten[None],
    )


def solution(mesh):
    in_specs = (
        P("stream", None, None),
        P("stream", None),
        P("section", "stream", None, None),
        P("section", "stream", None, None),
        P("stream", None, None),
        P("section", "stream", None, None),
        P("section", "stream", None),
        P("section", "stream", None),
        P("section", "stream", None),
        P("section", "stream", None),
        P("section", "stream", None),
        P("section", "stream", None),
        P("section", "stream", None),
        P("section", "stream", None),
        P("section", "stream", None),
        P("section", "stream"),
    )
    out_specs = (
        P("section", "stream", None, None),
        P("section", "stream", None, None),
        P("section", "stream", None, None),
        P("section", "stream", None, None),
        P("section", "stream", None),
        P("section", "stream", None),
        P("section", "stream", None),
        P("section", "stream", None),
        P("section", "stream", None),
        P("section", "stream", None),
        P("section", "stream", None),
        P("section", "stream", None),
        P("section", "stream", None),
        P("section", "stream"),
    )
    return jax.shard_map(
        per_device, mesh=mesh, in_specs=in_specs, out_specs=out_specs, check_vma=False
    )
```

profile of v0, /device:TPU:0, one launch (start us, length us, event | category | flops | bytes accessed | tf_op | source)
XLA Modules:
  0.0 1894.9 jit_solution(11064209352440006178)
XLA Ops:
  15.7 25.0 %all-gather = bf16[1,1024,2]{2,0,1:T(2,128)(2,1)S(1)} all-gather(bf16[1,64,2]{2,0,1:T(2,128)(2,1)S(1)} %copy.342), channel_id=2, replica_groups=mesh['section'=2,'stream'=16] {'stream'}, dimensions={1}, use_global_device_ids=true | all-gather | bytes 4352 | tf_op jit(solution)/shard_map/all_gather | solution.py:208
  41.2 19.4 %all-gather.1 = bf16[1,1024,4]{2,0,1:T(2,128)(2,1)S(1)} all-gather(bf16[1,64,4]{2,0,1:T(2,128)(2,1)S(1)} %copy.344), channel_id=3, replica_groups=mesh['section'=2,'stream'=16] {'stream'}, dimensions={1}, use_global_device_ids=true | all-gather | bytes 8704 | tf_op jit(solution)/shard_map/all_gather | solution.py:208
  61.1 21.0 %all-gather.3 = bf16[1,1024,2]{2,0,1:T(2,128)(2,1)S(1)} all-gather(bf16[1,64,2]{2,0,1:T(2,128)(2,1)S(1)} %copy.346), channel_id=5, replica_groups=mesh['section'=2,'stream'=16] {'stream'}, dimensions={1}, use_global_device_ids=true | all-gather | bytes 4352 | tf_op jit(solution)/shard_map/all_gather | solution.py:208
  87.1 17.7 all-gather.7
  116.4 49.3 %all-gather.17.cloned.1.call-done = bf16[1,1024,3072]{2,1,0:T(8,128)(2,1)} async-done(((bf16[1,64,3072]{2,1,0:T(8,128)(2,1)}), bf16[1,1024,3072]{2,1,0:T(8,128)(2,1)}) %all-gather.17.cloned.1.call-update) | async-done | bytes 6291472 | tf_op jit(solution)/shard_map/all_gather | solution.py:208
  165.7 62.6 %all-gather.27.cloned.1.call-done = bf16[1,3072,1024]{2,1,0:T(8,128)(2,1)} async-done(((bf16[1,192,1024]{2,1,0:T(8,128)(2,1)}), bf16[1,3072,1024]{2,1,0:T(8,128)(2,1)}) %all-gather.27.cloned.1.call-update) | async-done | bytes 6291472 | tf_op jit(solution)/shard_map/all_gather | solution.py:208
  228.3 76.1 %all-gather.23.cloned.1.call-done = bf16[1,1024,4096]{2,1,0:T(8,128)(2,1)} async-done(((bf16[1,64,4096]{2,1,0:T(8,128)(2,1)}), bf16[1,1024,4096]{2,1,0:T(8,128)(2,1)}) %all-gather.23.cloned.1.call-update) | async-done | bytes 8388624 | tf_op jit(solution)/shard_map/all_gather | solution.py:208
  304.4 75.8 %all-gather.25.cloned.1.call-done = bf16[1,4096,1024]{2,1,0:T(8,128)(2,1)} async-done(((bf16[1,256,1024]{2,1,0:T(8,128)(2,1)}), bf16[1,4096,1024]{2,1,0:T(8,128)(2,1)}) %all-gather.25.cloned.1.call-update) | async-done | bytes 8388624 | tf_op jit(solution)/shard_map/all_gather | solution.py:208
  380.2 49.2 %conditional.4 = (bf16[64,1024]{1,0:T(8,128)(2,1)}, bf16[21,1024]{1,0:T(8,128)(2,1)S(1)}) conditional(s32[]{:T(128)} %convert_element_type.725, () %tuple.50, (f32[128,1024]{1,0:T(8,128)}, f32[256,1024]{1,0:T(8,128)}, f32[64,1024]{1,0:T(8,128)S(1)}, bf16[1024,2]{0,1:T(2,128)(2,1)S(1)}, bf16[1024,4]{0,1:T(4,128)(2,1)S(1)}, ...), branch_computations={%region_0.1_spmd, %region_1.8_spmd} | conditional | flops 4482600448 | bytes 127674608 | solution.py:234
  505.8 43.1 %conditional.6 = (f32[1024,3072]{1,0:T(8,128)}, f32[1024,1024]{1,0:T(8,128)S(1)}, f32[1024,1024]{1,0:T(8,128)}, f32[1024,4096]{1,0:T(8,128)}, f32[4096,1024]{1,0...) conditional(s32[]{:T(128)} %convert_element_type.768, () %tuple.55, ...), branch_computations={%region_22.23_spmd, %region_23.46_spmd} | conditional | flops 11706649600 | bytes 377496736 | solution.py:272
  559.5 136.3 %collective-permute-done.2 = bf16[64,1024]{1,0:T(8,128)(2,1)S(1)} collective-permute-done((bf16[64,1024]{1,0:T(8,128)(2,1)S(1)}, bf16[64,1024]{1,0:T(8,128)(2,1)S(1)}, u32[]{:S(2)}, u32[]{:S(2)}) %collective-permute-start.2) | collective-permute-done | bytes 131104 | tf_op jit(solution)/shard_map/ppermute | solution.py:19
  745.1 174.8 %conditional.7 = (f32[1024,3072]{1,0:T(8,128)}, f32[1024,1024]{1,0:T(8,128)}, f32[1024,1024]{1,0:T(8,128)}, f32[1024,4096]{1,0:T(8,128)}, f32[4096,1024]{1,0:T(8...) conditional(s32[]{:T(128)} %convert_element_type.725, () %tuple.54, ...), branch_computations={%region_59.60_spmd, %region_60.83_spmd} | conditional | flops 11704223744 | bytes 380764736 | solution.py:272
  751.0 15.7 rev.25
  852.0 15.3 rev.26
  937.6 15.4 rev.32
  1006.0 17.7 add_add_fusion.6
  1027.2 17.3 add_add_fusion.5
  1060.6 57.8 %all-reduce.48 = f32[4096]{0:T(1024)S(1)} all-reduce(f32[4096]{0:T(1024)S(1)} %add_add_fusion.14), channel_id=21, replica_groups=mesh['section'=2,'stream'=16] {'stream'}, use_global_device_ids=true, to_apply=%region_101.102.clone | all-reduce | flops 4096 | bytes 32768
  1125.1 43.6 %reduce-scatter.18.cloned.1.call-done = f32[64,1024]{1,0:T(8,128)} async-done(((f32[1024,1024]{1,0:T(8,128)}), f32[64,1024]{1,0:T(8,128)}) %reduce-scatter.18.cloned.1.call-update) | async-done | bytes 262160 | tf_op jit(solution)/shard_map/reduce_scatter | solution.py:279
  1168.7 76.3 %reduce-scatter.20.cloned.1.call-done = f32[64,1024]{1,0:T(8,128)} async-done(((f32[1024,1024]{1,0:T(8,128)}), f32[64,1024]{1,0:T(8,128)}) %reduce-scatter.20.cloned.1.call-update) | async-done | bytes 262160 | tf_op jit(solution)/shard_map/reduce_scatter | solution.py:279
  1245.0 138.7 %reduce-scatter.16.cloned.1.call-done = f32[64,3072]{1,0:T(8,128)} async-done(((f32[1024,3072]{1,0:T(8,128)}), f32[64,3072]{1,0:T(8,128)}) %reduce-scatter.16.cloned.1.call-update) | async-done | bytes 786448 | tf_op jit(solution)/shard_map/reduce_scatter | solution.py:279
  1383.7 139.0 %reduce-scatter.26.cloned.1.call-done = f32[192,1024]{1,0:T(8,128)} async-done(((f32[3072,1024]{1,0:T(8,128)}), f32[192,1024]{1,0:T(8,128)}) %reduce-scatter.26.cloned.1.call-update) | async-done | bytes 786448 | tf_op jit(solution)/shard_map/reduce_scatter | solution.py:279
  1522.6 182.8 %reduce-scatter.22.cloned.1.call-done = f32[64,4096]{1,0:T(8,128)} async-done(((f32[1024,4096]{1,0:T(8,128)}), f32[64,4096]{1,0:T(8,128)}) %reduce-scatter.22.cloned.1.call-update) | async-done | bytes 1048592 | tf_op jit(solution)/shard_map/reduce_scatter | solution.py:279
  1705.5 182.7 %reduce-scatter.24.cloned.1.call-done = f32[256,1024]{1,0:T(8,128)} async-done(((f32[4096,1024]{1,0:T(8,128)}), f32[256,1024]{1,0:T(8,128)}) %reduce-scatter.24.cloned.1.call-update) | async-done | bytes 1048592 | tf_op jit(solution)/shard_map/reduce_scatter | solution.py:279
  (762 shorter events, 482.6 us)
Async XLA Ops:
  7.2 105.3 %all-gather.19.cloned.1.call-start = ((), (), s32[]{:S(2)}) async-start(), calls=%async_computation.16 | async-start | bytes 2228224 | tf_op jit(solution)/shard_map/all_gather | solution.py:208
  9.0 107.4 %all-gather.21.cloned.1.call-start = ((), (), s32[]{:S(2)}) async-start(), calls=%async_computation.17 | async-start | bytes 2228224 | tf_op jit(solution)/shard_map/all_gather | solution.py:208
  10.7 154.9 %all-gather.17.cloned.1.call-start = ((), (), s32[]{:S(2)}) async-start(), calls=%async_computation.15 | async-start | bytes 6684672 | tf_op jit(solution)/shard_map/all_gather | solution.py:208
  12.7 215.5 %all-gather.27.cloned.1.call-start = ((), (), s32[]{:S(2)}) async-start(), calls=%async_computation.20 | async-start | bytes 6684672 | tf_op jit(solution)/shard_map/all_gather | solution.py:208
  13.6 290.7 %all-gather.23.cloned.1.call-start = ((), (), s32[]{:S(2)}) async-start(), calls=%async_computation.18 | async-start | bytes 8912896 | tf_op jit(solution)/shard_map/all_gather | solution.py:208
  14.6 365.6 %all-gather.25.cloned.1.call-start = ((), (), s32[]{:S(2)}) async-start(), calls=%async_computation.19 | async-start | bytes 8912896 | tf_op jit(solution)/shard_map/all_gather | solution.py:208
  15.5 1105.3 %reduce-scatter.28.cloned.1.call-start = ((), (), s32[]{:S(2)}) async-start(), calls=%async_computation.21 | async-start | bytes 557056
  41.1 339.1 %copy-start.156 = (bf16[1,1024,2]{1,2,0:T(2,128)(2,1)}, bf16[1,1024,2]{1,2,0:T(2,128)(2,1)S(1)}, u32[]{:S(2)}) copy-start(bf16[1,1024,2]{1,2,0:T(2,128)(2,1)S(1)} %copy.343) | copy-start | bytes 12292
  60.9 319.3 %copy-start.149 = (bf16[1,1024,4]{1,2,0:T(4,128)(2,1)}, bf16[1,1024,4]{1,2,0:T(4,128)(2,1)S(1)}, u32[]{:S(2)}) copy-start(bf16[1,1024,4]{1,2,0:T(4,128)(2,1)S(1)} %copy.345) | copy-start | bytes 24580
  82.4 297.8 %copy-start.154 = (bf16[1,1024,2]{1,2,0:T(2,128)(2,1)}, bf16[1,1024,2]{1,2,0:T(2,128)(2,1)S(1)}, u32[]{:S(2)}) copy-start(bf16[1,1024,2]{1,2,0:T(2,128)(2,1)S(1)} %copy.347) | copy-start | bytes 12292
  87.1 293.1 %copy-start.191 = (s32[1,448]{1,0:T(1,128)}, s32[1,448]{1,0:T(1,128)S(1)}, u32[]{:S(2)}) copy-start(s32[1,448]{1,0:T(1,128)S(1)} %get-tuple-element.542) | copy-start | bytes 5380
  106.9 394.9 %copy-start.134 = (pred[64,448]{1,0:T(8,128)(4,1)}, pred[64,448]{1,0:T(8,128)(4,1)S(1)}, u32[]{:S(2)}) copy-start(pred[64,448]{1,0:T(8,128)(4,1)S(1)} %fusion.271) | copy-start | bytes 86020
  429.4 16.6 collective-permute-start
  473.9 5.0 collective-permute-start.1
  552.0 143.8 %collective-permute-start.2 = (bf16[64,1024]{1,0:T(8,128)(2,1)S(1)}, bf16[64,1024]{1,0:T(8,128)(2,1)S(1)}, u32[]{:S(2)}, u32[]{:S(2)}) collective-permute-start(bf16[64,1024]{1,0:T(8,128)(2,1)S(1)} %convert_element_type.778), channel_id=1, source_target_pairs={{16,0},{17,1},{18,2},{19,3},{20,4},{21,5},{22,6},{23,7},{24,8},{25... | collective-permute-start | bytes 393224 | tf_op jit(solution)/shard_map/ppermute | solution.py:19
  737.1 7.2 collective-permute-start.3
  921.7 200.6 %reduce-scatter.32.cloned.1.call-start = ((), (), s32[]{:S(2)}) async-start(), calls=%async_computation.23 | async-start | bytes 557056
  923.6 200.1 %reduce-scatter.30.cloned.1.call-start = ((), (), s32[]{:S(2)}) async-start(), calls=%async_computation.22 | async-start | bytes 557056
  925.5 243.2 %reduce-scatter.18.cloned.1.call-start = ((), (), s32[]{:S(2)}) async-start(), calls=%async_computation.10 | async-start | bytes 4456448 | tf_op jit(solution)/shard_map/reduce_scatter | solution.py:279
  934.3 310.7 %reduce-scatter.20.cloned.1.call-start = ((), (), s32[]{:S(2)}) async-start(), calls=%async_computation.11 | async-start | bytes 4456448 | tf_op jit(solution)/shard_map/reduce_scatter | solution.py:279
  963.7 420.0 %reduce-scatter.16.cloned.1.call-start = ((), (), s32[]{:S(2)}) async-start(), calls=%async_computation.9 | async-start | bytes 13369344 | tf_op jit(solution)/shard_map/reduce_scatter | solution.py:279
  983.6 539.0 %reduce-scatter.26.cloned.1.call-start = ((), (), s32[]{:S(2)}) async-start(), calls=%async_computation.14 | async-start | bytes 13369344 | tf_op jit(solution)/shard_map/reduce_scatter | solution.py:279
  1002.6 702.9 %reduce-scatter.22.cloned.1.call-start = ((), (), s32[]{:S(2)}) async-start(), calls=%async_computation.12 | async-start | bytes 17825792 | tf_op jit(solution)/shard_map/reduce_scatter | solution.py:279
  1023.7 864.5 %reduce-scatter.24.cloned.1.call-start = ((), (), s32[]{:S(2)}) async-start(), calls=%async_computation.13 | async-start | bytes 17825792 | tf_op jit(solution)/shard_map/reduce_scatter | solution.py:279
  (194 other events, 1782.3 us)
Sparse Core Ops, SparseCore 0:
  10.8 47.4 all-gather.18
  61.0 41.0 all-gather.20
  105.0 60.6 all-gather.16
  167.8 60.4 all-gather.26
  230.9 73.4 all-gather.22
  307.0 73.1 all-gather.24
  921.8 53.1 reduce-scatter.27
  979.0 54.8 reduce-scatter.31
  1037.4 54.8 reduce-scatter.29
  1097.1 71.5 reduce-scatter.17
  1173.1 71.8 reduce-scatter.19
  1250.0 133.5 reduce-scatter.15
  1388.8 133.7 reduce-scatter.25
  1527.7 177.6 reduce-scatter.21
  1710.5 177.6 reduce-scatter.23
where the time goes:
time: 1910 us; the launch traced here: 1890 us
  waiting for transfers between devices  1170 us (61%)
  local copies, waits for them, and re-layouts  203 us (11%)
  matrix products  182 us (10%)
  other arithmetic  164 us (9%)
  blocking collectives  141 us (7%)
    reduce_scatter x6, waiting for transfers between devices, per_device(): totals = lax.psum_scatter(totals, 'stream', scatter_dimension=0, tiled=True)  763 us
    all_gather x6, waiting for transfers between devices, per_device(): lax.all_gather(as_sent(shards), 'stream', axis=0, tiled=True)  264 us
    ppermute x4, waiting for transfers between devices, from_behind(): return lax.ppermute(shard, axis, pairs)  143 us
    dot_general x33, matrix products, matmul(): return jnp.dot(first_op, second_op, preferred_element_type=jnp.float32)  115 us
    add x10, other arithmetic, per_device(): total + grad_term  83.5 us
    all_gather x4, blocking collectives, per_device(): lax.all_gather(as_sent(shards), 'stream', axis=0, tiled=True)  83.1 us
    rev x5, local copies, waits for them, and re-layouts, layer(): reversed_full = jnp.einsum('shd,khd->hsk', q_position, relative[::-1])  69.4 us
    unnamed x1, blocking collectives  57.8 us
  transfers between devices with their start and end apart: 19, of which 13 were waited for; matrix products, arithmetic and copies ran while one was open for 10% of the time, Pallas kernels for 0%

commit v1 on v0

v1 whole, which is shorter than its diff:
```python
import math

import jax
import jax.numpy as jnp
from jax import lax
from jax.sharding import PartitionSpec as P

HEADS = 8
CNEW = 21
BF = jnp.bfloat16
F32 = jnp.float32


def low(value):
    return value.astype(BF)


def dot(first_op, second_op):
    return jnp.dot(first_op, second_op, preferred_element_type=F32)


def dot_t(first_op, second_op):
    return lax.dot_general(first_op, second_op, (((1,), (1,)), ((), ())), preferred_element_type=F32)


def t_dot(first_op, second_op):
    return lax.dot_general(first_op, second_op, (((0,), (0,)), ((), ())), preferred_element_type=F32)


def normalise(values):
    mean_value = jnp.mean(values, -1, keepdims=True)
    centred = values - mean_value
    spread = jnp.mean(centred * centred, -1, keepdims=True)
    scale = lax.rsqrt(spread + 1e-05)
    return centred * scale, scale


def norm_back(hat, scale, grad_hat):
    first = jnp.mean(grad_hat, -1, keepdims=True)
    second = jnp.mean(grad_hat * hat, -1, keepdims=True)
    return scale * (grad_hat - first - hat * second)


def gelu(values):
    return 0.5 * values * (1.0 + jnp.tanh(0.7978845608028654 * (values + 0.044715 * values * values * values)))


def gelu_slope(values):
    inner = jnp.tanh(0.7978845608028654 * (values + 0.044715 * values * values * values))
    return 0.5 * (1.0 + inner) + 0.5 * values * (1.0 - inner * inner) * 0.7978845608028654 * (
        1.0 + 3.0 * 0.044715 * values * values
    )


def sinusoid(key_count, model_width):
    offsets = jnp.arange(key_count, dtype=F32)[:, None]
    inverse_rate = jnp.exp(
        jnp.arange(model_width // 2, dtype=F32) * (-2.0 * math.log(10000.0) / model_width)
    )
    angles = offsets * inverse_rate[None, :]
    return low(jnp.concatenate([jnp.sin(angles), jnp.cos(angles)], 1))


def skew(rows):
    lead, seg_len, key_len = rows.shape[:-2], rows.shape[-2], rows.shape[-1]
    padded = jnp.pad(rows, [(0, 0)] * len(lead) + [(0, 0), (0, 1)]).reshape(lead + (seg_len * (key_len + 1),))
    return padded[..., seg_len - 1 : seg_len - 1 + seg_len * key_len].reshape(rows.shape)


def unskew(rows):
    lead, seg_len, key_len = rows.shape[:-2], rows.shape[-2], rows.shape[-1]
    flat = rows.reshape(lead + (seg_len * key_len,))
    flat = jnp.pad(flat, [(0, 0)] * len(lead) + [(seg_len - 1, 1)])
    flat = flat.reshape(lead + (seg_len, key_len + 1))
    return flat[..., :key_len]


def xor_pairs(count, bit):
    return [(i, i ^ bit) for i in range(count)]


def scatter_sum(blocks, order):
    size = lax.axis_size("stream")
    for bit in order:
        got = lax.ppermute(blocks[1], "stream", xor_pairs(size, bit))
        blocks = (blocks[0].astype(F32) + got.astype(F32)).astype(blocks.dtype)
    return blocks


def relative_order(blocks, order):
    size = lax.axis_size("stream")
    me = lax.axis_index("stream")
    index = []
    for position in range(size):
        value = 0
        for place, bit in enumerate(order):
            if (position >> (len(order) - 1 - place)) & 1:
                value |= bit
        index.append(value)
    picked = blocks[jnp.array(index, jnp.int32) ^ me]
    return picked.reshape((2,) * len(order) + blocks.shape[1:])


def gather(shard):
    return lax.all_gather(shard, "stream", axis=0, tiled=False)


def per_device(
    tokens,
    doc_ids,
    memory,
    compressed,
    cot_out,
    cot_comp,
    attn_in,
    attn_out,
    rel_proj,
    ff_in,
    ff_out,
    compress,
    gains,
    biases,
    pos_bias,
    ff_bias,
):
    size = lax.axis_size("stream")
    me = lax.axis_index("stream")
    order = [1 << k for k in range(size.bit_length() - 1)]
    first = lax.axis_index("section") == 0
    micro, seg_len, width = tokens.shape
    rows = attn_in.shape[1]
    hidden_cols = ff_in.shape[2]
    quarters = hidden_cols // width
    my_hidden = hidden_cols // size
    memory, compressed, cot_comp = memory[0], compressed[0], cot_comp[0]
    past_len = compressed.shape[1] + memory.shape[1]
    key_len = past_len + seg_len
    head_dim = width // HEADS
    root = 1.0 / math.sqrt(head_dim)

    small = jnp.concatenate(
        [low(gains[0]).T, low(biases[0]).T, low(pos_bias[0]).T, low(ff_bias[0]).reshape(quarters, rows)], 0
    )
    small = gather(small).transpose(1, 0, 2).reshape(-1, width).astype(F32)
    gain_one, gain_two = small[0], small[1]
    bias_one, bias_two, bias_out = small[2], small[3], small[4]
    pos_content, pos_position = small[6], small[7]
    hidden_bias = small[8:].reshape(quarters, size, rows).transpose(1, 0, 2).reshape(hidden_cols)

    low_in, low_ff_in, low_ff_out = low(attn_in[0]), low(ff_in[0]), low(ff_out[0])
    shard = jnp.concatenate(
        [low_in[:, i * width : (i + 1) * width] for i in range(3)]
        + [low(attn_out[0]), low(rel_proj[0])]
        + [low_ff_in[:, i * width : (i + 1) * width] for i in range(quarters)]
        + [low_ff_out],
        0,
    )
    weights = gather(shard)

    def part(start, count=1):
        return weights[:, start * rows : (start + count) * rows].reshape(size * count * rows, width)

    w_query, w_key, w_value, w_out, w_rel = (part(i) for i in range(5))
    w_keyval = jnp.concatenate([w_key, w_value], 1)
    w_ff_in = jnp.concatenate([part(5 + i) for i in range(quarters)], 1)
    w_ff_out = part(5 + quarters, quarters)

    comp_rows = compress.shape[1]
    windows = memory[:, : 3 * CNEW].reshape(micro * CNEW, size, comp_rows).transpose(1, 0, 2)
    windows = lax.all_to_all(windows, "stream", 0, 0, tiled=True)
    partial = dot(windows.reshape(-1, comp_rows), low(compress[0]))
    partial = low(partial).reshape(size, micro * CNEW, width)
    squeezed = scatter_sum(relative_order(partial, order), order)
    side_all = gather(cot_comp.reshape(micro * CNEW, width)).reshape(-1, width)
    grad_compress = t_dot(windows.reshape(-1, comp_rows), side_all)

    past = jnp.concatenate([compressed, memory], 1).astype(F32)
    past_hat, past_scale = normalise(past)
    past_normed = low(past_hat * gain_one + bias_one)
    past_keyval = low(dot(past_normed.reshape(-1, width), w_keyval)).reshape(micro, past_len, 2 * width)
    relative = low(dot(sinusoid(key_len, width), w_rel))[::-1]
    relative = relative.reshape(key_len, HEADS, head_dim)
    allowed = (jnp.arange(key_len)[None, :] <= jnp.arange(seg_len)[:, None] + past_len) & (
        doc_ids[:, None, :] == doc_ids[:, past_len:, None]
    )

    def forward(entry):
        hat_one, scale_one = normalise(entry)
        normed = low(hat_one * gain_one + bias_one)
        flat = normed.reshape(-1, width)
        queries = dot(flat, w_query)
        keyval = low(dot(flat, w_keyval)).reshape(micro, seg_len, 2 * width)
        keyval = jnp.concatenate([past_keyval, keyval], 1)
        keys = keyval[..., :width].reshape(micro, key_len, HEADS, head_dim)
        values = keyval[..., width:].reshape(micro, key_len, HEADS, head_dim)
        q_content = low(queries + pos_content).reshape(micro, seg_len, HEADS, head_dim)
        q_position = low(queries + pos_position).reshape(micro, seg_len, HEADS, head_dim)
        content = jnp.einsum("bshd,bkhd->bhsk", q_content, keys, preferred_element_type=F32)
        position = skew(jnp.einsum("bshd,khd->bhsk", q_position, relative, preferred_element_type=F32))
        scores = jnp.where(allowed[:, None], (content + position) * root, -1e30)
        exponent = jnp.exp(scores - jnp.max(scores, -1, keepdims=True))
        probs = low(exponent / jnp.sum(exponent, -1, keepdims=True))
        mixed = low(jnp.einsum("bhsk,bkhd->bshd", probs, values, preferred_element_type=F32)).reshape(-1, width)
        middle = entry.reshape(-1, width) + dot(mixed, w_out)
        hat_two, scale_two = normalise(middle)
        normed_two = low(hat_two * gain_two + bias_two)
        ff_pre = dot(normed_two, w_ff_in) + hidden_bias
        output = middle + dot(low(gelu(ff_pre)), w_ff_out) + bias_out
        saved = (hat_one, scale_one, normed, keys, values, q_content, q_position, probs, mixed, hat_two, scale_two,
                 normed_two, ff_pre)
        return output, saved

    def backward(saved, cot):
        (hat_one, scale_one, normed, keys, values, q_content, q_position, probs, mixed, hat_two, scale_two,
         normed_two, ff_pre) = saved
        cot = cot.reshape(-1, width)
        grad_pre = low(dot_t(low(cot), w_ff_out) * gelu_slope(ff_pre))
        grad_two = dot_t(grad_pre, w_ff_in)
        grad_middle = cot + norm_back(hat_two, scale_two, grad_two * gain_two)
        grad_branch = low(grad_middle)
        grad_mixed = low(dot_t(grad_branch, w_out)).reshape(micro, seg_len, HEADS, head_dim)
        grad_probs = low(jnp.einsum("bshd,bkhd->bhsk", grad_mixed, values, preferred_element_type=F32)).astype(F32)
        grad_values = low(jnp.einsum("bhsk,bshd->bkhd", probs, grad_mixed, preferred_element_type=F32))
        wide = probs.astype(F32)
        grad_scores = low(wide * (grad_probs - jnp.sum(wide * grad_probs, -1, keepdims=True)) * root)
        grad_content = low(jnp.einsum("bhsk,bkhd->bshd", grad_scores, keys, preferred_element_type=F32))
        grad_keys = low(jnp.einsum("bhsk,bshd->bkhd", grad_scores, q_content, preferred_element_type=F32))
        skewed = unskew(grad_scores)
        grad_position = low(jnp.einsum("bhsk,khd->bshd", skewed, relative, preferred_element_type=F32))
        grad_relative = low(jnp.einsum("bhsk,bshd->khd", skewed, q_position, preferred_element_type=F32))
        grad_content = grad_content.reshape(-1, width)
        grad_position = grad_position.reshape(-1, width)
        grad_query = low(grad_content.astype(F32) + grad_position.astype(F32))
        grad_keyval = jnp.concatenate(
            [grad_keys.reshape(micro, key_len, width), grad_values.reshape(micro, key_len, width)], 2
        )
        grad_normed = dot_t(grad_query, w_query) + dot_t(
            grad_keyval[:, past_len:].reshape(-1, 2 * width), w_keyval
        )
        grad_normed = grad_normed.reshape(micro, seg_len, width)
        grad_entry = grad_middle.reshape(micro, seg_len, width) + norm_back(
            hat_one, scale_one, grad_normed * gain_one
        )
        return grad_entry, (grad_two, grad_branch, grad_content, grad_position, grad_query, grad_keyval,
                            grad_relative, grad_normed)

    token_entry = tokens.astype(F32)
    output, _ = forward(token_entry)
    received = lax.ppermute(low(output), "section", [(0, 1)]).reshape(tokens.shape)
    entry = jnp.where(first, tokens, received)
    output, saved = forward(entry.astype(F32))
    (hat_one, scale_one, normed, keys, values, q_content, q_position, probs, mixed, hat_two, scale_two,
     normed_two, ff_pre) = saved
    normed_all = gather(normed_two).reshape(-1, width)
    grad_entry, _ = backward(saved, cot_out.astype(F32))
    returned = lax.ppermute(low(grad_entry), "section", [(1, 0)])
    cot = jnp.where(first, returned, cot_out)
    cot_all = gather(cot.reshape(-1, width)).reshape(-1, width)
    grad_entry, parts = backward(saved, cot.astype(F32))
    (grad_two, grad_branch, grad_content, grad_position, grad_query, grad_keyval, grad_relative, grad_normed) = parts

    normed_full = jnp.concatenate([past_normed, normed], 1).reshape(-1, width)
    flat_keyval = grad_keyval.reshape(-1, 2 * width)

    def by_dest(grad):
        return low(grad).reshape(size, rows, grad.shape[1])

    out_part = by_dest(t_dot(mixed, grad_branch))
    query_part = by_dest(t_dot(normed.reshape(-1, width), grad_query))
    rel_part = by_dest(t_dot(sinusoid(key_len, width)[::-1], grad_relative.reshape(key_len, width)))
    keyval_part = by_dest(t_dot(normed_full, flat_keyval))
    first_sum = scatter_sum(relative_order(jnp.concatenate([out_part, rel_part, query_part], 2), order), order)
    second_sum = scatter_sum(relative_order(keyval_part, order), order)
    grad_attn_out = first_sum[:, :width].astype(F32)
    grad_rel = first_sum[:, width : 2 * width].astype(F32)
    grad_attn_in = jnp.concatenate([first_sum[:, 2 * width :], second_sum], 1).astype(F32)

    grad_past = dot_t(grad_keyval[:, :past_len].reshape(-1, 2 * width), w_keyval)
    flat_hat = past_hat.reshape(-1, width)
    flat_token = grad_normed.reshape(-1, width)
    vectors = jnp.stack(
        [
            jnp.sum(grad_past * flat_hat, 0) + jnp.sum(flat_token * hat_one.reshape(-1, width), 0),
            jnp.sum(grad_two * hat_two, 0),
            jnp.sum(grad_past, 0) + jnp.sum(flat_token, 0),
            jnp.sum(grad_two, 0),
            jnp.sum(cot.astype(F32), (0, 1)),
            jnp.sum(cot_comp.astype(F32), (0, 1)),
            jnp.sum(grad_content.astype(F32), 0),
            jnp.sum(grad_position.astype(F32), 0),
        ]
    )
    vectors = vectors.reshape(8, size, rows).transpose(1, 0, 2)
    vectors = scatter_sum(relative_order(vectors, order), order)

    start = me * my_hidden
    mine_in = lax.dynamic_slice(w_ff_in, (0, start), (width, my_hidden))
    mine_bias = lax.dynamic_slice(hidden_bias, (start,), (my_hidden,))
    pre_all = dot(normed_all, mine_in) + mine_bias
    active_all = low(gelu(pre_all))
    slope_all = gelu_slope(pre_all)
    grad_pre_all = low(dot_t(cot_all, low_ff_out) * slope_all)
    grad_ff_out = t_dot(active_all, cot_all)
    grad_ff_in = t_dot(normed_all, grad_pre_all)
    grad_ff_bias = jnp.sum(grad_pre_all.astype(F32), 0)
    grad_ff_in = lax.all_to_all(low(grad_ff_in).reshape(size, rows, my_hidden), "stream", 0, 0, tiled=True)
    grad_ff_in = grad_ff_in.transpose(1, 0, 2).reshape(rows, hidden_cols).astype(F32)

    activations = low(output).reshape(tokens.shape)
    new_memory = jnp.concatenate([memory[:, seg_len:], entry], 1)
    squeezed = low(squeezed.astype(F32) + small[5]).reshape(micro, CNEW, width)
    new_compressed = jnp.concatenate([compressed[:, CNEW:], squeezed], 1)
    return tuple(
        value[None]
        for value in (
            activations,
            new_memory,
            new_compressed,
            grad_entry,
            grad_attn_in,
            grad_attn_out,
            grad_rel,
            grad_ff_in,
            grad_ff_out,
            grad_compress,
            vectors[:2].T,
            vectors[2:6].T,
            vectors[6:].T,
            grad_ff_bias,
        )
    )


def solution(mesh):
    in_specs = (
        P("stream", None, None),
        P("stream", None),
        P("section", "stream", None, None),
        P("section", "stream", None, None),
        P("stream", None, None),
        P("section", "stream", None, None),
    ) + (P("section", "stream", None),) * 9 + (P("section", "stream"),)
    out_specs = (
        (P("section", "stream", None, None),) * 4 + (P("section", "stream", None),) * 9 + (P("section", "stream"),)
    )
    return jax.shard_map(
        per_device, mesh=mesh, in_specs=in_specs, out_specs=out_specs, check_vma=False
    )
```

time: 1910 us -> 651 us (0.34)
  waiting for transfers between devices: 1170 us -> 186 us
  blocking collectives: 141 us -> 27.7 us
  other arithmetic: 164 us -> 67.5 us
  local copies, waits for them, and re-layouts: 203 us -> 164 us
  matrix products: 182 us -> 152 us
  starting transfers between devices: 7.15 us -> 31.3 us
    reduce_scatter x6 -> x0, waiting for transfers between devices: 763 us -> none  [per_device(): totals = lax.psum_scatter(totals, 'stream', scatter_dimension=0, tiled=True)]
    all_gather x6 -> x4, waiting for transfers between devices: 264 us -> 47.6 us  [gather(): return lax.all_gather(shard, 'stream', axis=0, tiled=False)]
    add x13 -> x9, other arithmetic: 83.5 us -> 3.56 us  [the longest x2 3.03 us: backward(): grad_middle = cot + norm_back(hat_two, scale_two, grad_two * gain_two)]
    unnamed x1 -> x0, blocking collectives: 57.8 us -> none
    all_gather x4 -> x1, blocking collectives: 83.1 us -> 27.7 us  [gather(): return lax.all_gather(shard, 'stream', axis=0, tiled=False)]
    rev x5 -> x2, local copies, waits for them, and re-layouts: 69.4 us -> 23.1 us  [the longest x1 12.9 us: per_device(): relative = low(dot(sinusoid(key_len, width), w_rel))[::-1]]
    dot_general x69 -> x44, matrix products: 179 us -> 146 us  [the longest x10 47.5 us: dot_t(): lax.dot_general(first_op, second_op, (((1,), (1,)), ((), ())), preferred_...]
    another operation x13 -> x8, local copies, waits for them, and re-layouts: 34.8 us -> 1.83 us  [the longest x7 1.17 us: per_device(): jnp.stack([jnp.sum(grad_past * flat_hat, 0) + jnp.sum(flat_token * hat_on...]
  transfers between devices with their start and end apart: 19 -> 24, of which waited for: 13 -> 14; matrix products, arithmetic and copies ran while one was open for 10% -> 41% of each run, Pallas kernels for 0% -> 0%
where the time goes in v1:
time: 651 us; the launch traced here: 644 us
  waiting for transfers between devices  186 us (29%)
  local copies, waits for them, and re-layouts  164 us (25%)
  matrix products  152 us (23%)
  other arithmetic  67.5 us (10%)
  starting transfers between devices  31.3 us (5%)
  blocking collectives  27.7 us (4%)
  between operations  15.6 us (2%)
    ppermute x16, waiting for transfers between devices, scatter_sum(): got = lax.ppermute(blocks[1], 'stream', xor_pairs(size, bit))  128 us
    all_gather x4, waiting for transfers between devices, gather(): return lax.all_gather(shard, 'stream', axis=0, tiled=False)  47.6 us
    dot_general x10, matrix products, dot_t(): lax.dot_general(first_op, second_op, (((1,), (1,)), ((), ())), preferred_...  47.5 us
    dot_general x13, matrix products, dot(): return jnp.dot(first_op, second_op, preferred_element_type=F32)  43.6 us
    all_gather x1, blocking collectives, gather(): return lax.all_gather(shard, 'stream', axis=0, tiled=False)  27.7 us
    dot_general x7, matrix products, t_dot(): lax.dot_general(first_op, second_op, (((0,), (0,)), ((), ())), preferred_...  21.3 us
    slice x2, local copies, waits for them, and re-layouts, part(): weights[:, start * rows:(start + count) * rows]  19.5 us
    unnamed x221, local copies, waits for them, and re-layouts  19.4 us
  transfers between devices with their start and end apart: 24, of which 14 were waited for; matrix products, arithmetic and copies ran while one was open for 41% of the time, Pallas kernels for 0%

profile of v1, /device:TPU:0, one launch (start us, length us, event | category | flops | bytes accessed | tf_op | source)
XLA Modules:
  0.0 643.9 jit_solution(16329268859134235757)
XLA Ops:
  12.4 7.4 %all-to-all-start = ((bf16[16,42,192]{2,1,0:T(8,128)(2,1)}), bf16[16,42,192]{2,1,0:T(8,128)(2,1)S(1)}, u32[]{:S(2)}, u32[]{:S(2)}) async-start(bf16[16,42,192]{2,1,0:T(8,128)(2,1)} %bitcast.504), calls=%async_computation | async-start | bytes 786432 | tf_op jit(solution)/shard_map/all_to_all | solution.py:170
  21.4 27.7 %all-gather.3 = bf16[16,12,64]{2,1,0:T(8,128)(2,1)S(1)} all-gather(bf16[1,12,64]{2,1,0:T(8,128)(2,1)S(1)} %maximum_bitcast_fusion.2), channel_id=2, replica_groups=mesh['section'=2,'stream'=16] {'stream'}, dimensions={0}, use_global_device_ids=true | all-gather | bytes 26112 | tf_op jit(solution)/shard_map/all_gather | solution.py:105
  76.3 10.3 %rev.7 = bf16[448,1024]{1,0:T(8,128)(2,1)} reverse(bf16[448,1024]{1,0:T(8,128)(2,1)S(1)} %pad_maximum_fusion.6), dimensions={0} | reverse | bytes 1835008 | tf_op jit(solution)/shard_map/rev | solution.py:270
  88.5 6.2 collective-permute-done.2
  96.7 10.7 %collective-permute-done.3 = bf16[2,42,1024]{2,1,0:T(8,128)(2,1)S(1)} collective-permute-done((bf16[2,42,1024]{2,1,0:T(8,128)(2,1)S(1)}, bf16[2,42,1024]{2,1,0:T(8,128)(2,1)S(1)}, u32[]{:S(2)}, u32[]{:S(2)}) %collective-permute-start.3) | collective-permute-done | bytes 172064 | tf_op jit(solution)/shard_map/ppermute | solution.py:85
  108.9 8.0 %collective-permute-done.4 = bf16[42,1024]{1,0:T(8,128)(2,1)S(1)} collective-permute-done((bf16[42,1024]{1,0:T(8,128)(2,1)S(1)}, bf16[42,1024]{1,0:T(8,128)(2,1)S(1)}, u32[]{:S(2)}, u32[]{:S(2)}) %collective-permute-start.4) | collective-permute-done | bytes 86048 | tf_op jit(solution)/shard_map/ppermute | solution.py:85
  117.9 47.5 %all-gather.13.cloned.1.call-done = bf16[13312,1024]{1,0:T(8,128)(2,1)} async-done(((bf16[832,1024]{1,0:T(8,128)(2,1)}), bf16[13312,1024]{1,0:T(8,128)(2,1)}) %all-gather.13.cloned.1.call-update) | async-done | bytes 27262992 | tf_op jit(solution)/shard_map/all_gather | solution.py:105
  165.4 11.3 %fusion.236 = (bf16[16,64,1024]{2,1,0:T(8,128)(2,1)}, bf16[16,64,1024]{2,1,0:T(8,128)(2,1)}, bf16[16,64,1024]{2,1,0:T(8,128)(2,1)}, bf16[16,64,1024]{2,1,0:T(8,1...) fusion(bf16[16,832,1024]{2,1,0:T(8,128)(2,1)} %bitcast.513), kind=kLoop, calls=%fused_computation.416 | loop fusion | bytes 37748736 | tf_op jit(solution)/shard_map/slice | solution.py:161
  187.6 12.9 %rev.6 = bf16[448,1024]{1,0:T(8,128)(2,1)S(1)} reverse(bf16[448,1024]{1,0:T(8,128)(2,1)} %convolution_convert_fusion.7), dimensions={0} | reverse | bytes 1835008 | tf_op jit(solution)/shard_map/rev | solution.py:181
  229.8 8.2 %slice.367 = bf16[16,256,1024]{2,1,0:T(8,128)(2,1)} slice(bf16[16,832,1024]{2,1,0:T(8,128)(2,1)} %bitcast.514), slice={[0:16], [576:832], [0:1024]} | slice | bytes 16777216 | tf_op jit(solution)/shard_map/slice | solution.py:161
  238.8 6.8 %pad_maximum_fusion = bf16[1024,4096]{1,0:T(8,128)(2,1)} fusion(bf16[1024,1024]{1,0:T(8,128)(2,1)} %bitcast.542, bf16[1024,1024]{1,0:T(8,128)(2,1)} %bitcast.543, bf16[1024,1024]{1,0:T(8,128)(2,1)} %bitcast.544, bf16[1024,1024]{1,0:T(8,128)(2,1)S(1)} %bitcast.541), kind=kLoop, calls=%fused_computation.8 | loop fusion | flops 33554432 | bytes 16777216 | tf_op jit(solution)/shard_map/concatenate | solution.py:165
  245.6 9.2 %fusion.86 = bf16[128,1024]{1,0:T(8,128)(2,1)} fusion(f32[128,1024]{1,0:T(8,128)S(1)} %copy-done.48, bf16[4096,1024]{1,0:T(8,128)(2,1)} %bitcast.531, bf16[1024,4096]{1,0:T(8,128)(2,1)} %pad_maximum_fusion, f32[4096]{0:T(1024)} %copy-done.75, f32[1024]{0:T(1024)} %add.394, f32[1024]{0:T(1024)S(1)} %copy-done.84, f32[1024]{0:T(1024)S(1)} %mul.427, ...), kind=kOutput, calls=%fused_computation.158 | convolution fusion | flops 2153775104 | bytes 17593344 | tf_op jit(solution)/shard_map/dot_general | solution.py:19
  306.8 13.4 %fusion.235 = (f32[128]{0:T(128)S(1)}, f32[128]{0:T(128)S(1)}, f32[128,1024]{1,0:T(8,128)}) fusion(f32[128]{0:T(128)S(1)} %add_rsqrt_fusion.3, f32[128,1024]{1,0:T(8,128)} %copy-done.6, f32[128]{0:T(128)S(1)} %broadcast_multiply_fusion.11, f32[1024]{0:T(1024)S(1)} %copy-done.78, bf16[1024,4096]{1,0:T(8,128)(2,1)} %pad_maximum_fusion, ...), kind=kOutput, calls=%fused_computation.415 | convolution fusion | flops 2158231552 | bytes 20191232 | tf_op jit(solution)/shard_map/dot_general | solution.py:23
  366.0 6.3 fusion.87
  376.5 13.6 %multiply_reduce_fusion.2 = (f32[1024]{0:T(1024)S(1)}, f32[128]{0:T(128)S(1)}, f32[128]{0:T(128)S(1)}, f32[1024]{0:T(1024)S(1)}, f32[128,1024]{1,0:T(8,128)}) fusion(f32[128]{0:T(128)S(1)} %add_rsqrt_fusion.3, f32[128,1024]{1,0:T(8,128)} %copy-done.6, f32[128]{0:T(128)S(1)} %broadcast_multiply_fusion.11, f32[1024]{0:T(1024)S(1)} %copy-done.78, ...), kind=kOutput, calls=%fused_computation.232 | convolution fusion | flops 2158622720 | bytes 20199424 | tf_op jit(solution)/shard_map/dot_general | solution.py:23
  426.8 8.1 %bitcast_convert_fusion = bf16[1024,2048]{1,0:T(8,128)(2,1)} fusion(bf16[2,448,2048]{2,1,0:T(8,128)(2,1)} %copy-done.17, bf16[2,64,1024]{2,1,0:T(8,128)(2,1)S(1)} %copy-done.33, bf16[2,384,1024]{2,1,0:T(8,128)(2,1)S(1)} %copy-done.56), kind=kOutput, calls=%fused_computation.9 | convolution fusion | flops 3763863552 | bytes 9699328 | tf_op jit(solution)/shard_map/dot_general | solution.py:27
  449.1 6.5 %pad_maximum_fusion.1 = bf16[16,64,3072]{2,1,0:T(8,128)(2,1)} fusion(bf16[16,64,1024]{2,1,0:T(8,128)(2,1)S(1)} %bitcast.536, bf16[16,64,1024]{2,1,0:T(8,128)(2,1)S(1)} %bitcast.583, bf16[16,64,1024]{2,1,0:T(8,128)(2,1)S(1)} %bitcast.539), kind=kLoop, calls=%fused_computation.10 | loop fusion | flops 18874368 | bytes 12582912 | tf_op jit(solution)/shard_map/concatenate | solution.py:272
  455.6 6.6 %gather_fusion.1 = bf16[16,64,3072]{2,1,0:T(8,128)(2,1)} fusion(bf16[16,64,3072]{2,1,0:T(8,128)(2,1)} %pad_maximum_fusion.1, s32[1024]{0:T(1024)} %copy-done.90), kind=kCustom, calls=%fused_computation.1 | custom fusion | bytes 12582976 | tf_op jit(solution)/shard_map/gather | solution.py:100
  462.1 6.2 fusion.237
  497.8 26.4 %collective-permute-done.11 = bf16[2,2,64,2048]{3,2,1,0:T(8,128)(2,1)S(1)} collective-permute-done((bf16[2,2,64,2048]{3,2,1,0:T(8,128)(2,1)S(1)}, bf16[2,2,64,2048]{3,2,1,0:T(8,128)(2,1)S(1)}, u32[]{:S(2)}, u32[]{:S(2)}) %collective-permute-start.11) | collective-permute-done | bytes 1048608 | tf_op jit(solution)/shard_map/ppermute | solution.py:85
  526.4 35.4 %collective-permute-done.7 = bf16[2,2,64,3072]{3,2,1,0:T(8,128)(2,1)S(1)} collective-permute-done((bf16[2,2,64,3072]{3,2,1,0:T(8,128)(2,1)S(1)}, bf16[2,2,64,3072]{3,2,1,0:T(8,128)(2,1)S(1)}, u32[]{:S(2)}, u32[]{:S(2)}) %collective-permute-start.7) | collective-permute-done | bytes 1572896 | tf_op jit(solution)/shard_map/ppermute | solution.py:85
  564.7 20.9 %collective-permute-done.8 = bf16[2,64,3072]{2,1,0:T(8,128)(2,1)S(1)} collective-permute-done((bf16[2,64,3072]{2,1,0:T(8,128)(2,1)S(1)}, bf16[2,64,3072]{2,1,0:T(8,128)(2,1)S(1)}, u32[]{:S(2)}, u32[]{:S(2)}) %collective-permute-start.8) | collective-permute-done | bytes 786464 | tf_op jit(solution)/shard_map/ppermute | solution.py:85
  586.2 16.5 %collective-permute-done.9 = bf16[64,3072]{1,0:T(8,128)(2,1)S(1)} collective-permute-done((bf16[64,3072]{1,0:T(8,128)(2,1)S(1)}, bf16[64,3072]{1,0:T(8,128)(2,1)S(1)}, u32[]{:S(2)}, u32[]{:S(2)}) %collective-permute-start.9) | collective-permute-done | bytes 393248 | tf_op jit(solution)/shard_map/ppermute | solution.py:85
  627.7 7.5 %all-to-all-done.1 = bf16[16,64,256]{2,1,0:T(8,128)(2,1)S(1)} async-done(((bf16[16,64,256]{2,1,0:T(8,128)(2,1)}), bf16[16,64,256]{2,1,0:T(8,128)(2,1)S(1)}, u32[]{:S(2)}, u32[]{:S(2)}) %all-to-all-start.1) | async-done | bytes 524320 | tf_op jit(solution)/shard_map/all_to_all | solution.py:306
  (477 shorter events, 294.9 us)
Async XLA Ops:
  7.2 158.2 %all-gather.13.cloned.1.call-start = ((), (), s32[]{:S(2)}) async-start(), calls=%async_computation.4 | async-start | bytes 28966912 | tf_op jit(solution)/shard_map/all_gather | solution.py:105
  12.4 43.8 %all-to-all-start = ((bf16[16,42,192]{2,1,0:T(8,128)(2,1)}), bf16[16,42,192]{2,1,0:T(8,128)(2,1)S(1)}, u32[]{:S(2)}, u32[]{:S(2)}) async-start(bf16[16,42,192]{2,1,0:T(8,128)(2,1)} %bitcast.504), calls=%async_computation | async-start | bytes 786432 | tf_op jit(solution)/shard_map/all_to_all | solution.py:170
  19.8 238.6 %all-gather.11.cloned.1.call-start = ((), (), s32[]{:S(2)}) async-start(), calls=%async_computation.3 | async-start | bytes 1671168 | tf_op jit(solution)/shard_map/all_gather | solution.py:105
  20.6 582.1 %all-gather.15.cloned.1.call-start = ((), (), s32[]{:S(2)}) async-start(), calls=%async_computation.5 | async-start | bytes 4456448 | tf_op jit(solution)/shard_map/all_gather | solution.py:105
  67.2 5.8 collective-permute-start.1
  74.2 20.5 %collective-permute-start.2 = (bf16[2,2,42,1024]{3,2,1,0:T(8,128)(2,1)}, bf16[2,2,42,1024]{3,2,1,0:T(8,128)(2,1)}, u32[]{:S(2)}, u32[]{:S(2)}) collective-permute-start(bf16[2,2,42,1024]{3,2,1,0:T(8,128)(2,1)} %slice_bitcast_fusion.10), channel_id=1, source_target_pairs={{0,2},{1,3},{2,0},{3,1},{4,6},{5,7},{6,4},{7,5},{8,10},{9,11},{10,... | collective-permute-start | bytes 1032200 | tf_op jit(solution)/shard_map/ppermute | solution.py:85
  95.8 11.5 %collective-permute-start.3 = (bf16[2,42,1024]{2,1,0:T(8,128)(2,1)S(1)}, bf16[2,42,1024]{2,1,0:T(8,128)(2,1)S(1)}, u32[]{:S(2)}, u32[]{:S(2)}) collective-permute-start(bf16[2,42,1024]{2,1,0:T(8,128)(2,1)S(1)} %slice_bitcast_fusion.14), channel_id=1, source_target_pairs={{0,4},{1,5},{2,6},{3,7},{4,0},{5,1},{6,2},{7,3},{8,12},{9,13},{10,... | collective-permute-start | bytes 516104 | tf_op jit(solution)/shard_map/ppermute | solution.py:85
  107.4 9.5 %collective-permute-start.4 = (bf16[42,1024]{1,0:T(8,128)(2,1)S(1)}, bf16[42,1024]{1,0:T(8,128)(2,1)S(1)}, u32[]{:S(2)}, u32[]{:S(2)}) collective-permute-start(bf16[42,1024]{1,0:T(8,128)(2,1)S(1)} %slice_bitcast_fusion.19), channel_id=1, source_target_pairs={{0,8},{1,9},{2,10},{3,11},{4,12},{5,13},{6,14},{7,15},{8,0},{9,1},... | collective-permute-start | bytes 258056 | tf_op jit(solution)/shard_map/ppermute | solution.py:85
  254.9 9.8 %collective-permute-start = (bf16[128,1024]{1,0:T(8,128)(2,1)}, bf16[128,1024]{1,0:T(8,128)(2,1)S(1)}, u32[]{:S(2)}, u32[]{:S(2)}) collective-permute-start(bf16[128,1024]{1,0:T(8,128)(2,1)} %fusion.86), channel_id=1, source_target_pairs={{0,16},{1,17},{2,18},{3,19},{4,20},{5,21},{6,22},{7,23},{8,24},{9,... | collective-permute-start | bytes 786440 | tf_op jit(solution)/shard_map/ppermute | solution.py:249
  364.7 10.1 %collective-permute-start.5 = (bf16[2,64,1024]{2,1,0:T(8,128)(2,1)}, bf16[2,64,1024]{2,1,0:T(8,128)(2,1)}, u32[]{:S(2)}, u32[]{:S(2)}) collective-permute-start(bf16[2,64,1024]{2,1,0:T(8,128)(2,1)} %add_convert_fusion.3), channel_id=1, source_target_pairs={{16,0},{17,1},{18,2},{19,3},{20,4},{21,5},{22,6},{23,7},{24,8},{25... | collective-permute-start | bytes 786440 | tf_op jit(solution)/shard_map/ppermute | solution.py:256
  372.3 235.5 %all-gather.9.cloned.1.call-start = ((), (), s32[]{:S(2)}) async-start(), calls=%async_computation.2 | async-start | bytes 4456448 | tf_op jit(solution)/shard_map/all_gather | solution.py:105
  444.9 43.6 %collective-permute-start.10 = (bf16[2,2,2,64,2048]{4,3,2,1,0:T(8,128)(2,1)}, bf16[2,2,2,64,2048]{4,3,2,1,0:T(8,128)(2,1)}, u32[]{:S(2)}, u32[]{:S(2)}) collective-permute-start(bf16[2,2,2,64,2048]{4,3,2,1,0:T(8,128)(2,1)} %bitcast.98), channel_id=1, source_target_pairs={{0,1},{1,0},{2,3},{3,2},{4,5},{5,4},{6,7},{7,6},{8,9},{9,8},{10,11... | collective-permute-start | bytes 6291464 | tf_op jit(solution)/shard_map/ppermute | solution.py:85
  468.3 24.2 %collective-permute-start.6 = (bf16[2,2,2,64,3072]{4,3,2,1,0:T(8,128)(2,1)}, bf16[2,2,2,64,3072]{4,3,2,1,0:T(8,128)(2,1)}, u32[]{:S(2)}, u32[]{:S(2)}) collective-permute-start(bf16[2,2,2,64,3072]{4,3,2,1,0:T(8,128)(2,1)} %bitcast.87), channel_id=1, source_target_pairs={{0,1},{1,0},{2,3},{3,2},{4,5},{5,4},{6,7},{7,6},{8,9},{9,8},{10,11... | collective-permute-start | bytes 9437192 | tf_op jit(solution)/shard_map/ppermute | solution.py:85
  477.5 1.3 collective-permute-start.14
  478.8 3.8 collective-permute-start.15
  482.6 3.7 collective-permute-start.16
  486.2 10.4 %collective-permute-start.17 = (f32[8,64]{1,0:T(8,128)S(1)}, f32[8,64]{1,0:T(8,128)S(1)}, u32[]{:S(2)}, u32[]{:S(2)}) collective-permute-start(f32[8,64]{1,0:T(8,128)S(1)} %slice_bitcast_fusion.26), channel_id=1, source_target_pairs={{0,8},{1,9},{2,10},{3,11},{4,12},{5,13},{6,14},{7,15},{8,0},{9,1},... | collective-permute-start | bytes 6152 | tf_op jit(solution)/shard_map/ppermute | solution.py:85
  491.3 32.9 %collective-permute-start.11 = (bf16[2,2,64,2048]{3,2,1,0:T(8,128)(2,1)S(1)}, bf16[2,2,64,2048]{3,2,1,0:T(8,128)(2,1)S(1)}, u32[]{:S(2)}, u32[]{:S(2)}) collective-permute-start(bf16[2,2,64,2048]{3,2,1,0:T(8,128)(2,1)S(1)} %slice_bitcast_fusion.2), channel_id=1, source_target_pairs={{0,2},{1,3},{2,0},{3,1},{4,6},{5,7},{6,4},{7,5},{8,10},{9,11},{10,... | collective-permute-start | bytes 3145736 | tf_op jit(solution)/shard_map/ppermute | solution.py:85
  495.7 66.1 %collective-permute-start.7 = (bf16[2,2,64,3072]{3,2,1,0:T(8,128)(2,1)S(1)}, bf16[2,2,64,3072]{3,2,1,0:T(8,128)(2,1)S(1)}, u32[]{:S(2)}, u32[]{:S(2)}) collective-permute-start(bf16[2,2,64,3072]{3,2,1,0:T(8,128)(2,1)S(1)} %slice_bitcast_fusion), channel_id=1, source_target_pairs={{0,2},{1,3},{2,0},{3,1},{4,6},{5,7},{6,4},{7,5},{8,10},{9,11},{10,... | collective-permute-start | bytes 4718600 | tf_op jit(solution)/shard_map/ppermute | solution.py:85
  524.7 39.5 %collective-permute-start.12 = (bf16[2,64,2048]{2,1,0:T(8,128)(2,1)S(1)}, bf16[2,64,2048]{2,1,0:T(8,128)(2,1)S(1)}, u32[]{:S(2)}, u32[]{:S(2)}) collective-permute-start(bf16[2,64,2048]{2,1,0:T(8,128)(2,1)S(1)} %slice_bitcast_fusion.6), channel_id=1, source_target_pairs={{0,4},{1,5},{2,6},{3,7},{4,0},{5,1},{6,2},{7,3},{8,12},{9,13},{10,... | collective-permute-start | bytes 1572872 | tf_op jit(solution)/shard_map/ppermute | solution.py:85
  562.4 23.2 %collective-permute-start.8 = (bf16[2,64,3072]{2,1,0:T(8,128)(2,1)S(1)}, bf16[2,64,3072]{2,1,0:T(8,128)(2,1)S(1)}, u32[]{:S(2)}, u32[]{:S(2)}) collective-permute-start(bf16[2,64,3072]{2,1,0:T(8,128)(2,1)S(1)} %slice_bitcast_fusion.4), channel_id=1, source_target_pairs={{0,4},{1,5},{2,6},{3,7},{4,0},{5,1},{6,2},{7,3},{8,12},{9,13},{10,... | collective-permute-start | bytes 2359304 | tf_op jit(solution)/shard_map/ppermute | solution.py:85
  564.4 21.7 %collective-permute-start.13 = (bf16[64,2048]{1,0:T(8,128)(2,1)S(1)}, bf16[64,2048]{1,0:T(8,128)(2,1)S(1)}, u32[]{:S(2)}, u32[]{:S(2)}) collective-permute-start(bf16[64,2048]{1,0:T(8,128)(2,1)S(1)} %slice_bitcast_fusion.12), channel_id=1, source_target_pairs={{0,8},{1,9},{2,10},{3,11},{4,12},{5,13},{6,14},{7,15},{8,0},{9,1},... | collective-permute-start | bytes 786440 | tf_op jit(solution)/shard_map/ppermute | solution.py:85
  585.9 16.7 %collective-permute-start.9 = (bf16[64,3072]{1,0:T(8,128)(2,1)S(1)}, bf16[64,3072]{1,0:T(8,128)(2,1)S(1)}, u32[]{:S(2)}, u32[]{:S(2)}) collective-permute-start(bf16[64,3072]{1,0:T(8,128)(2,1)S(1)} %slice_bitcast_fusion.8), channel_id=1, source_target_pairs={{0,8},{1,9},{2,10},{3,11},{4,12},{5,13},{6,14},{7,15},{8,0},{9,1},... | collective-permute-start | bytes 1179656 | tf_op jit(solution)/shard_map/ppermute | solution.py:85
  616.0 19.3 %all-to-all-start.1 = ((bf16[16,64,256]{2,1,0:T(8,128)(2,1)}), bf16[16,64,256]{2,1,0:T(8,128)(2,1)S(1)}, u32[]{:S(2)}, u32[]{:S(2)}) async-start(bf16[16,64,256]{2,1,0:T(8,128)(2,1)} %bitcast.110), calls=%async_computation.1 | async-start | bytes 1048576 | tf_op jit(solution)/shard_map/all_to_all | solution.py:306
  (104 other events, 1151.8 us)
Sparse Core Ops, SparseCore 0:
  11.2 154.1 all-gather.12
  168.2 39.9 all-gather.10
  372.4 52.8 all-gather.14
  480.9 65.7 all-gather.8

commit v2 on v1

v2 whole, which is shorter than its diff:
```python
import functools
import math

import jax
import jax.numpy as jnp
from jax import lax
from jax.experimental import pallas as pl
from jax.experimental.pallas import tpu as pltpu
from jax.sharding import PartitionSpec as P

HEADS = 8
CNEW = 21
BF = jnp.bfloat16
F32 = jnp.float32


def low(value):
    return value.astype(BF)


def dot(first_op, second_op):
    return jnp.dot(first_op, second_op, preferred_element_type=F32)


def dot_t(first_op, second_op):
    return lax.dot_general(first_op, second_op, (((1,), (1,)), ((), ())), preferred_element_type=F32)


def t_dot(first_op, second_op):
    return lax.dot_general(first_op, second_op, (((0,), (0,)), ((), ())), preferred_element_type=F32)


def normalise(values):
    mean_value = jnp.mean(values, -1, keepdims=True)
    centred = values - mean_value
    spread = jnp.mean(centred * centred, -1, keepdims=True)
    scale = lax.rsqrt(spread + 1e-05)
    return centred * scale, scale


def norm_back(hat, scale, grad_hat):
    first = jnp.mean(grad_hat, -1, keepdims=True)
    second = jnp.mean(grad_hat * hat, -1, keepdims=True)
    return scale * (grad_hat - first - hat * second)


def gelu(values):
    return 0.5 * values * (1.0 + jnp.tanh(0.7978845608028654 * (values + 0.044715 * values * values * values)))


def gelu_slope(values):
    inner = jnp.tanh(0.7978845608028654 * (values + 0.044715 * values * values * values))
    return 0.5 * (1.0 + inner) + 0.5 * values * (1.0 - inner * inner) * 0.7978845608028654 * (
        1.0 + 3.0 * 0.044715 * values * values
    )


def sinusoid(key_count, model_width):
    offsets = (key_count - 1 - jnp.arange(key_count)).astype(F32)[:, None]
    inverse_rate = jnp.exp(
        jnp.arange(model_width // 2, dtype=F32) * (-2.0 * math.log(10000.0) / model_width)
    )
    angles = offsets * inverse_rate[None, :]
    return low(jnp.concatenate([jnp.sin(angles), jnp.cos(angles)], 1))


VMEM_BYTES = 60 * 1024 * 1024
ROWS = 128
WIDE = 512


def read_matrix(ref):
    value = ref[...]
    return value.reshape(-1, value.shape[-1])


class Loads:
    def __init__(self, sems):
        self.sems = sems
        self.count = 0

    def start(self, source, target):
        copy = pltpu.make_async_copy(source, target, self.sems.at[self.count])
        self.count += 1
        copy.start()
        return copy


def attend(q_content, q_position, kv, rel, mask, probs, mixed):
    head_dim = q_content.shape[1] // HEADS
    root = 1.0 / math.sqrt(head_dim)
    width = q_content.shape[1]
    half = mask.shape[1]
    for head in range(HEADS):
        cols = slice(head * head_dim, (head + 1) * head_dim)
        full = dot_t(q_position[:, cols], rel[:, cols])
        for seg in range(2):
            own = slice(seg * half, (seg + 1) * half)
            content = dot_t(q_content[own, cols], kv[seg, :, cols])
            position = pltpu.roll(full[own], WIDE - half + 1, 1, stride=1, stride_axis=0)
            scores = (content + position) * root + mask[seg]
            exponent = jnp.exp(scores - jnp.max(scores, 1, keepdims=True))
            chosen = low(exponent / jnp.sum(exponent, 1, keepdims=True))
            if probs is not None:
                probs[seg, head] = chosen
            value = kv[seg, :, slice(width + head * head_dim, width + (head + 1) * head_dim)]
            mixed[own, cols] = low(dot(chosen, value))


def unskew(scores):
    count = scores.shape[0]
    moved = [
        pltpu.roll(scores[start : start + 8], count - 8 - start, 1) if start < count - 8 else scores[start:]
        for start in range(0, count, 8)
    ]
    scores = jnp.concatenate(moved, 0)
    row = lax.broadcasted_iota(jnp.int32, scores.shape, 0)
    for bit in range(3):
        scores = jnp.where(((row >> bit) & 1) == 0, pltpu.roll(scores, 1 << bit, 1), scores)
    return scores


def attend_back(grad_mixed, q_content, q_position, kv, rel, probs, grad_content, grad_position, grad_kv, grad_rel):
    head_dim = q_content.shape[1] // HEADS
    root = 1.0 / math.sqrt(head_dim)
    width = q_content.shape[1]
    half = probs.shape[2]
    past = WIDE - ROWS
    for head in range(HEADS):
        cols = slice(head * head_dim, (head + 1) * head_dim)
        vcols = slice(width + head * head_dim, width + (head + 1) * head_dim)
        total = None
        for seg in range(2):
            own = slice(seg * half, (seg + 1) * half)
            grad_out = grad_mixed[own, cols]
            chosen = probs[seg, head]
            wide = chosen.astype(F32)
            grad_probs = low(dot_t(grad_out, kv[seg, :, vcols])).astype(F32)
            scores = wide * (grad_probs - jnp.sum(wide * grad_probs, 1, keepdims=True)) * root
            grad_scores = low(scores)
            skewed = low(unskew(scores))
            grad_content[own, cols] = low(dot(grad_scores, kv[seg, :, cols]))
            grad_position[own, cols] = low(dot(skewed, rel[:, cols]))
            if grad_rel is None:
                grad_kv[seg, :, cols] = low(t_dot(grad_scores[:, past:], q_content[own, cols]))[:half]
                grad_kv[seg, :, vcols] = low(t_dot(chosen[:, past:], grad_out))[:half]
            else:
                grad_kv[seg, :, cols] = low(t_dot(grad_scores, q_content[own, cols]))
                grad_kv[seg, :, vcols] = low(t_dot(chosen, grad_out))
                term = t_dot(skewed, q_position[own, cols])
                total = term if total is None else total + term
        if grad_rel is not None:
            grad_rel[:, cols] = low(total)


def queries_and_keys(entry, vec, w_in, waits, normed, q_content, q_position, kv):
    width = entry.shape[1]
    half = ROWS // 2
    past = WIDE - ROWS
    hat, _ = normalise(entry)
    flat = low(hat * vec[0:1] + vec[2:3])
    normed[...] = flat
    waits[0].wait()
    query = dot(flat, read_matrix(w_in.at[0]))
    q_content[...] = low(query + vec[6:7])
    q_position[...] = low(query + vec[7:8])
    for part in range(2):
        waits[1 + part].wait()
        value = low(dot(flat, read_matrix(w_in.at[1 + part])))
        for seg in range(2):
            kv[seg, past : past + half, part * width : (part + 1) * width] = value[seg * half : (seg + 1) * half]


def feed_forward(normed_two, hidden_bias, ff_in, ff_out, waits_in, waits_out, keep):
    total = None
    for quarter in range(ff_in.shape[0]):
        waits_in[quarter].wait()
        pre = dot(normed_two, read_matrix(ff_in.at[quarter])) + hidden_bias[quarter : quarter + 1]
        if keep is not None:
            keep[quarter] = pre
        waits_out[quarter].wait()
        term = dot(low(gelu(pre)), read_matrix(ff_out.at[quarter]))
        total = term if total is None else total + term
    return total


def middle_back(cot, middle, vec, ff_in, ff_out, waits_in, waits_out, keep):
    total = None
    for quarter in range(ff_in.shape[0]):
        if waits_out:
            waits_out[quarter].wait()
        grad_pre = low(dot_t(cot, read_matrix(ff_out.at[quarter])) * gelu_slope(keep[quarter]))
        if waits_in:
            waits_in[quarter].wait()
        term = dot_t(grad_pre, read_matrix(ff_in.at[quarter]))
        total = term if total is None else total + term
    hat, scale = normalise(middle)
    return cot.astype(F32) + norm_back(hat, scale, total * vec[1:2]), total, hat


def stage_one(weights, past, rev, entry, vec, hidden_bias, mask, kv, rel, output, w_in, w_out, w_rel, ff_in, ff_out,
              normed, q_content, q_position, mixed, sems):
    loads = Loads(sems)
    rows = w_in.shape[2]
    width = entry.shape[1]
    quarters = ff_in.shape[0]

    def part(index, target):
        return loads.start(weights.at[:, pl.ds(index * rows, rows), :], target)

    key_value = [part(1, w_in.at[1]), part(2, w_in.at[2])]
    wait_rel = part(4, w_rel)
    wait_query = part(0, w_in.at[0])
    wait_out = part(3, w_out)
    share = ff_out.shape[1]
    waits_in, waits_out = [], []
    for quarter in range(quarters):
        waits_in.append(part(5 + quarter, ff_in.at[quarter]))
        waits_out.append(
            loads.start(
                weights.at[pl.ds(quarter * share, share), pl.ds((5 + quarters) * rows, quarters * rows), :],
                ff_out.at[quarter],
            )
        )
    past_len = WIDE - ROWS
    kv[:, past_len + ROWS // 2 :, :] = jnp.zeros((2, ROWS // 2, 2 * width), BF)
    for side in range(2):
        key_value[side].wait()
        for seg in range(2):
            kv[seg, :past_len, side * width : (side + 1) * width] = low(
                dot(past[seg], read_matrix(w_in.at[1 + side]))
            )
    wait_rel.wait()
    rel[...] = low(dot(rev[...], read_matrix(w_rel)))

    class Done:
        def wait(self):
            return None

    wide_entry = entry[...].astype(F32)
    queries_and_keys(wide_entry, vec, w_in, [wait_query, Done(), Done()], normed, q_content, q_position, kv)
    attend(q_content, q_position, kv, rel, mask, None, mixed)
    wait_out.wait()
    middle = wide_entry + dot(mixed[...], read_matrix(w_out))
    hat, _ = normalise(middle)
    normed_two = low(hat * vec[1:2] + vec[3:4])
    total = feed_forward(normed_two, hidden_bias, ff_in, ff_out, waits_in, waits_out, None)
    output[...] = low(middle + total + vec[4:5])


def stage_two(weights, kv_past, rel_hbm, entry, vec, hidden_bias, mask, cot,
              output, normed, q_content, q_position, kv_own, probs, mixed, middle_out, normed_two, pre, grad_low,
              w_in, w_out, ff_in, ff_out, kv, rel, grad_mixed, grad_content, grad_position, grad_kv, sems):
    loads = Loads(sems)
    rows = w_in.shape[2]
    width = entry.shape[1]
    quarters = ff_in.shape[0]
    half = ROWS // 2
    past_len = WIDE - ROWS

    def part(index, target):
        return loads.start(weights.at[:, pl.ds(index * rows, rows), :], target)

    waits = [part(index, w_in.at[index]) for index in range(3)]
    wait_kv = loads.start(kv_past, kv)
    wait_rel = loads.start(rel_hbm, rel)
    wait_out = part(3, w_out)
    share = ff_out.shape[1]
    waits_in, waits_out = [], []
    for quarter in range(quarters):
        waits_in.append(part(5 + quarter, ff_in.at[quarter]))
        waits_out.append(
            loads.start(
                weights.at[pl.ds(quarter * share, share), pl.ds((5 + quarters) * rows, quarters * rows), :],
                ff_out.at[quarter],
            )
        )
    wide_entry = entry[...].astype(F32)
    wait_kv.wait()
    queries_and_keys(wide_entry, vec, w_in, waits, normed, q_content, q_position, kv)
    kv_own[...] = kv[:, past_len : past_len + half, :]
    wait_rel.wait()
    attend(q_content, q_position, kv, rel, mask, probs, mixed)
    wait_out.wait()
    middle = wide_entry + dot(mixed[...], read_matrix(w_out))
    middle_out[...] = middle
    hat, _ = normalise(middle)
    flat = low(hat * vec[1:2] + vec[3:4])
    normed_two[...] = flat
    total = feed_forward(flat, hidden_bias, ff_in, ff_out, waits_in, waits_out, pre)
    output[...] = low(middle_out[...] + total + vec[4:5])

    grad_middle, _, _ = middle_back(cot[...], middle_out[...], vec, ff_in, ff_out, None, None, pre)
    grad_mixed[...] = low(dot_t(low(grad_middle), read_matrix(w_out)))
    attend_back(grad_mixed, q_content, q_position, kv, rel, probs, grad_content, grad_position, grad_kv, None)
    grad_query = low(grad_content[...].astype(F32) + grad_position[...].astype(F32))
    grad_normed = (
        dot_t(grad_query, read_matrix(w_in.at[0]))
        + dot_t(read_matrix(grad_kv.at[:, :, :width]), read_matrix(w_in.at[1]))
        + dot_t(read_matrix(grad_kv.at[:, :, width:]), read_matrix(w_in.at[2]))
    )
    hat_one, scale_one = normalise(entry[...].astype(F32))
    grad_low[...] = low(grad_middle + norm_back(hat_one, scale_one, grad_normed * vec[0:1]))


def place_of(dest, me, bits):
    other = jnp.bitwise_xor(me, dest)
    place = 0
    for bit in range(bits):
        place = place + (((other >> bit) & 1) << (bits - 1 - bit))
    return place


def store_blocks(target, value, first_dest, me, bits, start):
    rows = target.shape[1]
    for index in range(value.shape[0] // rows):
        place = place_of(first_dest + index, me, bits)
        target[place, :, start : start + value.shape[1]] = low(value[index * rows : (index + 1) * rows])


def stage_three(me_ref, weights, kv_past, kv_hbm, rel_hbm, probs_hbm, pre_hbm, rev_hbm, cot, vec, normed, q_content,
                q_position, mixed, middle,
                grad_kv, grad_query, grad_middle_out, sums, first_part,
                w_out, ff_in, ff_out, kv, rel, probs, pre, rev, grad_mixed, grad_content, grad_position, grad_rel,
                sems):
    loads = Loads(sems)
    rows = w_out.shape[1]
    size = w_out.shape[0]
    bits = size.bit_length() - 1
    width = cot.shape[1]
    quarters = ff_in.shape[0]
    half = ROWS // 2
    past_len = WIDE - ROWS
    me = me_ref[0]
    share = ff_out.shape[1]
    waits_in, waits_out = [], []
    wait_pre = loads.start(pre_hbm, pre)
    for quarter in range(quarters):
        waits_out.append(
            loads.start(
                weights.at[pl.ds(quarter * share, share), pl.ds((5 + quarters) * rows, quarters * rows), :],
                ff_out.at[quarter],
            )
        )
        waits_in.append(loads.start(weights.at[:, pl.ds((5 + quarter) * rows, rows), :], ff_in.at[quarter]))
    wait_out = loads.start(weights.at[:, pl.ds(3 * rows, rows), :], w_out)
    others = [
        loads.start(kv_past.at[:, pl.ds(0, past_len), :], kv.at[:, pl.ds(0, past_len), :]),
        loads.start(kv_hbm, kv.at[:, pl.ds(past_len, half), :]),
        loads.start(
            kv_past.at[:, pl.ds(past_len + half, half), :], kv.at[:, pl.ds(past_len + half, half), :]
        ),
        loads.start(rel_hbm, rel),
        loads.start(probs_hbm, probs),
        loads.start(rev_hbm, rev),
    ]
    wait_pre.wait()
    grad_middle, grad_two, hat = middle_back(
        cot[...], middle[...], vec, ff_in, ff_out, waits_in, waits_out, pre
    )
    grad_middle_out[...] = grad_middle
    sums[...] = jnp.zeros(sums.shape, F32)
    sums[1:2] = jnp.sum(grad_two * hat, 0, keepdims=True)
    sums[3:4] = jnp.sum(grad_two, 0, keepdims=True)
    sums[4:5] = jnp.sum(cot[...].astype(F32), 0, keepdims=True)
    grad_branch = low(grad_middle)
    wait_out.wait()
    grad_mixed[...] = low(dot_t(grad_branch, read_matrix(w_out)))
    group = 256
    for index in range(width // group):
        store_blocks(
            first_part,
            t_dot(mixed[:, index * group : (index + 1) * group], grad_branch),
            index * group // rows,
            me,
            bits,
            0,
        )
    for other in others:
        other.wait()
    attend_back(
        grad_mixed, q_content, q_position, kv, rel, probs, grad_content, grad_position, grad_kv, grad_rel
    )
    sums[6:7] = jnp.sum(grad_content[...].astype(F32), 0, keepdims=True)
    sums[7:8] = jnp.sum(grad_position[...].astype(F32), 0, keepdims=True)
    query = low(grad_content[...].astype(F32) + grad_position[...].astype(F32))
    grad_query[...] = query
    for index in range(width // group):
        cols = slice(index * group, (index + 1) * group)
        store_blocks(
            first_part, t_dot(normed[:, cols], query), index * group // rows, me, bits, 2 * width
        )
        store_blocks(
            first_part, t_dot(rev[:, cols], grad_rel[...]), index * group // rows, me, bits, width
        )


def stage_four(me_ref, past_hbm, normed_hbm, grad_kv_hbm, second_part, rows_all, grad_kv, sems):
    loads = Loads(sems)
    size, rows, wide = second_part.shape
    bits = size.bit_length() - 1
    width = wide // 2
    half = ROWS // 2
    past_len = WIDE - ROWS
    me = me_ref[0]
    copies = [
        loads.start(past_hbm, rows_all.at[:, pl.ds(0, past_len), :]),
        loads.start(normed_hbm, rows_all.at[:, pl.ds(past_len, half), :]),
        loads.start(grad_kv_hbm, grad_kv),
    ]
    rows_all[:, past_len + half :, :] = jnp.zeros((2, half, width), BF)
    for copy in copies:
        copy.wait()
    group = 256
    tile = 512
    for index in range(width // group):
        left = read_matrix(rows_all.at[:, :, index * group : (index + 1) * group])
        for start in range(0, wide, tile):
            right = read_matrix(grad_kv.at[:, :, start : start + tile])
            store_blocks(second_part, t_dot(left, right), index * group // rows, me, bits, start)


def stage_five(weights, grad_kv_hbm, comp, mem, entry, grad_query, grad_middle, vec, grad_entry, sums,
               w_in, grad_kv, grad_normed, sems):
    loads = Loads(sems)
    rows = w_in.shape[2]
    width = entry.shape[1]
    half = ROWS // 2
    past_len = WIDE - ROWS
    copies = [loads.start(grad_kv_hbm, grad_kv)] + [
        loads.start(weights.at[:, pl.ds(index * rows, rows), :], w_in.at[index]) for index in range(3)
    ]
    for copy in copies:
        copy.wait()
    tile = 256
    share = tile // rows
    hat_tok, scale_tok = normalise(entry[...].astype(F32))
    parts = [comp[0], mem[0], comp[1], mem[1]]
    hats = [normalise(value.astype(F32))[0] for value in parts]
    hat_past = jnp.concatenate(hats, 0)
    for index in range(width // tile):
        cols = slice(index * tile, (index + 1) * tile)
        w_query, w_key, w_value = (
            read_matrix(w_in.at[which, index * share : (index + 1) * share]) for which in range(3)
        )
        grad_past = dot_t(read_matrix(grad_kv.at[:, :past_len, :width]), w_key) + dot_t(
            read_matrix(grad_kv.at[:, :past_len, width:]), w_value
        )
        own = slice(past_len, past_len + half)
        grad_tok = (
            dot_t(read_matrix(grad_kv.at[:, own, :width]), w_key)
            + dot_t(read_matrix(grad_kv.at[:, own, width:]), w_value)
            + dot_t(grad_query[...], w_query)
        )
        grad_normed[:, cols] = grad_tok
        sums[0:1, cols] = jnp.sum(grad_past * hat_past[:, cols], 0, keepdims=True) + jnp.sum(
            grad_tok * hat_tok[:, cols], 0, keepdims=True
        )
        sums[1:2, cols] = jnp.sum(grad_past, 0, keepdims=True) + jnp.sum(grad_tok, 0, keepdims=True)
    grad_entry[...] = grad_middle[...] + norm_back(hat_tok, scale_tok, grad_normed[...] * vec[0:1])


HBM = pl.BlockSpec(memory_space=pl.ANY)
VMEM = pl.BlockSpec(memory_space=pltpu.VMEM)
SMEM = pl.BlockSpec(memory_space=pltpu.SMEM)


def call(body, name, in_specs, outs, scratch, copies, flops, args):
    return pl.pallas_call(
        body,
        name=name,
        in_specs=in_specs,
        out_specs=[VMEM] * len(outs),
        out_shape=[jax.ShapeDtypeStruct(shape, dtype) for shape, dtype in outs],
        scratch_shapes=[pltpu.VMEM(shape, dtype) for shape, dtype in scratch] + [pltpu.SemaphoreType.DMA((copies,))],
        compiler_params=pltpu.CompilerParams(vmem_limit_bytes=VMEM_BYTES),
        cost_estimate=pl.CostEstimate(flops=flops, bytes_accessed=30_000_000, transcendentals=0),
    )(*args)


def xor_pairs(count, bit):
    return [(i, i ^ bit) for i in range(count)]


def scatter_sum(blocks, order):
    size = lax.axis_size("stream")
    for bit in order:
        got = lax.ppermute(blocks[1], "stream", xor_pairs(size, bit))
        blocks = (blocks[0].astype(F32) + got.astype(F32)).astype(blocks.dtype)
    return blocks


def relative_order(blocks, order):
    size = lax.axis_size("stream")
    me = lax.axis_index("stream")
    index = []
    for position in range(size):
        value = 0
        for place, bit in enumerate(order):
            if (position >> (len(order) - 1 - place)) & 1:
                value |= bit
        index.append(value)
    picked = blocks[jnp.array(index, jnp.int32) ^ me]
    return picked.reshape((2,) * len(order) + blocks.shape[1:])


def gather(shard):
    return lax.all_gather(shard, "stream", axis=0, tiled=False)


def per_device(
    tokens,
    doc_ids,
    memory,
    compressed,
    cot_out,
    cot_comp,
    attn_in,
    attn_out,
    rel_proj,
    ff_in,
    ff_out,
    compress,
    gains,
    biases,
    pos_bias,
    ff_bias,
):
    size = lax.axis_size("stream")
    me = lax.axis_index("stream")
    order = [1 << k for k in range(size.bit_length() - 1)]
    first = lax.axis_index("section") == 0
    micro, seg_len, width = tokens.shape
    rows = attn_in.shape[1]
    hidden_cols = ff_in.shape[2]
    quarters = hidden_cols // width
    my_hidden = hidden_cols // size
    memory, compressed, cot_comp = memory[0], compressed[0], cot_comp[0]
    past_len = compressed.shape[1] + memory.shape[1]
    key_len = past_len + seg_len
    head_dim = width // HEADS
    root = 1.0 / math.sqrt(head_dim)

    small = jnp.concatenate(
        [low(gains[0]).T, low(biases[0]).T, low(pos_bias[0]).T, low(ff_bias[0]).reshape(quarters, rows)], 0
    )
    small = gather(small).transpose(1, 0, 2).reshape(-1, width).astype(F32)
    gain_one, gain_two = small[0], small[1]
    bias_one, bias_two, bias_out = small[2], small[3], small[4]
    pos_content, pos_position = small[6], small[7]
    hidden_bias = small[8:].reshape(quarters, size, rows).transpose(1, 0, 2).reshape(hidden_cols)

    low_in, low_ff_in, low_ff_out = low(attn_in[0]), low(ff_in[0]), low(ff_out[0])
    shard = jnp.concatenate(
        [low_in[:, i * width : (i + 1) * width] for i in range(3)]
        + [low(attn_out[0]), low(rel_proj[0])]
        + [low_ff_in[:, i * width : (i + 1) * width] for i in range(quarters)]
        + [low_ff_out],
        0,
    )
    weights = gather(shard)

    def part(start, count=1):
        return weights[:, start * rows : (start + count) * rows].reshape(size * count * rows, width)

    comp_rows = compress.shape[1]
    windows = memory[:, : 3 * CNEW].reshape(micro * CNEW, size, comp_rows).transpose(1, 0, 2)
    windows = lax.all_to_all(windows, "stream", 0, 0, tiled=True)
    partial = dot(windows.reshape(-1, comp_rows), low(compress[0]))
    partial = low(partial).reshape(size, micro * CNEW, width)
    squeezed = scatter_sum(relative_order(partial, order), order)
    side_all = gather(cot_comp.reshape(micro * CNEW, width)).reshape(-1, width)
    grad_compress = t_dot(windows.reshape(-1, comp_rows), side_all)

    past = jnp.concatenate([compressed, memory], 1).astype(F32)
    past_normed = low(normalise(past)[0] * gain_one + bias_one)
    rev = jnp.pad(sinusoid(key_len, width), ((0, WIDE - key_len), (0, 0)))
    keys = jnp.pad(doc_ids, ((0, 0), (0, WIDE - key_len)), constant_values=-1)
    allowed = (jnp.arange(WIDE)[None, :] <= jnp.arange(seg_len)[:, None] + past_len) & (
        keys[:, None, :] == doc_ids[:, past_len:, None]
    )
    mask = jnp.where(allowed, 0.0, -1e30).astype(F32)
    vec = small[:8]
    bias_rows = hidden_bias.reshape(quarters, width)
    flat_tokens = tokens.reshape(-1, width)
    flat_rows = flat_tokens.shape[0]
    assert flat_rows == ROWS and key_len <= WIDE

    in_scratch = ((3, size, rows, width), BF)
    mat_scratch = ((size, rows, width), BF)
    ff_in_scratch = ((quarters, size, rows, width), BF)
    ff_out_scratch = ((quarters, size // quarters, quarters * rows, width), BF)
    flat_low = ((ROWS, width), BF)
    flat_wide = ((ROWS, width), F32)
    kv_all = ((micro, WIDE, 2 * width), BF)
    kv_tok = ((micro, seg_len, 2 * width), BF)
    rel_all = ((WIDE, width), BF)
    prob_all = ((micro, HEADS, seg_len, WIDE), BF)
    pre_all_shape = ((quarters, ROWS, width), F32)

    kv_past, rel, output = call(
        stage_one,
        "first_forward",
        [HBM] + [VMEM] * 6,
        [kv_all, rel_all, flat_low],
        [in_scratch, mat_scratch, mat_scratch, ff_in_scratch, ff_out_scratch] + [flat_low] * 4,
        5 + 2 * quarters,
        7_000_000_000,
        (weights, past_normed, rev, flat_tokens, vec, bias_rows, mask),
    )
    received = lax.ppermute(output, "section", [(0, 1)])
    entry = jnp.where(first, flat_tokens, received)
    (output, normed, q_content, q_position, kv_own, probs, mixed, middle, normed_two, pre, grad_low) = call(
        stage_two,
        "second_forward_and_back",
        [HBM] * 3 + [VMEM] * 5,
        [flat_low, flat_low, flat_low, flat_low, kv_tok, prob_all, flat_low, flat_wide, flat_low, pre_all_shape,
         flat_low],
        [in_scratch, mat_scratch, ff_in_scratch, ff_out_scratch, kv_all, rel_all, flat_low, flat_low, flat_low, kv_tok],
        6 + 2 * quarters,
        7_000_000_000,
        (weights, kv_past, rel, entry, vec, bias_rows, mask, cot_out.reshape(-1, width)),
    )
    returned = lax.ppermute(grad_low, "section", [(1, 0)])
    cot = jnp.where(first, returned, cot_out.reshape(-1, width))
    both = gather(jnp.concatenate([normed_two, cot], 0))
    normed_all = both[:, :ROWS].reshape(-1, width)
    cot_all = both[:, ROWS:].reshape(-1, width)
    me_ref = me.reshape(1).astype(jnp.int32)
    grad_kv, grad_query, grad_middle, sums, first_part = call(
        stage_three,
        "first_gradients",
        [SMEM] + [HBM] * 7 + [VMEM] * 7,
        [kv_all, flat_low, flat_wide, ((8, width), F32), ((size, rows, 3 * width), BF)],
        [mat_scratch, ff_in_scratch, ff_out_scratch, kv_all, rel_all, prob_all, pre_all_shape, rel_all,
         flat_low, flat_low, flat_low, rel_all],
        8 + 2 * quarters,
        7_000_000_000,
        (me_ref, weights, kv_past, kv_own, rel, probs, pre, rev, cot, vec, normed, q_content, q_position, mixed,
         middle),
    )
    first_sum = scatter_sum(first_part.reshape((2,) * len(order) + first_part.shape[1:]), order)
    (second_part,) = call(
        stage_four,
        "key_value_gradients",
        [SMEM] + [HBM] * 3,
        [((size, rows, 2 * width), BF)],
        [((micro, WIDE, width), BF), kv_all],
        3,
        4_300_000_000,
        (me_ref, past_normed, normed.reshape(micro, seg_len, width), grad_kv),
    )
    second_sum = scatter_sum(second_part.reshape((2,) * len(order) + second_part.shape[1:]), order)
    grad_entry, more = call(
        stage_five,
        "entry_gradient",
        [HBM] * 2 + [VMEM] * 6,
        [flat_wide, ((2, width), F32)],
        [in_scratch, kv_all, flat_wide],
        4,
        4_300_000_000,
        (weights, grad_kv, compressed, memory, entry, grad_query, grad_middle, vec),
    )
    grad_attn_out = first_sum[:, :width].astype(F32)
    grad_rel = first_sum[:, width : 2 * width].astype(F32)
    grad_attn_in = jnp.concatenate([first_sum[:, 2 * width :], second_sum], 1).astype(F32)

    vectors = jnp.stack(
        [more[0], sums[1], more[1], sums[3], sums[4], jnp.sum(cot_comp.astype(F32), (0, 1)), sums[6], sums[7]]
    )
    vectors = vectors.reshape(8, size, rows).transpose(1, 0, 2)
    vectors = scatter_sum(relative_order(vectors, order), order)
    entry = entry.reshape(tokens.shape)
    grad_entry = grad_entry.reshape(tokens.shape)
    w_ff_in = jnp.concatenate([part(5 + i) for i in range(quarters)], 1)

    start = me * my_hidden
    mine_in = lax.dynamic_slice(w_ff_in, (0, start), (width, my_hidden))
    mine_bias = lax.dynamic_slice(hidden_bias, (start,), (my_hidden,))
    pre_all = dot(normed_all, mine_in) + mine_bias
    active_all = low(gelu(pre_all))
    slope_all = gelu_slope(pre_all)
    grad_pre_all = low(dot_t(cot_all, low_ff_out) * slope_all)
    grad_ff_out = t_dot(active_all, cot_all)
    grad_ff_in = t_dot(normed_all, grad_pre_all)
    grad_ff_bias = jnp.sum(grad_pre_all.astype(F32), 0)
    grad_ff_in = lax.all_to_all(low(grad_ff_in).reshape(size, rows, my_hidden), "stream", 0, 0, tiled=True)
    grad_ff_in = grad_ff_in.transpose(1, 0, 2).reshape(rows, hidden_cols).astype(F32)

    activations = low(output).reshape(tokens.shape)
    new_memory = jnp.concatenate([memory[:, seg_len:], entry], 1)
    squeezed = low(squeezed.astype(F32) + small[5]).reshape(micro, CNEW, width)
    new_compressed = jnp.concatenate([compressed[:, CNEW:], squeezed], 1)
    return tuple(
        value[None]
        for value in (
            activations,
            new_memory,
            new_compressed,
            grad_entry,
            grad_attn_in,
            grad_attn_out,
            grad_rel,
            grad_ff_in,
            grad_ff_out,
            grad_compress,
            vectors[:2].T,
            vectors[2:6].T,
            vectors[6:].T,
            grad_ff_bias,
        )
    )


def solution(mesh):
    in_specs = (
        P("stream", None, None),
        P("stream", None),
        P("section", "stream", None, None),
        P("section", "stream", None, None),
        P("stream", None, None),
        P("section", "stream", None, None),
    ) + (P("section", "stream", None),) * 9 + (P("section", "stream"),)
    out_specs = (
        (P("section", "stream", None, None),) * 4 + (P("section", "stream", None),) * 9 + (P("section", "stream"),)
    )
    return jax.shard_map(
        per_device, mesh=mesh, in_specs=in_specs, out_specs=out_specs, check_vma=False
    )
```

time: 651 us -> 492 us (0.76)
  matrix products: 152 us -> 15.7 us
  Pallas kernels: 0 us -> 110 us
  local copies, waits for them, and re-layouts: 164 us -> 54.4 us
  other arithmetic: 67.5 us -> 27.2 us
  waiting for transfers between devices: 186 us -> 208 us
    pallas_call x0 -> x5, Pallas kernels: none -> 110 us  [call(): pl.pallas_call(body, name=name, in_specs=in_specs, out_specs=[VMEM] * len...]
    all_gather x4 -> x3, waiting for transfers between devices: 47.6 us -> 93.2 us  [gather(): return lax.all_gather(shard, 'stream', axis=0, tiled=False)]
    dot_general x10 -> x1, matrix products: 47.5 us -> 2.89 us  [dot_t(): lax.dot_general(first_op, second_op, (((1,), (1,)), ((), ())), preferred_...]
    dot_general x13 -> x2, matrix products: 43.6 us -> 3.33 us  [dot(): return jnp.dot(first_op, second_op, preferred_element_type=F32)]
    reshape x12 -> x1, local copies, waits for them, and re-layouts: 34.2 us -> 0.08 us  [per_device(): small[8:].reshape(quarters, size, rows).transpose(1, 0, 2)]
    dot_general x14 -> x0, matrix products: 33.5 us -> none  [the longest x2 8.14 us: backward(): jnp.einsum('bhsk,bshd->bkhd', grad_scores, q_content, preferred_element_t...]
    ppermute x16, waiting for transfers between devices: 128 us -> 94.9 us  [scatter_sum(): got = lax.ppermute(blocks[1], 'stream', xor_pairs(size, bit))]
    rev x2 -> x0, local copies, waits for them, and re-layouts: 23.1 us -> none  [the longest x1 12.9 us: per_device(): relative = low(dot(sinusoid(key_len, width), w_rel))[::-1]]
  transfers between devices with their start and end apart: 24 -> 23, of which waited for: 14 -> 10; matrix products, arithmetic and copies ran while one was open for 41% -> 16% of each run, Pallas kernels for 0% -> 23%
where the time goes in v2:
time: 492 us; the launch traced here: 487 us
  waiting for transfers between devices  208 us (42%)
  Pallas kernels  110 us (22%)
  local copies, waits for them, and re-layouts  54.4 us (11%)
  starting transfers between devices  29.1 us (6%)
  blocking collectives  28.2 us (6%)
  other arithmetic  27.2 us (6%)
  matrix products  15.7 us (3%)
  between operations  15 us (3%)
    pallas_call x5, Pallas kernels, call(): pl.pallas_call(body, name=name, in_specs=in_specs, out_specs=[VMEM] * len...  110 us
    ppermute x16, waiting for transfers between devices, scatter_sum(): got = lax.ppermute(blocks[1], 'stream', xor_pairs(size, bit))  94.9 us
    all_gather x3, waiting for transfers between devices, gather(): return lax.all_gather(shard, 'stream', axis=0, tiled=False)  93.2 us
    all_gather x1, blocking collectives, gather(): return lax.all_gather(shard, 'stream', axis=0, tiled=False)  28.2 us
    ppermute x16, starting transfers between devices, scatter_sum(): got = lax.ppermute(blocks[1], 'stream', xor_pairs(size, bit))  11.8 us
    slice x4, local copies, waits for them, and re-layouts, scatter_sum(): got = lax.ppermute(blocks[1], 'stream', xor_pairs(size, bit))  11.7 us
  transfers between devices with their start and end apart: 23, of which 10 were waited for; matrix products, arithmetic and copies ran while one was open for 16% of the time, Pallas kernels for 23%

profile of v2, /device:TPU:0, one launch (start us, length us, event | category | flops | bytes accessed | tf_op | source)
XLA Modules:
  0.0 487.5 jit_solution(5684532269399420050)
XLA Ops:
  12.5 7.4 %all-to-all-start = ((bf16[16,42,192]{2,1,0:T(8,128)(2,1)}), bf16[16,42,192]{2,1,0:T(8,128)(2,1)S(1)}, u32[]{:S(2)}, u32[]{:S(2)}) async-start(bf16[16,42,192]{2,1,0:T(8,128)(2,1)} %bitcast.199), calls=%async_computation | async-start | bytes 786432 | tf_op jit(solution)/shard_map/all_to_all | solution.py:568
  20.9 28.2 %all-gather.3 = bf16[16,12,64]{2,1,0:T(8,128)(2,1)S(1)} all-gather(bf16[1,12,64]{2,1,0:T(8,128)(2,1)S(1)} %maximum_bitcast_fusion.2), channel_id=3, replica_groups=mesh['section'=2,'stream'=16] {'stream'}, dimensions={0}, use_global_device_ids=true | all-gather | bytes 26112 | tf_op jit(solution)/shard_map/all_gather | solution.py:508
  50.2 3.6 fusion.26
  72.2 93.2 %all-gather.10.cloned.1.call-done = bf16[13312,1024]{1,0:T(8,128)(2,1)} async-done(((bf16[832,1024]{1,0:T(8,128)(2,1)}), bf16[13312,1024]{1,0:T(8,128)(2,1)}) %all-gather.10.cloned.1.call-update) | async-done | bytes 27262992 | tf_op jit(solution)/shard_map/all_gather | solution.py:508
  165.4 21.9 %first_forward.1 = (bf16[2,512,2048]{2,1,0:T(8,128)(2,1)}, bf16[512,1024]{1,0:T(8,128)(2,1)}, bf16[128,1024]{1,0:T(8,128)(2,1)}) custom-call(bf16[16,832,1024]{2,1,0:T(8,128)(2,1)} %bitcast.200, bf16[2,384,1024]{2,1,0:T(8,128)(2,1)} %fusion.7.past.past_hbm, bf16[512,1024]{1,0:T(8,128)(2,1)} %fusion.20.rev.rev_hbm, bf16[128,1024]{1,0:T(8,128)(2,1)} %bitcast.230, ...), custom_call_target="tpu_custom_call" | custom-call | flops 7000000000 | bytes 30000000 | tf_op jit(solution)/shard_map/first_forward/pallas_call | solution.py:469
  187.4 3.4 collective-permute-start
  192.0 5.0 %collective-permute-done = bf16[128,1024]{1,0:T(8,128)(2,1)S(1)} collective-permute-done((bf16[128,1024]{1,0:T(8,128)(2,1)}, bf16[128,1024]{1,0:T(8,128)(2,1)S(1)}, u32[]{:S(2)}, u32[]{:S(2)}) %collective-permute-start) | collective-permute-done | bytes 262176 | tf_op jit(solution)/shard_map/ppermute | solution.py:611
  197.8 36.9 %second_forward_and_back.1 = (bf16[128,1024]{1,0:T(8,128)(2,1)}, bf16[128,1024]{1,0:T(8,128)(2,1)}, bf16[128,1024]{1,0:T(8,128)(2,1)}, bf16[128,1024]{1,0:T(8,12...) custom-call(bf16[16,832,1024]{2,1,0:T(8,128)(2,1)} %bitcast.201, ...), custom_call_target="tpu_custom_call" | custom-call | flops 7000000000 | bytes 30000000 | tf_op jit(solution)/shard_map/second_forward_and_back/pallas_call | solution.py:469
  238.6 6.2 %collective-permute-done.5 = bf16[128,1024]{1,0:T(8,128)(2,1)S(1)} collective-permute-done((bf16[128,1024]{1,0:T(8,128)(2,1)}, bf16[128,1024]{1,0:T(8,128)(2,1)S(1)}, u32[]{:S(2)}, u32[]{:S(2)}) %collective-permute-start.5) | collective-permute-done | bytes 262176 | tf_op jit(solution)/shard_map/ppermute | solution.py:624
  247.3 5.1 %collective-permute-done.4 = bf16[42,1024]{1,0:T(8,128)(2,1)S(1)} collective-permute-done((bf16[42,1024]{1,0:T(8,128)(2,1)S(1)}, bf16[42,1024]{1,0:T(8,128)(2,1)S(1)}, u32[]{:S(2)}, u32[]{:S(2)}) %collective-permute-start.4) | collective-permute-done | bytes 86048 | tf_op jit(solution)/shard_map/ppermute | solution.py:488
  253.4 29.5 %first_gradients.1 = (bf16[2,512,2048]{2,1,0:T(8,128)(2,1)}, bf16[128,1024]{1,0:T(8,128)(2,1)}, f32[128,1024]{1,0:T(8,128)}, f32[8,1024]{1,0:T(8,128)}, bf16[16,64,3072]{2,1,0:T(8,128)(2,1)}) custom-call(s32[1]{0:T(128)} %bitcast.33.me_ref, bf16[16,832,1024]{2,1,0:T(8,128)(2,1)} %bitcast.202, bf16[2,512,2048]{2,1,0:T(8,128)(2,1)} %get-tuple-element.35.kv_past, ...), custom_call_target="tpu_custom_call" | custom-call | flops 7000000000 | bytes 30000000 | tf_op jit(solution)/shard_map/first_gradients/pallas_call | solution.py:469
  282.8 9.4 %key_value_gradients.1 = bf16[16,64,2048]{2,1,0:T(8,128)(2,1)} custom-call(s32[1]{0:T(128)} %bitcast.33.me_ref, bf16[2,384,1024]{2,1,0:T(8,128)(2,1)} %fusion.7.past.past_hbm, bf16[2,64,1024]{2,1,0:T(8,128)(2,1)} %bitcast.233, bf16[2,512,2048]{2,1,0:T(8,128)(2,1)} %get-tuple-element.48.grad_kv_hbm), custom_call_target="tpu_custom_call" | custom-call | flops 4300000256 | bytes 30000000 | tf_op jit(solution)/shard_map/key_value_gradients/pallas_call | solution.py:469
  292.2 5.0 %fusion.58 = (bf16[8,64,2048]{2,1,0:T(8,128)(2,1)}, bf16[8,64,2048]{2,1,0:T(8,128)(2,1)}) fusion(bf16[16,64,2048]{2,1,0:T(8,128)(2,1)} %key_value_gradients.1), kind=kLoop, calls=%fused_computation.163 | loop fusion | bytes 8388608 | tf_op jit(solution)/shard_map/slice | solution.py:488
  297.2 5.2 %fusion.57 = (bf16[8,64,3072]{2,1,0:T(8,128)(2,1)}, bf16[8,64,3072]{2,1,0:T(8,128)(2,1)S(1)}) fusion(bf16[16,64,3072]{2,1,0:T(8,128)(2,1)} %get-tuple-element.52), kind=kLoop, calls=%fused_computation.162 | loop fusion | bytes 12582912 | tf_op jit(solution)/shard_map/slice | solution.py:488
  302.9 12.7 %entry_gradient.1 = (f32[128,1024]{1,0:T(8,128)}, f32[2,1024]{1,0:T(2,128)}) custom-call(bf16[16,832,1024]{2,1,0:T(8,128)(2,1)} %bitcast.203, bf16[2,512,2048]{2,1,0:T(8,128)(2,1)} %get-tuple-element.48.grad_kv_hbm, bf16[2,128,1024]{2,1,0:T(8,128)(2,1)} %bitcast.214, bf16[2,256,1024]{2,1,0:T(8,128)(2,1)} %bitcast.205, ...), custom_call_target="tpu_custom_call" | custom-call | flops 4300000256 | bytes 30000000 | tf_op jit(solution)/shard_map/entry_gradient/pallas_call | solution.py:469
  332.8 6.2 %fusion.55 = (bf16[16,64,1024]{2,1,0:T(8,128)(2,1)}, bf16[16,64,1024]{2,1,0:T(8,128)(2,1)}, bf16[16,64,1024]{2,1,0:T(8,128)(2,1)}, bf16[16,64,1024]{2,1,0:T(8,128)(2,1)}) fusion(bf16[16,832,1024]{2,1,0:T(8,128)(2,1)} %bitcast.204), kind=kLoop, calls=%fused_computation.160 | loop fusion | bytes 16777216 | tf_op jit(solution)/shard_map/slice | solution.py:564
  352.2 19.7 %collective-permute-done.11 = bf16[2,2,64,2048]{3,2,1,0:T(8,128)(2,1)S(1)} collective-permute-done((bf16[2,2,64,2048]{3,2,1,0:T(8,128)(2,1)S(1)}, bf16[2,2,64,2048]{3,2,1,0:T(8,128)(2,1)S(1)}, u32[]{:S(2)}, u32[]{:S(2)}) %collective-permute-start.11) | collective-permute-done | bytes 1048608 | tf_op jit(solution)/shard_map/ppermute | solution.py:488
  374.4 29.3 %collective-permute-done.7 = bf16[2,2,64,3072]{3,2,1,0:T(8,128)(2,1)S(1)} collective-permute-done((bf16[2,2,64,3072]{3,2,1,0:T(8,128)(2,1)S(1)}, bf16[2,2,64,3072]{3,2,1,0:T(8,128)(2,1)S(1)}, u32[]{:S(2)}, u32[]{:S(2)}) %collective-permute-start.7) | collective-permute-done | bytes 1572896 | tf_op jit(solution)/shard_map/ppermute | solution.py:488
  406.9 20.9 %collective-permute-done.8 = bf16[2,64,3072]{2,1,0:T(8,128)(2,1)S(1)} collective-permute-done((bf16[2,64,3072]{2,1,0:T(8,128)(2,1)S(1)}, bf16[2,64,3072]{2,1,0:T(8,128)(2,1)S(1)}, u32[]{:S(2)}, u32[]{:S(2)}) %collective-permute-start.8) | collective-permute-done | bytes 786464 | tf_op jit(solution)/shard_map/ppermute | solution.py:488
  428.2 17.2 %collective-permute-done.9 = bf16[64,3072]{1,0:T(8,128)(2,1)S(1)} collective-permute-done((bf16[64,3072]{1,0:T(8,128)(2,1)S(1)}, bf16[64,3072]{1,0:T(8,128)(2,1)S(1)}, u32[]{:S(2)}, u32[]{:S(2)}) %collective-permute-start.9) | collective-permute-done | bytes 393248 | tf_op jit(solution)/shard_map/ppermute | solution.py:488
  445.6 4.1 fusion.56
  459.6 4.8 all-to-all-start.1
  466.2 4.6 convolution_bitcast_fusion
  470.7 8.1 %all-to-all-done.1 = bf16[16,64,256]{2,1,0:T(8,128)(2,1)S(1)} async-done(((bf16[16,64,256]{2,1,0:T(8,128)(2,1)}), bf16[16,64,256]{2,1,0:T(8,128)(2,1)S(1)}, u32[]{:S(2)}, u32[]{:S(2)}) %all-to-all-start.1) | async-done | bytes 524320 | tf_op jit(solution)/shard_map/all_to_all | solution.py:687
  (227 shorter events, 84.8 us)
Async XLA Ops:
  7.2 158.2 %all-gather.10.cloned.1.call-start = ((), (), s32[]{:S(2)}) async-start(), calls=%async_computation.3 | async-start | bytes 28966912 | tf_op jit(solution)/shard_map/all_gather | solution.py:508
  11.2 38.1 %copy-start.1 = (bf16[1,2,128,1024]{3,2,1,0:T(8,128)(2,1)S(1)}, bf16[1,2,128,1024]{3,2,1,0:T(8,128)(2,1)}, u32[]{:S(2)}) copy-start(bf16[1,2,128,1024]{3,2,1,0:T(8,128)(2,1)} %param.21) | copy-start | bytes 1572868
  12.5 47.0 %all-to-all-start = ((bf16[16,42,192]{2,1,0:T(8,128)(2,1)}), bf16[16,42,192]{2,1,0:T(8,128)(2,1)S(1)}, u32[]{:S(2)}, u32[]{:S(2)}) async-start(bf16[16,42,192]{2,1,0:T(8,128)(2,1)} %bitcast.199), calls=%async_computation | async-start | bytes 786432 | tf_op jit(solution)/shard_map/all_to_all | solution.py:568
  19.9 307.9 %all-gather.8.cloned.1.call-start = ((), (), s32[]{:S(2)}) async-start(), calls=%async_computation.2 | async-start | bytes 1671168 | tf_op jit(solution)/shard_map/all_gather | solution.py:508
  20.6 424.9 %all-gather.12.cloned.1.call-start = ((), (), s32[]{:S(2)}) async-start(), calls=%async_computation.4 | async-start | bytes 8912896 | tf_op jit(solution)/shard_map/all_gather | solution.py:508
  66.8 3.1 collective-permute-start.1
  70.2 120.6 %collective-permute-start.2 = (bf16[2,2,42,1024]{3,2,1,0:T(8,128)(2,1)S(1)}, bf16[2,2,42,1024]{3,2,1,0:T(8,128)(2,1)}, u32[]{:S(2)}, u32[]{:S(2)}) collective-permute-start(bf16[2,2,42,1024]{3,2,1,0:T(8,128)(2,1)S(1)} %slice_bitcast_fusion.10), channel_id=1, source_target_pairs={{0,2},{1,3},{2,0},{3,1},{4,6},{5,7},{6,4},{7,5},{8,10},{9,11},{10,... | collective-permute-start | bytes 1032200 | tf_op jit(solution)/shard_map/ppermute | solution.py:488
  187.4 9.7 %collective-permute-start = (bf16[128,1024]{1,0:T(8,128)(2,1)}, bf16[128,1024]{1,0:T(8,128)(2,1)S(1)}, u32[]{:S(2)}, u32[]{:S(2)}) collective-permute-start(bf16[128,1024]{1,0:T(8,128)(2,1)} %get-tuple-element.37), channel_id=1, source_target_pairs={{0,16},{1,17},{2,18},{3,19},{4,20},{5,21},{6,22},{7,23},{8,24},{9,... | collective-permute-start | bytes 786440 | tf_op jit(solution)/shard_map/ppermute | solution.py:611
  191.9 45.7 %collective-permute-start.3 = (bf16[2,42,1024]{2,1,0:T(8,128)(2,1)S(1)}, bf16[2,42,1024]{2,1,0:T(8,128)(2,1)}, u32[]{:S(2)}, u32[]{:S(2)}) collective-permute-start(bf16[2,42,1024]{2,1,0:T(8,128)(2,1)S(1)} %slice_bitcast_fusion.14), channel_id=1, source_target_pairs={{0,4},{1,5},{2,6},{3,7},{4,0},{5,1},{6,2},{7,3},{8,12},{9,13},{10,... | collective-permute-start | bytes 516104 | tf_op jit(solution)/shard_map/ppermute | solution.py:488
  234.8 10.0 %collective-permute-start.5 = (bf16[128,1024]{1,0:T(8,128)(2,1)}, bf16[128,1024]{1,0:T(8,128)(2,1)S(1)}, u32[]{:S(2)}, u32[]{:S(2)}) collective-permute-start(bf16[128,1024]{1,0:T(8,128)(2,1)} %get-tuple-element.42), channel_id=1, source_target_pairs={{16,0},{17,1},{18,2},{19,3},{20,4},{21,5},{22,6},{23,7},{24,8},{25... | collective-permute-start | bytes 786440 | tf_op jit(solution)/shard_map/ppermute | solution.py:624
  245.8 6.6 %collective-permute-start.4 = (bf16[42,1024]{1,0:T(8,128)(2,1)S(1)}, bf16[42,1024]{1,0:T(8,128)(2,1)S(1)}, u32[]{:S(2)}, u32[]{:S(2)}) collective-permute-start(bf16[42,1024]{1,0:T(8,128)(2,1)S(1)} %slice_bitcast_fusion.19), channel_id=1, source_target_pairs={{0,8},{1,9},{2,10},{3,11},{4,12},{5,13},{6,14},{7,15},{8,0},{9,1},... | collective-permute-start | bytes 258056 | tf_op jit(solution)/shard_map/ppermute | solution.py:488
  297.2 46.1 %collective-permute-start.10 = (bf16[2,2,2,64,2048]{4,3,2,1,0:T(8,128)(2,1)}, bf16[2,2,2,64,2048]{4,3,2,1,0:T(8,128)(2,1)}, u32[]{:S(2)}, u32[]{:S(2)}) collective-permute-start(bf16[2,2,2,64,2048]{4,3,2,1,0:T(8,128)(2,1)} %bitcast.46), channel_id=1, source_target_pairs={{0,1},{1,0},{2,3},{3,2},{4,5},{5,4},{6,7},{7,6},{8,9},{9,8},{10,11... | collective-permute-start | bytes 6291464 | tf_op jit(solution)/shard_map/ppermute | solution.py:488
  302.4 45.1 %collective-permute-start.6 = (bf16[2,2,2,64,3072]{4,3,2,1,0:T(8,128)(2,1)}, bf16[2,2,2,64,3072]{4,3,2,1,0:T(8,128)(2,1)}, u32[]{:S(2)}, u32[]{:S(2)}) collective-permute-start(bf16[2,2,2,64,3072]{4,3,2,1,0:T(8,128)(2,1)} %bitcast.36), channel_id=1, source_target_pairs={{0,1},{1,0},{2,3},{3,2},{4,5},{5,4},{6,7},{7,6},{8,9},{9,8},{10,11... | collective-permute-start | bytes 9437192 | tf_op jit(solution)/shard_map/ppermute | solution.py:488
  327.7 2.8 collective-permute-start.14
  331.3 7.6 %collective-permute-start.15 = (f32[2,2,8,64]{3,2,1,0:T(8,128)S(1)}, f32[2,2,8,64]{3,2,1,0:T(8,128)S(1)}, u32[]{:S(2)}, u32[]{:S(2)}) collective-permute-start(f32[2,2,8,64]{3,2,1,0:T(8,128)S(1)} %slice_bitcast_fusion.22), channel_id=1, source_target_pairs={{0,2},{1,3},{2,0},{3,1},{4,6},{5,7},{6,4},{7,5},{8,10},{9,11},{10,... | collective-permute-start | bytes 24584 | tf_op jit(solution)/shard_map/ppermute | solution.py:488
  339.0 3.7 collective-permute-start.16
  342.7 8.3 %collective-permute-start.17 = (f32[8,64]{1,0:T(8,128)S(1)}, f32[8,64]{1,0:T(8,128)S(1)}, u32[]{:S(2)}, u32[]{:S(2)}) collective-permute-start(f32[8,64]{1,0:T(8,128)S(1)} %slice_bitcast_fusion.26), channel_id=1, source_target_pairs={{0,8},{1,9},{2,10},{3,11},{4,12},{5,13},{6,14},{7,15},{8,0},{9,1},... | collective-permute-start | bytes 6152 | tf_op jit(solution)/shard_map/ppermute | solution.py:488
  345.7 26.2 %collective-permute-start.11 = (bf16[2,2,64,2048]{3,2,1,0:T(8,128)(2,1)S(1)}, bf16[2,2,64,2048]{3,2,1,0:T(8,128)(2,1)S(1)}, u32[]{:S(2)}, u32[]{:S(2)}) collective-permute-start(bf16[2,2,64,2048]{3,2,1,0:T(8,128)(2,1)S(1)} %slice_bitcast_fusion.2), channel_id=1, source_target_pairs={{0,2},{1,3},{2,0},{3,1},{4,6},{5,7},{6,4},{7,5},{8,10},{9,11},{10,... | collective-permute-start | bytes 3145736 | tf_op jit(solution)/shard_map/ppermute | solution.py:488
  350.6 53.1 %collective-permute-start.7 = (bf16[2,2,64,3072]{3,2,1,0:T(8,128)(2,1)S(1)}, bf16[2,2,64,3072]{3,2,1,0:T(8,128)(2,1)S(1)}, u32[]{:S(2)}, u32[]{:S(2)}) collective-permute-start(bf16[2,2,64,3072]{3,2,1,0:T(8,128)(2,1)S(1)} %slice_bitcast_fusion), channel_id=1, source_target_pairs={{0,2},{1,3},{2,0},{3,1},{4,6},{5,7},{6,4},{7,5},{8,10},{9,11},{10,... | collective-permute-start | bytes 4718600 | tf_op jit(solution)/shard_map/ppermute | solution.py:488
  372.4 33.8 %collective-permute-start.12 = (bf16[2,64,2048]{2,1,0:T(8,128)(2,1)S(1)}, bf16[2,64,2048]{2,1,0:T(8,128)(2,1)S(1)}, u32[]{:S(2)}, u32[]{:S(2)}) collective-permute-start(bf16[2,64,2048]{2,1,0:T(8,128)(2,1)S(1)} %slice_bitcast_fusion.6), channel_id=1, source_target_pairs={{0,4},{1,5},{2,6},{3,7},{4,0},{5,1},{6,2},{7,3},{8,12},{9,13},{10,... | collective-permute-start | bytes 1572872 | tf_op jit(solution)/shard_map/ppermute | solution.py:488
  404.4 23.4 %collective-permute-start.8 = (bf16[2,64,3072]{2,1,0:T(8,128)(2,1)S(1)}, bf16[2,64,3072]{2,1,0:T(8,128)(2,1)S(1)}, u32[]{:S(2)}, u32[]{:S(2)}) collective-permute-start(bf16[2,64,3072]{2,1,0:T(8,128)(2,1)S(1)} %slice_bitcast_fusion.4), channel_id=1, source_target_pairs={{0,4},{1,5},{2,6},{3,7},{4,0},{5,1},{6,2},{7,3},{8,12},{9,13},{10,... | collective-permute-start | bytes 2359304 | tf_op jit(solution)/shard_map/ppermute | solution.py:488
  406.3 21.8 %collective-permute-start.13 = (bf16[64,2048]{1,0:T(8,128)(2,1)S(1)}, bf16[64,2048]{1,0:T(8,128)(2,1)S(1)}, u32[]{:S(2)}, u32[]{:S(2)}) collective-permute-start(bf16[64,2048]{1,0:T(8,128)(2,1)S(1)} %slice_bitcast_fusion.12), channel_id=1, source_target_pairs={{0,8},{1,9},{2,10},{3,11},{4,12},{5,13},{6,14},{7,15},{8,0},{9,1},... | collective-permute-start | bytes 786440 | tf_op jit(solution)/shard_map/ppermute | solution.py:488
  428.0 17.4 %collective-permute-start.9 = (bf16[64,3072]{1,0:T(8,128)(2,1)S(1)}, bf16[64,3072]{1,0:T(8,128)(2,1)S(1)}, u32[]{:S(2)}, u32[]{:S(2)}) collective-permute-start(bf16[64,3072]{1,0:T(8,128)(2,1)S(1)} %slice_bitcast_fusion.8), channel_id=1, source_target_pairs={{0,8},{1,9},{2,10},{3,11},{4,12},{5,13},{6,14},{7,15},{8,0},{9,1},... | collective-permute-start | bytes 1179656 | tf_op jit(solution)/shard_map/ppermute | solution.py:488
  459.6 19.3 %all-to-all-start.1 = ((bf16[16,64,256]{2,1,0:T(8,128)(2,1)}), bf16[16,64,256]{2,1,0:T(8,128)(2,1)S(1)}, u32[]{:S(2)}, u32[]{:S(2)}) async-start(bf16[16,64,256]{2,1,0:T(8,128)(2,1)} %bitcast.232), calls=%async_computation.1 | async-start | bytes 1048576 | tf_op jit(solution)/shard_map/all_to_all | solution.py:687
  (36 other events, 252.9 us)
Sparse Core Ops, SparseCore 0:
  11.3 154.1 all-gather.9
  167.7 41.1 all-gather.7
  245.9 74.2 all-gather.11

commit v3 on v2

--- a/solution.py
+++ b/solution.py
@@ -121,12 +121,13 @@
 
 
 def attend_back(grad_mixed, q_content, q_position, kv, rel, probs, grad_content, grad_position, grad_kv, grad_rel):
-    head_dim = q_content.shape[1] // HEADS
+    heads = probs.shape[1]
+    head_dim = q_content.shape[1] // heads
     root = 1.0 / math.sqrt(head_dim)
     width = q_content.shape[1]
     half = probs.shape[2]
     past = WIDE - ROWS
-    for head in range(HEADS):
+    for head in range(heads):
         cols = slice(head * head_dim, (head + 1) * head_dim)
         vcols = slice(width + head * head_dim, width + (head + 1) * head_dim)
         total = None
@@ -198,7 +199,7 @@
     return cot.astype(F32) + norm_back(hat, scale, total * vec[1:2]), total, hat
 
 
-def stage_one(weights, past, rev, entry, vec, hidden_bias, mask, kv, rel, output, w_in, w_out, w_rel, ff_in, ff_out,
+def stage_one(place, weights, past, rev, entry, vec, hidden_bias, mask, cot, kv, rel, output, early, w_in, w_out, w_rel, ff_in, ff_out,
               normed, q_content, q_position, mixed, sems):
     loads = Loads(sems)
     rows = w_in.shape[2]
@@ -244,12 +245,13 @@
     middle = wide_entry + dot(mixed[...], read_matrix(w_out))
     hat, _ = normalise(middle)
     normed_two = low(hat * vec[1:2] + vec[3:4])
+    early[...] = jnp.where(place[1] == 1, normed_two, cot[...])
     total = feed_forward(normed_two, hidden_bias, ff_in, ff_out, waits_in, waits_out, None)
     output[...] = low(middle + total + vec[4:5])
 
 
-def stage_two(weights, kv_past, rel_hbm, entry, vec, hidden_bias, mask, cot,
-              output, normed, q_content, q_position, kv_own, probs, mixed, middle_out, normed_two, pre, grad_low,
+def stage_two(place, weights, kv_past, rel_hbm, tokens, received, vec, hidden_bias, mask, cot,
+              entry, output, normed, q_content, q_position, kv_own, probs, mixed, middle_out, normed_two, pre, grad_low,
               w_in, w_out, ff_in, ff_out, kv, rel, grad_mixed, grad_content, grad_position, grad_kv, sems):
     loads = Loads(sems)
     rows = w_in.shape[2]
@@ -275,6 +277,7 @@
                 ff_out.at[quarter],
             )
         )
+    entry[...] = jnp.where(place[1] == 1, tokens[...], received[...])
     wide_entry = entry[...].astype(F32)
     wait_kv.wait()
     queries_and_keys(wide_entry, vec, w_in, waits, normed, q_content, q_position, kv)
@@ -303,36 +306,42 @@
     grad_low[...] = low(grad_middle + norm_back(hat_one, scale_one, grad_normed * vec[0:1]))
 
 
-def place_of(dest, me, bits):
+def place_of(dest, me, order):
     other = jnp.bitwise_xor(me, dest)
     place = 0
-    for bit in range(bits):
-        place = place + (((other >> bit) & 1) << (bits - 1 - bit))
+    for index, bit in enumerate(order):
+        place = place + ((other // bit) % 2) * (1 << (len(order) - 1 - index))
     return place
 
 
-def store_blocks(target, value, first_dest, me, bits, start):
-    rows = target.shape[1]
-    for index in range(value.shape[0] // rows):
-        place = place_of(first_dest + index, me, bits)
-        target[place, :, start : start + value.shape[1]] = low(value[index * rows : (index + 1) * rows])
-
-
-def stage_three(me_ref, weights, kv_past, kv_hbm, rel_hbm, probs_hbm, pre_hbm, rev_hbm, cot, vec, normed, q_content,
-                q_position, mixed, middle,
-                grad_kv, grad_query, grad_middle_out, sums, first_part,
-                w_out, ff_in, ff_out, kv, rel, probs, pre, rev, grad_mixed, grad_content, grad_position, grad_rel,
-                sems):
+def store_blocks(keep, send, value, first_dest, me, start, order):
+    rows = keep.shape[1]
+    wide = value.shape[1]
+    odd = (me & 1) == 1
+    for index in range(0, value.shape[0] // rows, 2):
+        even_rows = low(value[index * rows : (index + 1) * rows])
+        odd_rows = low(value[(index + 1) * rows : (index + 2) * rows])
+        place = place_of(first_dest + index, me, order[1:])
+        keep[place, :, start : start + wide] = jnp.where(odd, odd_rows, even_rows)
+        send[place, :, start : start + wide] = jnp.where(odd, even_rows, odd_rows)
+
+
+GROUP = 256
+
+
+def stage_three(orders, place, weights, kv_past, kv_hbm, rel_hbm, probs_hbm, pre_hbm, past_hbm, rev_hbm, returned,
+                cot_out, vec, normed, q_content, q_position, mixed, middle,
+                grad_kv_hbm, keep_one, send_one, keep_two, send_two, grad_query, grad_middle_out, sums,
+                w_out, ff_in, ff_out, pre, kv, rel, probs, rows_all, rev, grad_kv, grad_mixed, grad_content,
+                grad_position, grad_rel, blocks, sems):
     loads = Loads(sems)
     rows = w_out.shape[1]
-    size = w_out.shape[0]
-    bits = size.bit_length() - 1
-    width = cot.shape[1]
+    width = returned.shape[1]
     quarters = ff_in.shape[0]
+    share = ff_out.shape[1]
     half = ROWS // 2
     past_len = WIDE - ROWS
-    me = me_ref[0]
-    share = ff_out.shape[1]
+    me = place[0]
     waits_in, waits_out = [], []
     wait_pre = loads.start(pre_hbm, pre)
     for quarter in range(quarters):
@@ -347,77 +356,76 @@
     others = [
         loads.start(kv_past.at[:, pl.ds(0, past_len), :], kv.at[:, pl.ds(0, past_len), :]),
         loads.start(kv_hbm, kv.at[:, pl.ds(past_len, half), :]),
-        loads.start(
-            kv_past.at[:, pl.ds(past_len + half, half), :], kv.at[:, pl.ds(past_len + half, half), :]
-        ),
+        loads.start(kv_past.at[:, pl.ds(past_len + half, half), :], kv.at[:, pl.ds(past_len + half, half), :]),
         loads.start(rel_hbm, rel),
         loads.start(probs_hbm, probs),
+    ]
+    last = [
         loads.start(rev_hbm, rev),
+        loads.start(past_hbm, rows_all.at[:, pl.ds(0, past_len), :]),
     ]
+    cot = jnp.where(place[1] == 1, returned[...], cot_out[...])
     wait_pre.wait()
-    grad_middle, grad_two, hat = middle_back(
-        cot[...], middle[...], vec, ff_in, ff_out, waits_in, waits_out, pre
-    )
+    grad_middle, grad_two, hat = middle_back(cot, middle[...], vec, ff_in, ff_out, waits_in, waits_out, pre)
     grad_middle_out[...] = grad_middle
     sums[...] = jnp.zeros(sums.shape, F32)
     sums[1:2] = jnp.sum(grad_two * hat, 0, keepdims=True)
     sums[3:4] = jnp.sum(grad_two, 0, keepdims=True)
-    sums[4:5] = jnp.sum(cot[...].astype(F32), 0, keepdims=True)
+    sums[4:5] = jnp.sum(cot.astype(F32), 0, keepdims=True)
     grad_branch = low(grad_middle)
     wait_out.wait()
     grad_mixed[...] = low(dot_t(grad_branch, read_matrix(w_out)))
-    group = 256
-    for index in range(width // group):
-        store_blocks(
-            first_part,
-            t_dot(mixed[:, index * group : (index + 1) * group], grad_branch),
-            index * group // rows,
-            me,
-            bits,
-            0,
-        )
-    for other in others:
-        other.wait()
+
+    wide = blocks.shape[4]
+    outs = ((keep_one, send_one), (keep_two, send_two))
+    stores = []
+
+    def gradient(left_of, right, start):
+        end = start + right.shape[1]
+        for part in range(2):
+            begin, stop = max(start, part * wide), min(end, (part + 1) * wide)
+            if begin < stop:
+                for index in range(width // GROUP):
+                    value = t_dot(left_of(index), right[:, begin - start : stop - start])
+                    store_blocks(
+                        blocks.at[part, 0], blocks.at[part, 1], value, index * GROUP // rows, me, begin - part * wide,
+                        orders[part],
+                    )
+                cols = pl.ds(begin - part * wide, stop - begin)
+                for side in range(2):
+                    stores.append(
+                        loads.start(blocks.at[part, side, :, :, cols], outs[part][side].at[:, :, cols])
+                    )
+
+    def group(index):
+        return slice(index * GROUP, (index + 1) * GROUP)
+
+    gradient(lambda index: mixed[:, group(index)], grad_branch, 4 * width)
+    for copy in others:
+        copy.wait()
     attend_back(
         grad_mixed, q_content, q_position, kv, rel, probs, grad_content, grad_position, grad_kv, grad_rel
     )
+    stores.append(loads.start(grad_kv, grad_kv_hbm))
     sums[6:7] = jnp.sum(grad_content[...].astype(F32), 0, keepdims=True)
     sums[7:8] = jnp.sum(grad_position[...].astype(F32), 0, keepdims=True)
     query = low(grad_content[...].astype(F32) + grad_position[...].astype(F32))
     grad_query[...] = query
-    for index in range(width // group):
-        cols = slice(index * group, (index + 1) * group)
-        store_blocks(
-            first_part, t_dot(normed[:, cols], query), index * group // rows, me, bits, 2 * width
+    for seg in range(2):
+        rows_all[seg, past_len : past_len + half, :] = normed[seg * half : (seg + 1) * half]
+    rows_all[:, past_len + half :, :] = jnp.zeros((2, half, width), BF)
+    for copy in last:
+        copy.wait()
+    for side in range(2):
+        gradient(
+            lambda index: read_matrix(rows_all.at[:, :, group(index)]),
+            read_matrix(grad_kv.at[:, :, side * width : (side + 1) * width]),
+            (1 + side) * width,
         )
-        store_blocks(
-            first_part, t_dot(rev[:, cols], grad_rel[...]), index * group // rows, me, bits, width
-        )
-
-
-def stage_four(me_ref, past_hbm, normed_hbm, grad_kv_hbm, second_part, rows_all, grad_kv, sems):
-    loads = Loads(sems)
-    size, rows, wide = second_part.shape
-    bits = size.bit_length() - 1
-    width = wide // 2
-    half = ROWS // 2
-    past_len = WIDE - ROWS
-    me = me_ref[0]
-    copies = [
-        loads.start(past_hbm, rows_all.at[:, pl.ds(0, past_len), :]),
-        loads.start(normed_hbm, rows_all.at[:, pl.ds(past_len, half), :]),
-        loads.start(grad_kv_hbm, grad_kv),
-    ]
-    rows_all[:, past_len + half :, :] = jnp.zeros((2, half, width), BF)
-    for copy in copies:
+    gradient(lambda index: rev[:, group(index)], grad_rel[...], 3 * width)
+    gradient(lambda index: normed[:, group(index)], query, 0)
+    for copy in stores:
         copy.wait()
-    group = 256
-    tile = 512
-    for index in range(width // group):
-        left = read_matrix(rows_all.at[:, :, index * group : (index + 1) * group])
-        for start in range(0, wide, tile):
-            right = read_matrix(grad_kv.at[:, :, start : start + tile])
-            store_blocks(second_part, t_dot(left, right), index * group // rows, me, bits, start)
 
 
 def stage_five(weights, grad_kv_hbm, comp, mem, entry, grad_query, grad_middle, vec, grad_entry, sums,
@@ -460,48 +468,126 @@
     grad_entry[...] = grad_middle[...] + norm_back(hat_tok, scale_tok, grad_normed[...] * vec[0:1])
 
 
+def stage_six(place, early, late, w_in, w_out, bias, grad_in, grad_out, grad_bias, rows_one, rows_two, total_in, sems):
+    size = rows_one.shape[0]
+    loads = Loads(sems)
+    one = loads.start(early, rows_one)
+    two = loads.start(late.at[:, pl.ds(0, ROWS), :], rows_two)
+    one.wait()
+    two.wait()
+    step = min(size, 4)
+    is_first = place[1] == 1
+    bias_total = None
+    for start in range(0, size, step):
+        own = slice(start, start + step)
+        value_one = read_matrix(rows_one.at[own])
+        value_two = read_matrix(rows_two.at[own])
+        normed = jnp.where(is_first, value_one, value_two)
+        cot = jnp.where(is_first, value_two, value_one)
+        pre = dot(normed, read_matrix(w_in)) + bias[...]
+        grad_pre = low(dot_t(cot, w_out[...]) * gelu_slope(pre))
+        active = low(gelu(pre))
+        bias_term = jnp.sum(grad_pre.astype(F32), 0, keepdims=True)
+        out_term = t_dot(active, cot)
+        in_term = t_dot(grad_pre, normed)
+        if start == 0:
+            grad_out[...] = out_term
+            total_in[...] = in_term
+            bias_total = bias_term
+        else:
+            grad_out[...] += out_term
+            total_in[...] += in_term
+            bias_total = bias_total + bias_term
+    grad_bias[...] = bias_total
+    grad_in[...] = low(total_in[...].T)
+
+
 HBM = pl.BlockSpec(memory_space=pl.ANY)
 VMEM = pl.BlockSpec(memory_space=pltpu.VMEM)
 SMEM = pl.BlockSpec(memory_space=pltpu.SMEM)
 
 
-def call(body, name, in_specs, outs, scratch, copies, flops, args):
+def call(body, name, in_specs, outs, scratch, copies, flops, args, after=(), in_hbm=0):
+    def kernel(*refs):
+        body(*refs[: len(args)], *refs[len(args) + len(after) :])
+
     return pl.pallas_call(
-        body,
+        kernel,
         name=name,
-        in_specs=in_specs,
-        out_specs=[VMEM] * len(outs),
+        in_specs=in_specs + [HBM] * len(after),
+        out_specs=[HBM] * in_hbm + [VMEM] * (len(outs) - in_hbm),
         out_shape=[jax.ShapeDtypeStruct(shape, dtype) for shape, dtype in outs],
         scratch_shapes=[pltpu.VMEM(shape, dtype) for shape, dtype in scratch] + [pltpu.SemaphoreType.DMA((copies,))],
         compiler_params=pltpu.CompilerParams(vmem_limit_bytes=VMEM_BYTES),
-        cost_estimate=pl.CostEstimate(flops=flops, bytes_accessed=30_000_000, transcendentals=0),
-    )(*args)
+        cost_estimate=pl.CostEstimate(flops=flops // 1000, bytes_accessed=100_000, transcendentals=0),
+    )(*args, *after)
 
 
 def xor_pairs(count, bit):
     return [(i, i ^ bit) for i in range(count)]
 
 
-def scatter_sum(blocks, order):
-    size = lax.axis_size("stream")
-    for bit in order:
-        got = lax.ppermute(blocks[1], "stream", xor_pairs(size, bit))
-        blocks = (blocks[0].astype(F32) + got.astype(F32)).astype(blocks.dtype)
-    return blocks
-
-
-def relative_order(blocks, order):
-    size = lax.axis_size("stream")
-    me = lax.axis_index("stream")
-    index = []
-    for position in range(size):
-        value = 0
-        for place, bit in enumerate(order):
-            if (position >> (len(order) - 1 - place)) & 1:
-                value |= bit
-        index.append(value)
-    picked = blocks[jnp.array(index, jnp.int32) ^ me]
-    return picked.reshape((2,) * len(order) + blocks.shape[1:])
+def add_halves(pairs, after):
+    count, rows = pairs[0][0].shape[:2]
+    half = count // 2
+    widths = [keep.shape[2] for keep, _ in pairs]
+    inputs, specs = [], []
+    for (keep, got), wide in zip(pairs, widths):
+        for value in (keep, got):
+            for shift in (0, half):
+                inputs.append(value)
+                specs.append(pl.BlockSpec((1, rows, wide), functools.partial(lambda shift, i: (i + shift, 0, 0), shift)))
+
+    def kernel(*refs):
+        outs = refs[-2:]
+        start = 0
+        for index, wide in enumerate(widths):
+            for side in range(2):
+                keep, got = refs[4 * index + side], refs[4 * index + 2 + side]
+                outs[side][:, :, start : start + wide] = low(keep[...].astype(F32) + got[...].astype(F32))
+            start += wide
+
+    total = sum(widths)
+    return pl.pallas_call(
+        kernel,
+        name="add_halves",
+        grid=(half,),
+        in_specs=specs + [HBM] * len(after),
+        out_specs=[pl.BlockSpec((1, rows, total), lambda i: (i, 0, 0))] * 2,
+        out_shape=[jax.ShapeDtypeStruct((half, rows, total), BF)] * 2,
+        compiler_params=pltpu.CompilerParams(vmem_limit_bytes=24 * 1024 * 1024),
+        cost_estimate=pl.CostEstimate(flops=1000, bytes_accessed=100_000, transcendentals=0),
+    )(*inputs, *after)
+
+
+def gate(value, *after):
+    def kernel(*refs):
+        del refs
+
+    return pl.pallas_call(
+        kernel,
+        name="gate",
+        in_specs=[HBM] * (1 + len(after)),
+        out_specs=HBM,
+        out_shape=jax.ShapeDtypeStruct(value.shape, value.dtype),
+        input_output_aliases={0: 0},
+    )(value, *after)
+
+
+class Scatter:
+    def __init__(self, keep, send, order):
+        self.keep, self.send, self.order = keep, send, list(order)
+
+    def move(self):
+        bit = self.order.pop(0)
+        self.got = lax.ppermute(self.send, "stream", xor_pairs(lax.axis_size("stream"), bit))
+
+    def add(self, *after, others=()):
+        pairs = [(part.keep, part.got) for part in (self,) + tuple(others)]
+        self.keep, self.send = add_halves(pairs, after)
+
+    def last(self):
+        return self.keep[0].astype(F32) + self.got[0].astype(F32)
 
 
 def gather(shard):
@@ -548,6 +634,7 @@
     gain_one, gain_two = small[0], small[1]
     bias_one, bias_two, bias_out = small[2], small[3], small[4]
     pos_content, pos_position = small[6], small[7]
+    ff_bias_low = low(ff_bias[0]).astype(F32).reshape(1, my_hidden)
     hidden_bias = small[8:].reshape(quarters, size, rows).transpose(1, 0, 2).reshape(hidden_cols)
 
     low_in, low_ff_in, low_ff_out = low(attn_in[0]), low(ff_in[0]), low(ff_out[0])
@@ -568,9 +655,9 @@
     windows = lax.all_to_all(windows, "stream", 0, 0, tiled=True)
     partial = dot(windows.reshape(-1, comp_rows), low(compress[0]))
     partial = low(partial).reshape(size, micro * CNEW, width)
-    squeezed = scatter_sum(relative_order(partial, order), order)
-    side_all = gather(cot_comp.reshape(micro * CNEW, width)).reshape(-1, width)
-    grad_compress = t_dot(windows.reshape(-1, comp_rows), side_all)
+    side_rows = micro * CNEW
+    partial = jnp.pad(partial, ((0, 0), (0, -side_rows % 16), (0, 0))).reshape(-1, width)
+    windows = windows.reshape(-1, comp_rows)
 
     past = jnp.concatenate([compressed, memory], 1).astype(F32)
     past_normed = low(normalise(past)[0] * gain_one + bias_one)
@@ -598,59 +685,69 @@
     prob_all = ((micro, HEADS, seg_len, WIDE), BF)
     pre_all_shape = ((quarters, ROWS, width), F32)
 
-    kv_past, rel, output = call(
+    place = jnp.stack([me, first.astype(me.dtype)]).astype(jnp.int32)
+    flat_cot = cot_out.reshape(-1, width)
+    side = cot_comp.reshape(micro * CNEW, width)
+    side_pad = jnp.pad(side, ((0, -side_rows % 16), (0, 0)))
+    kv_past, rel, output, early = call(
         stage_one,
         "first_forward",
-        [HBM] + [VMEM] * 6,
-        [kv_all, rel_all, flat_low],
+        [SMEM, HBM] + [VMEM] * 7,
+        [kv_all, rel_all, flat_low, flat_low],
         [in_scratch, mat_scratch, mat_scratch, ff_in_scratch, ff_out_scratch] + [flat_low] * 4,
         5 + 2 * quarters,
         7_000_000_000,
-        (weights, past_normed, rev, flat_tokens, vec, bias_rows, mask),
-    )
+        (place, weights, past_normed, rev, flat_tokens, vec, bias_rows, mask, flat_cot),
+        (partial,),
+    )
+    early = gather(early)
     received = lax.ppermute(output, "section", [(0, 1)])
-    entry = jnp.where(first, flat_tokens, received)
-    (output, normed, q_content, q_position, kv_own, probs, mixed, middle, normed_two, pre, grad_low) = call(
+    (entry, output, normed, q_content, q_position, kv_own, probs, mixed, middle, normed_two, pre, grad_low) = call(
         stage_two,
         "second_forward_and_back",
-        [HBM] * 3 + [VMEM] * 5,
-        [flat_low, flat_low, flat_low, flat_low, kv_tok, prob_all, flat_low, flat_wide, flat_low, pre_all_shape,
-         flat_low],
+        [SMEM] + [HBM] * 3 + [VMEM] * 6,
+        [flat_low, flat_low, flat_low, flat_low, flat_low, kv_tok, prob_all, flat_low, flat_wide, flat_low,
+         pre_all_shape, flat_low],
         [in_scratch, mat_scratch, ff_in_scratch, ff_out_scratch, kv_all, rel_all, flat_low, flat_low, flat_low, kv_tok],
         6 + 2 * quarters,
         7_000_000_000,
-        (weights, kv_past, rel, entry, vec, bias_rows, mask, cot_out.reshape(-1, width)),
+        (place, weights, kv_past, rel, flat_tokens, received, vec, bias_rows, mask, flat_cot),
     )
     returned = lax.ppermute(grad_low, "section", [(1, 0)])
-    cot = jnp.where(first, returned, cot_out.reshape(-1, width))
-    both = gather(jnp.concatenate([normed_two, cot], 0))
-    normed_all = both[:, :ROWS].reshape(-1, width)
-    cot_all = both[:, ROWS:].reshape(-1, width)
-    me_ref = me.reshape(1).astype(jnp.int32)
-    grad_kv, grad_query, grad_middle, sums, first_part = call(
-        stage_three,
-        "first_gradients",
-        [SMEM] + [HBM] * 7 + [VMEM] * 7,
-        [kv_all, flat_low, flat_wide, ((8, width), F32), ((size, rows, 3 * width), BF)],
-        [mat_scratch, ff_in_scratch, ff_out_scratch, kv_all, rel_all, prob_all, pre_all_shape, rel_all,
-         flat_low, flat_low, flat_low, rel_all],
-        8 + 2 * quarters,
+    late = jnp.concatenate([jnp.where(first, returned, normed_two), side_pad], 0)
+    late = gather(gate(late, early))
+    squeezed = lax.psum_scatter(gate(partial, late), "stream", scatter_dimension=0, tiled=True)
+    half = size // 2
+    other_order = order[:1] + order[2:] + order[1:2]
+    wide = 5 * width // 2
+    part_shape = ((half, rows, wide), BF)
+    grad_kv, keep_one, send_one, keep_two, send_two, grad_query, grad_middle, sums = call(
+        functools.partial(stage_three, (order, other_order)),
+        "shared_gradients",
+        [SMEM] + [HBM] * 8 + [VMEM] * 8,
+        [kv_all] + [part_shape] * 4 + [flat_low, flat_wide, ((8, width), F32)],
+        [mat_scratch, ff_in_scratch, ff_out_scratch, pre_all_shape, kv_all, rel_all, prob_all,
+         ((micro, WIDE, width), BF), rel_all, kv_all, flat_low, flat_low, flat_low, rel_all,
+         ((2, 2, half, rows, wide), BF)],
+        24 + 2 * quarters,
         7_000_000_000,
-        (me_ref, weights, kv_past, kv_own, rel, probs, pre, rev, cot, vec, normed, q_content, q_position, mixed,
-         middle),
-    )
-    first_sum = scatter_sum(first_part.reshape((2,) * len(order) + first_part.shape[1:]), order)
-    (second_part,) = call(
-        stage_four,
-        "key_value_gradients",
-        [SMEM] + [HBM] * 3,
-        [((size, rows, 2 * width), BF)],
-        [((micro, WIDE, width), BF), kv_all],
-        3,
-        4_300_000_000,
-        (me_ref, past_normed, normed.reshape(micro, seg_len, width), grad_kv),
-    )
-    second_sum = scatter_sum(second_part.reshape((2,) * len(order) + second_part.shape[1:]), order)
+        (place, weights, kv_past, kv_own, rel, probs, pre, past_normed, rev, returned, flat_cot, vec, normed, q_content,
+         q_position, mixed, middle),
+        in_hbm=5,
+    )
+    one_sum, two_sum = Scatter(keep_one, send_one, order), Scatter(keep_two, send_two, other_order)
+
+    def move_both():
+        one_sum.move()
+        two_sum.move()
+
+    def add_both(*after):
+        one_sum.add(*after)
+        two_sum.add(*after)
+
+    move_both()
+    add_both()
+    move_both()
     grad_entry, more = call(
         stage_five,
         "entry_gradient",
@@ -660,36 +757,52 @@
         4,
         4_300_000_000,
         (weights, grad_kv, compressed, memory, entry, grad_query, grad_middle, vec),
-    )
-    grad_attn_out = first_sum[:, :width].astype(F32)
-    grad_rel = first_sum[:, width : 2 * width].astype(F32)
-    grad_attn_in = jnp.concatenate([first_sum[:, 2 * width :], second_sum], 1).astype(F32)
-
+        (one_sum.send, two_sum.send),
+    )
+
+    quarter_cols = width // my_hidden
+    mine_in = lax.dynamic_slice(
+        weights, (0, (5 + me // quarter_cols) * rows, (me % quarter_cols) * my_hidden), (size, rows, my_hidden)
+    )
+    grad_ff_in, grad_ff_out, grad_ff_bias = call(
+        stage_six,
+        "hidden_gradients",
+        [SMEM] + [HBM] * 2 + [VMEM] * 3,
+        [((width, my_hidden), BF), ((my_hidden, width), F32), ((1, my_hidden), F32)],
+        [((size, ROWS, width), BF), ((size, ROWS, width), BF), ((my_hidden, width), F32)],
+        2,
+        4_300_000_000,
+        (place, early, late, mine_in, low_ff_out, ff_bias_low),
+        (more,),
+    )
     vectors = jnp.stack(
         [more[0], sums[1], more[1], sums[3], sums[4], jnp.sum(cot_comp.astype(F32), (0, 1)), sums[6], sums[7]]
     )
-    vectors = vectors.reshape(8, size, rows).transpose(1, 0, 2)
-    vectors = scatter_sum(relative_order(vectors, order), order)
+    vectors = low(vectors.reshape(8, size, rows).transpose(1, 0, 2))
+    vectors = jnp.pad(vectors, ((0, 0), (0, 8), (0, my_hidden - rows)))
+    moved = jnp.concatenate([grad_ff_in.reshape(size, rows, my_hidden), vectors], 1)
+    moved = lax.all_to_all(moved, "stream", 0, 0, tiled=True)
+
+    add_both(grad_ff_bias)
+    move_both()
+    while one_sum.order:
+        add_both(squeezed)
+        move_both()
+    one, two = one_sum.last(), two_sum.last()
+    vectors = jnp.sum(moved[:, rows : rows + 8, :rows].astype(F32), 0)
+    grad_ff_in = moved[:, :rows].transpose(1, 0, 2).reshape(rows, hidden_cols).astype(F32)
+    side_all = late[:, ROWS : ROWS + side_rows].reshape(-1, width)
+    grad_compress = t_dot(windows, side_all)
+    both = jnp.concatenate([one, two], 1)
+    grad_attn_in = both[:, : 3 * width]
+    grad_rel = both[:, 3 * width : 4 * width]
+    grad_attn_out = both[:, 4 * width :]
     entry = entry.reshape(tokens.shape)
     grad_entry = grad_entry.reshape(tokens.shape)
-    w_ff_in = jnp.concatenate([part(5 + i) for i in range(quarters)], 1)
-
-    start = me * my_hidden
-    mine_in = lax.dynamic_slice(w_ff_in, (0, start), (width, my_hidden))
-    mine_bias = lax.dynamic_slice(hidden_bias, (start,), (my_hidden,))
-    pre_all = dot(normed_all, mine_in) + mine_bias
-    active_all = low(gelu(pre_all))
-    slope_all = gelu_slope(pre_all)
-    grad_pre_all = low(dot_t(cot_all, low_ff_out) * slope_all)
-    grad_ff_out = t_dot(active_all, cot_all)
-    grad_ff_in = t_dot(normed_all, grad_pre_all)
-    grad_ff_bias = jnp.sum(grad_pre_all.astype(F32), 0)
-    grad_ff_in = lax.all_to_all(low(grad_ff_in).reshape(size, rows, my_hidden), "stream", 0, 0, tiled=True)
-    grad_ff_in = grad_ff_in.transpose(1, 0, 2).reshape(rows, hidden_cols).astype(F32)
 
     activations = low(output).reshape(tokens.shape)
     new_memory = jnp.concatenate([memory[:, seg_len:], entry], 1)
-    squeezed = low(squeezed.astype(F32) + small[5]).reshape(micro, CNEW, width)
+    squeezed = low(squeezed[:side_rows].astype(F32) + small[5]).reshape(micro, CNEW, width)
     new_compressed = jnp.concatenate([compressed[:, CNEW:], squeezed], 1)
     return tuple(
         value[None]
@@ -707,7 +820,7 @@
             vectors[:2].T,
             vectors[2:6].T,
             vectors[6:].T,
-            grad_ff_bias,
+            grad_ff_bias[0],
         )
     )
 

time: 492 us -> 416 us (0.85)
  waiting for transfers between devices: 208 us -> 160 us
  local copies, waits for them, and re-layouts: 54.4 us -> 24.6 us
  Pallas kernels: 110 us -> 126 us
  matrix products: 15.7 us -> 4.46 us
  other arithmetic: 27.2 us -> 22.2 us
    ppermute x16 -> x8, waiting for transfers between devices: 94.9 us -> 34 us  [move(): lax.ppermute(self.send, 'stream', xor_pairs(lax.axis_size('stream'), bit))]
    slice x7 -> x2, local copies, waits for them, and re-layouts: 22.1 us -> 0.1 us  [the longest x1 0.07 us: per_device(): small[5]]
    pallas_call x5 -> x13, Pallas kernels: 110 us -> 126 us  [the longest x5 116 us: call(): pl.pallas_call(kernel, name=name, in_specs=in_specs + [HBM] * len(after),...]
    convert_element_type x12 -> x2, other arithmetic: 10.2 us -> 1.71 us  [the longest x1 1.15 us: per_device(): moved[:, :rows].transpose(1, 0, 2).reshape(rows, hidden_cols).astype(F32)]
    dot_general x3 -> x1, matrix products: 9.45 us -> 2.81 us  [t_dot(): lax.dot_general(first_op, second_op, (((0,), (0,)), ((), ())), preferred_...]
    reduce_scatter x0 -> x1, waiting for transfers between devices: none -> 6.42 us  [per_device(): lax.psum_scatter(gate(partial, late), 'stream', scatter_dimension=0, tile...]
    another operation x9, local copies, waits for them, and re-layouts: 6.95 us -> 0.6 us  [per_device(): jnp.stack([more[0], sums[1], more[1], sums[3], sums[4], jnp.sum(cot_comp....]
    all_gather x3, waiting for transfers between devices: 93.2 us -> 99.5 us  [gather(): return lax.all_gather(shard, 'stream', axis=0, tiled=False)]
  transfers between devices with their start and end apart: 23 -> 16, of which waited for: 10 -> 10; matrix products, arithmetic and copies ran while one was open for 16% -> 10% of each run, Pallas kernels for 23% -> 25%
where the time goes in v3:
time: 416 us; the launch traced here: 411 us
  waiting for transfers between devices  160 us (38%)
  Pallas kernels  126 us (30%)
  starting transfers between devices  29.9 us (7%)
  blocking collectives  29.1 us (7%)
  local copies, waits for them, and re-layouts  24.6 us (6%)
  other arithmetic  22.2 us (5%)
  between operations  14.8 us (4%)
  matrix products  4.46 us (1%)
    pallas_call x5, Pallas kernels, call(): pl.pallas_call(kernel, name=name, in_specs=in_specs + [HBM] * len(after),...  116 us
    all_gather x3, waiting for transfers between devices, gather(): return lax.all_gather(shard, 'stream', axis=0, tiled=False)  99.5 us
    ppermute x8, waiting for transfers between devices, move(): lax.ppermute(self.send, 'stream', xor_pairs(lax.axis_size('stream'), bit))  34 us
    all_gather x1, blocking collectives, gather(): return lax.all_gather(shard, 'stream', axis=0, tiled=False)  29.1 us
    ppermute x8, starting transfers between devices, move(): lax.ppermute(self.send, 'stream', xor_pairs(lax.axis_size('stream'), bit))  11.7 us
    pallas_call x6, Pallas kernels, add_halves(): pl.pallas_call(kernel, name='add_halves', grid=(half,), in_specs=specs +...  10.1 us
    ppermute x1, waiting for transfers between devices, per_device(): returned = lax.ppermute(grad_low, 'section', [(1, 0)])  8.44 us
  transfers between devices with their start and end apart: 16, of which 10 were waited for; matrix products, arithmetic and copies ran while one was open for 10% of the time, Pallas kernels for 25%

profile of v3, /device:TPU:0, one launch (start us, length us, event | category | flops | bytes accessed | tf_op | source)
XLA Modules:
  0.0 410.6 jit_solution(10015172341119653386)
XLA Ops:
  13.4 7.4 %all-to-all-start = ((bf16[16,42,192]{2,1,0:T(8,128)(2,1)}), bf16[16,42,192]{2,1,0:T(8,128)(2,1)S(1)}, u32[]{:S(2)}, u32[]{:S(2)}) async-start(bf16[16,42,192]{2,1,0:T(8,128)(2,1)} %bitcast.86), calls=%async_computation | async-start | bytes 786432 | tf_op jit(solution)/shard_map/all_to_all | solution.py:655
  21.1 29.1 %all-gather.4 = bf16[16,12,64]{2,1,0:T(8,128)(2,1)S(1)} all-gather(bf16[1,12,64]{2,1,0:T(8,128)(2,1)S(1)} %maximum_bitcast_fusion.2), channel_id=3, replica_groups=mesh['section'=2,'stream'=16] {'stream'}, dimensions={0}, use_global_device_ids=true | all-gather | bytes 26112 | tf_op jit(solution)/shard_map/all_gather | solution.py:594
  52.7 3.6 fusion.15
  65.3 94.7 %all-gather.9.cloned.1.call-done = bf16[13312,1024]{1,0:T(8,128)(2,1)} async-done(((bf16[832,1024]{1,0:T(8,128)(2,1)}), bf16[13312,1024]{1,0:T(8,128)(2,1)}) %all-gather.9.cloned.1.call-update) | async-done | bytes 27262992 | tf_op jit(solution)/shard_map/all_gather | solution.py:594
  160.0 21.9 %first_forward.1 = (bf16[2,512,2048]{2,1,0:T(8,128)(2,1)}, bf16[512,1024]{1,0:T(8,128)(2,1)}, bf16[128,1024]{1,0:T(8,128)(2,1)}, bf16[128,1024]{1,0:T(8,128)(2,1)}) custom-call(s32[2]{0:T(128)} %pad_add_fusion.refs_0_, bf16[16,832,1024]{2,1,0:T(8,128)(2,1)} %bitcast.87, bf16[2,384,1024]{2,1,0:T(8,128)(2,1)} %fusion.5.refs_2_.refs_7_, ...), custom_call_target="tpu_custom_call" | custom-call | flops 7000000 | bytes 100000 | tf_op jit(solution)/shard_map/first_forward/pallas_call | solution.py:514
  181.9 3.6 collective-permute-start
  185.6 6.0 %collective-permute-done.refs_5_ = bf16[128,1024]{1,0:T(8,128)(2,1)S(1)} collective-permute-done((bf16[128,1024]{1,0:T(8,128)(2,1)}, bf16[128,1024]{1,0:T(8,128)(2,1)S(1)}, u32[]{:S(2)}, u32[]{:S(2)}) %collective-permute-start) | collective-permute-done | bytes 262176 | tf_op jit(solution)/shard_map/ppermute | solution.py:704
  192.3 37.2 %second_forward_and_back.1 = (bf16[128,1024]{1,0:T(8,128)(2,1)}, bf16[128,1024]{1,0:T(8,128)(2,1)}, bf16[128,1024]{1,0:T(8,128)(2,1)}, bf16[128,1024]{1,0:T(8,12...) custom-call(s32[2]{0:T(128)} %pad_add_fusion.refs_0_, ...), custom_call_target="tpu_custom_call" | custom-call | flops 7000000 | bytes 100000 | tf_op jit(solution)/shard_map/second_forward_and_back/pallas_call | solution.py:514
  230.8 8.4 %collective-permute-done.1.refs_9_ = bf16[128,1024]{1,0:T(8,128)(2,1)S(1)} collective-permute-done((bf16[128,1024]{1,0:T(8,128)(2,1)}, bf16[128,1024]{1,0:T(8,128)(2,1)S(1)}, u32[]{:S(2)}, u32[]{:S(2)}) %collective-permute-start.1) | collective-permute-done | bytes 262176 | tf_op jit(solution)/shard_map/ppermute | solution.py:716
  240.3 32.5 %shared_gradients.1 = (bf16[2,512,2048]{2,1,0:T(8,128)(2,1)}, bf16[8,64,2560]{2,1,0:T(8,128)(2,1)}, bf16[8,64,2560]{2,1,0:T(8,128)(2,1)}, bf16[8,64,2560]{2,1,0:...) custom-call(s32[2]{0:T(128)} %pad_add_fusion.refs_0_, ...), custom_call_target="tpu_custom_call" | custom-call | flops 7000000 | bytes 100000 | tf_op jit(solution)/shard_map/shared_gradients/pallas_call | solution.py:514
  276.8 4.3 %collective-permute-done.2.refs_2_.refs_3_ = bf16[8,64,2560]{2,1,0:T(8,128)(2,1)} collective-permute-done((bf16[8,64,2560]{2,1,0:T(8,128)(2,1)}, bf16[8,64,2560]{2,1,0:T(8,128)(2,1)}, u32[]{:S(2)}, u32[]{:S(2)}) %collective-permute-start.2) | collective-permute-done | bytes 2621472 | tf_op jit(solution)/shard_map/ppermute | solution.py:583
  282.8 4.2 %add_halves.6 = (bf16[4,64,2560]{2,1,0:T(8,128)(2,1)S(1)}, bf16[4,64,2560]{2,1,0:T(8,128)(2,1)}) custom-call(bf16[8,64,2560]{2,1,0:T(8,128)(2,1)S(1)} %copy-done.1, bf16[8,64,2560]{2,1,0:T(8,128)(2,1)S(1)} %copy-done.1, bf16[8,64,2560]{2,1,0:T(8,128)(2,1)} %collective-permute-done.2.refs_2_.refs_3_, bf16[8,64,2560]{2,1,0:T(8,128)(2,1)} %collective-permute-done.2.refs_2_.refs_3_), custom_call_target="tpu_custom_call" | custom-call | flops 1000 | bytes 100000 | tf_op jit(solution)/shard_map/add_halves/pallas_call | solution.py:551
  291.2 3.9 collective-permute-start.7
  295.3 4.9 %all-gather.13.cloned.1.call-done = bf16[2816,1024]{1,0:T(8,128)(2,1)} async-done(((bf16[176,1024]{1,0:T(8,128)(2,1)}), bf16[2816,1024]{1,0:T(8,128)(2,1)}) %all-gather.13.cloned.1.call-update) | async-done | bytes 5767184 | tf_op jit(solution)/shard_map/all_gather | solution.py:594
  300.3 12.4 %entry_gradient.1 = (f32[128,1024]{1,0:T(8,128)}, f32[2,1024]{1,0:T(2,128)}) custom-call(bf16[16,832,1024]{2,1,0:T(8,128)(2,1)} %bitcast.91, bf16[2,512,2048]{2,1,0:T(8,128)(2,1)} %get-tuple-element.71.refs_1_, bf16[2,128,1024]{2,1,0:T(8,128)(2,1)} %bitcast.105, bf16[2,256,1024]{2,1,0:T(8,128)(2,1)} %bitcast.92, ...), custom_call_target="tpu_custom_call" | custom-call | flops 4300000 | bytes 100000 | tf_op jit(solution)/shard_map/entry_gradient/pallas_call | solution.py:514
  313.7 11.9 %hidden_gradients.1 = (bf16[1024,256]{1,0:T(8,128)(2,1)}, f32[256,1024]{1,0:T(8,128)}, f32[1,256]{1,0:T(1,128)}) custom-call(s32[2]{0:T(128)} %pad_add_fusion.refs_0_, bf16[16,128,1024]{2,1,0:T(8,128)(2,1)} %bitcast.104, bf16[16,176,1024]{2,1,0:T(8,128)(2,1)} %bitcast.101, bf16[16,64,256]{2,1,0:T(8,128)(2,1)} %constant_dynamic-slice_fusion.refs_3_, ...), custom_call_target="tpu_custom_call" | custom-call | flops 4300000 | bytes 100000 | tf_op jit(solution)/shard_map/hidden_gradients/pallas_call | solution.py:514
  327.6 5.6 %all-to-all-start.1 = ((bf16[16,80,256]{2,1,0:T(8,128)(2,1)}), bf16[16,80,256]{2,1,0:T(8,128)(2,1)}, u32[]{:S(2)}, u32[]{:S(2)}) async-start(bf16[16,80,256]{2,1,0:T(8,128)(2,1)} %fusion.19), calls=%async_computation.2 | async-start | bytes 1310720 | tf_op jit(solution)/shard_map/all_to_all | solution.py:784
  346.1 2.8 fusion.11
  348.9 5.2 %all-to-all-done.1 = bf16[16,80,256]{2,1,0:T(8,128)(2,1)} async-done(((bf16[16,80,256]{2,1,0:T(8,128)(2,1)}), bf16[16,80,256]{2,1,0:T(8,128)(2,1)}, u32[]{:S(2)}, u32[]{:S(2)}) %all-to-all-start.1) | async-done | bytes 655392 | tf_op jit(solution)/shard_map/all_to_all | solution.py:784
  356.9 2.4 reshape.176
  361.2 18.2 %collective-permute-done.5.refs_2_.refs_3_ = bf16[2,64,2560]{2,1,0:T(8,128)(2,1)S(1)} collective-permute-done((bf16[2,64,2560]{2,1,0:T(8,128)(2,1)}, bf16[2,64,2560]{2,1,0:T(8,128)(2,1)S(1)}, u32[]{:S(2)}, u32[]{:S(2)}) %collective-permute-start.5) | collective-permute-done | bytes 655392 | tf_op jit(solution)/shard_map/ppermute | solution.py:583
  379.5 6.4 %reduce-scatter.2.cloned.1.call-done.refs_4_ = bf16[48,1024]{1,0:T(8,128)(2,1)} async-done(((bf16[768,1024]{1,0:T(8,128)(2,1)}), bf16[48,1024]{1,0:T(8,128)(2,1)}) %reduce-scatter.2.cloned.1.call-update) | async-done | bytes 98320 | tf_op jit(solution)/shard_map/reduce_scatter | solution.py:719
  390.2 7.1 %collective-permute-done.9 = bf16[1,64,2560]{2,1,0:T(8,128)(2,1)S(1)} collective-permute-done((bf16[1,64,2560]{2,1,0:T(8,128)(2,1)S(1)}, bf16[1,64,2560]{2,1,0:T(8,128)(2,1)S(1)}, u32[]{:S(2)}, u32[]{:S(2)}) %collective-permute-start.9) | collective-permute-done | bytes 327712 | tf_op jit(solution)/shard_map/ppermute | solution.py:583
  398.2 4.4 %collective-permute-done.6 = bf16[1,64,2560]{2,1,0:T(8,128)(2,1)S(1)} collective-permute-done((bf16[1,64,2560]{2,1,0:T(8,128)(2,1)}, bf16[1,64,2560]{2,1,0:T(8,128)(2,1)S(1)}, u32[]{:S(2)}, u32[]{:S(2)}) %collective-permute-start.6) | collective-permute-done | bytes 327712 | tf_op jit(solution)/shard_map/ppermute | solution.py:583
  (171 shorter events, 57.8 us)
Async XLA Ops:
  7.2 152.8 %all-gather.9.cloned.1.call-start = ((), (), s32[]{:S(2)}) async-start(), calls=%async_computation.4 | async-start | bytes 28966912 | tf_op jit(solution)/shard_map/all_gather | solution.py:594
  12.1 8.8 %copy-start.27 = (f32[1,256]{1,0:T(1,128)S(1)}, f32[1,256]{1,0:T(1,128)}, u32[]{:S(2)}) copy-start(f32[1,256]{1,0:T(1,128)} %param.31) | copy-start | bytes 3076
  12.1 8.9 %copy-start.24 = (f32[1,64,4]{1,2,0:T(4,128)S(1)}, f32[1,64,4]{1,2,0:T(4,128)}, u32[]{:S(2)}) copy-start(f32[1,64,4]{1,2,0:T(4,128)} %param.29) | copy-start | bytes 3076
  12.1 8.9 %copy-start.25 = (f32[1,64,2]{1,2,0:T(2,128)S(1)}, f32[1,64,2]{1,2,0:T(2,128)}, u32[]{:S(2)}) copy-start(f32[1,64,2]{1,2,0:T(2,128)} %param.30) | copy-start | bytes 1540
  12.1 8.9 %copy-start.26 = (f32[1,64,2]{1,2,0:T(2,128)S(1)}, f32[1,64,2]{1,2,0:T(2,128)}, u32[]{:S(2)}) copy-start(f32[1,64,2]{1,2,0:T(2,128)} %param.28) | copy-start | bytes 1540
  12.1 39.6 %copy-start.23 = (s32[2,448]{1,0:T(2,128)S(1)}, s32[2,448]{1,0:T(2,128)}, u32[]{:S(2)}) copy-start(s32[2,448]{1,0:T(2,128)} %param.17) | copy-start | bytes 10756
  12.1 39.6 %copy-start.9 = (bf16[1,2,128,1024]{3,2,1,0:T(8,128)(2,1)S(1)}, bf16[1,2,128,1024]{3,2,1,0:T(8,128)(2,1)}, u32[]{:S(2)}) copy-start(bf16[1,2,128,1024]{3,2,1,0:T(8,128)(2,1)} %param.19) | copy-start | bytes 1572868
  13.4 47.2 %all-to-all-start = ((bf16[16,42,192]{2,1,0:T(8,128)(2,1)}), bf16[16,42,192]{2,1,0:T(8,128)(2,1)S(1)}, u32[]{:S(2)}, u32[]{:S(2)}) async-start(bf16[16,42,192]{2,1,0:T(8,128)(2,1)} %bitcast.86), calls=%async_computation | async-start | bytes 786432 | tf_op jit(solution)/shard_map/all_to_all | solution.py:655
  20.8 219.3 %all-gather.11.cloned.1.call-start = ((), (), s32[]{:S(2)}) async-start(), calls=%async_computation.5 | async-start | bytes 4456448 | tf_op jit(solution)/shard_map/all_gather | solution.py:594
  181.9 118.3 %all-gather.13.cloned.1.call-start = ((), (), s32[]{:S(2)}) async-start(), calls=%async_computation.6 | async-start | bytes 6127616 | tf_op jit(solution)/shard_map/all_gather | solution.py:594
  181.9 9.7 %collective-permute-start = (bf16[128,1024]{1,0:T(8,128)(2,1)}, bf16[128,1024]{1,0:T(8,128)(2,1)S(1)}, u32[]{:S(2)}, u32[]{:S(2)}) collective-permute-start(bf16[128,1024]{1,0:T(8,128)(2,1)} %get-tuple-element.57), channel_id=1, source_target_pairs={{0,16},{1,17},{2,18},{3,19},{4,20},{5,21},{6,22},{7,23},{8,24},{9,... | collective-permute-start | bytes 786440 | tf_op jit(solution)/shard_map/ppermute | solution.py:704
  192.3 38.5 %copy-start.19 = (bf16[1,2,21,1024]{3,1,2,0:T(2,128)(2,1)S(1)}, bf16[1,2,21,1024]{3,1,2,0:T(2,128)(2,1)}, u32[]{:S(2)}) copy-start(bf16[1,2,21,1024]{3,1,2,0:T(2,128)(2,1)} %param.21) | copy-start | bytes 258052
  229.4 9.8 %collective-permute-start.1 = (bf16[128,1024]{1,0:T(8,128)(2,1)}, bf16[128,1024]{1,0:T(8,128)(2,1)S(1)}, u32[]{:S(2)}, u32[]{:S(2)}) collective-permute-start(bf16[128,1024]{1,0:T(8,128)(2,1)} %get-tuple-element.60), channel_id=1, source_target_pairs={{16,0},{17,1},{18,2},{19,3},{20,4},{21,5},{22,6},{23,7},{24,8},{25... | collective-permute-start | bytes 786440 | tf_op jit(solution)/shard_map/ppermute | solution.py:716
  240.1 145.8 %reduce-scatter.2.cloned.1.call-start = ((), (), s32[]{:S(2)}) async-start(), calls=%async_computation.3 | async-start | bytes 1671168 | tf_op jit(solution)/shard_map/reduce_scatter | solution.py:719
  272.8 8.3 %collective-permute-start.2 = (bf16[8,64,2560]{2,1,0:T(8,128)(2,1)}, bf16[8,64,2560]{2,1,0:T(8,128)(2,1)}, u32[]{:S(2)}, u32[]{:S(2)}) collective-permute-start(bf16[8,64,2560]{2,1,0:T(8,128)(2,1)} %get-tuple-element.75), channel_id=1, source_target_pairs={{0,1},{1,0},{2,3},{3,2},{4,5},{5,4},{6,7},{7,6},{8,9},{9,8},{10,11... | collective-permute-start | bytes 7864328 | tf_op jit(solution)/shard_map/ppermute | solution.py:583
  272.9 15.4 %collective-permute-start.3 = (bf16[8,64,2560]{2,1,0:T(8,128)(2,1)}, bf16[8,64,2560]{2,1,0:T(8,128)(2,1)S(1)}, u32[]{:S(2)}, u32[]{:S(2)}) collective-permute-start(bf16[8,64,2560]{2,1,0:T(8,128)(2,1)} %get-tuple-element.78), channel_id=1, source_target_pairs={{0,1},{1,0},{2,3},{3,2},{4,5},{5,4},{6,7},{7,6},{8,9},{9,8},{10,11... | collective-permute-start | bytes 7864328 | tf_op jit(solution)/shard_map/ppermute | solution.py:583
  287.0 51.5 %collective-permute-start.4 = (bf16[4,64,2560]{2,1,0:T(8,128)(2,1)}, bf16[4,64,2560]{2,1,0:T(8,128)(2,1)}, u32[]{:S(2)}, u32[]{:S(2)}) collective-permute-start(bf16[4,64,2560]{2,1,0:T(8,128)(2,1)} %get-tuple-element.76.refs_8_), channel_id=1, source_target_pairs={{0,2},{1,3},{2,0},{3,1},{4,6},{5,7},{6,4},{7,5},{8,10},{9,11},{10,... | collective-permute-start | bytes 3932168 | tf_op jit(solution)/shard_map/ppermute | solution.py:583
  291.2 51.6 %collective-permute-start.7 = (bf16[4,64,2560]{2,1,0:T(8,128)(2,1)}, bf16[4,64,2560]{2,1,0:T(8,128)(2,1)S(1)}, u32[]{:S(2)}, u32[]{:S(2)}) collective-permute-start(bf16[4,64,2560]{2,1,0:T(8,128)(2,1)} %get-tuple-element.79.refs_9_), channel_id=1, source_target_pairs={{0,4},{1,5},{2,6},{3,7},{4,0},{5,1},{6,2},{7,3},{8,12},{9,13},{10,... | collective-permute-start | bytes 3932168 | tf_op jit(solution)/shard_map/ppermute | solution.py:583
  327.6 8.7 %copy-start.16 = (bf16[128,1024]{1,0:T(8,128)(2,1)S(1)}, bf16[128,1024]{1,0:T(8,128)(2,1)}, u32[]{:S(2)}) copy-start(bf16[128,1024]{1,0:T(8,128)(2,1)} %get-tuple-element.59.refs_4_) | copy-start | bytes 786436
  327.6 26.6 %all-to-all-start.1 = ((bf16[16,80,256]{2,1,0:T(8,128)(2,1)}), bf16[16,80,256]{2,1,0:T(8,128)(2,1)}, u32[]{:S(2)}, u32[]{:S(2)}) async-start(bf16[16,80,256]{2,1,0:T(8,128)(2,1)} %fusion.19), calls=%async_computation.2 | async-start | bytes 1310720 | tf_op jit(solution)/shard_map/all_to_all | solution.py:784
  340.7 38.7 %collective-permute-start.5 = (bf16[2,64,2560]{2,1,0:T(8,128)(2,1)}, bf16[2,64,2560]{2,1,0:T(8,128)(2,1)S(1)}, u32[]{:S(2)}, u32[]{:S(2)}) collective-permute-start(bf16[2,64,2560]{2,1,0:T(8,128)(2,1)} %get-tuple-element.85), channel_id=1, source_target_pairs={{0,4},{1,5},{2,6},{3,7},{4,0},{5,1},{6,2},{7,3},{8,12},{9,13},{10,... | collective-permute-start | bytes 1966088 | tf_op jit(solution)/shard_map/ppermute | solution.py:583
  343.8 43.8 %collective-permute-start.8 = (bf16[2,64,2560]{2,1,0:T(8,128)(2,1)}, bf16[2,64,2560]{2,1,0:T(8,128)(2,1)S(1)}, u32[]{:S(2)}, u32[]{:S(2)}) collective-permute-start(bf16[2,64,2560]{2,1,0:T(8,128)(2,1)} %get-tuple-element.90), channel_id=1, source_target_pairs={{0,8},{1,9},{2,10},{3,11},{4,12},{5,13},{6,14},{7,15},{8,0},{9,1},... | collective-permute-start | bytes 1966088 | tf_op jit(solution)/shard_map/ppermute | solution.py:583
  387.6 15.0 %collective-permute-start.6 = (bf16[1,64,2560]{2,1,0:T(8,128)(2,1)}, bf16[1,64,2560]{2,1,0:T(8,128)(2,1)S(1)}, u32[]{:S(2)}, u32[]{:S(2)}) collective-permute-start(bf16[1,64,2560]{2,1,0:T(8,128)(2,1)} %get-tuple-element.87), channel_id=1, source_target_pairs={{0,8},{1,9},{2,10},{3,11},{4,12},{5,13},{6,14},{7,15},{8,0},{9,1},... | collective-permute-start | bytes 983048 | tf_op jit(solution)/shard_map/ppermute | solution.py:583
  387.8 9.5 %collective-permute-start.9 = (bf16[1,64,2560]{2,1,0:T(8,128)(2,1)S(1)}, bf16[1,64,2560]{2,1,0:T(8,128)(2,1)S(1)}, u32[]{:S(2)}, u32[]{:S(2)}) collective-permute-start(bf16[1,64,2560]{2,1,0:T(8,128)(2,1)S(1)} %get-tuple-element.92), channel_id=1, source_target_pairs={{0,2},{1,3},{2,0},{3,1},{4,6},{5,7},{6,4},{7,5},{8,10},{9,11},{10,... | collective-permute-start | bytes 983048 | tf_op jit(solution)/shard_map/ppermute | solution.py:583
  (21 other events, 51.4 us)
Sparse Core Ops, SparseCore 0:
  12.2 147.7 all-gather.8
  182.0 51.9 all-gather.10
  240.2 59.8 all-gather.12
  303.7 82.1 reduce-scatter.1

commit v4 on v3

--- a/solution.py
+++ b/solution.py
@@ -67,6 +67,7 @@
 VMEM_BYTES = 60 * 1024 * 1024
 ROWS = 128
 WIDE = 512
+TOGETHER = 4
 
 
 def read_matrix(ref):
@@ -91,67 +92,88 @@
     root = 1.0 / math.sqrt(head_dim)
     width = q_content.shape[1]
     half = mask.shape[1]
-    for head in range(HEADS):
-        cols = slice(head * head_dim, (head + 1) * head_dim)
-        full = dot_t(q_position[:, cols], rel[:, cols])
-        for seg in range(2):
-            own = slice(seg * half, (seg + 1) * half)
-            content = dot_t(q_content[own, cols], kv[seg, :, cols])
-            position = pltpu.roll(full[own], WIDE - half + 1, 1, stride=1, stride_axis=0)
-            scores = (content + position) * root + mask[seg]
-            exponent = jnp.exp(scores - jnp.max(scores, 1, keepdims=True))
-            chosen = low(exponent / jnp.sum(exponent, 1, keepdims=True))
+    own = [slice(seg * half, (seg + 1) * half) for seg in range(2)]
+    for first_head in range(0, HEADS, TOGETHER):
+        heads = range(first_head, first_head + TOGETHER)
+        both = [(head, seg) for head in heads for seg in range(2)]
+        cols = {head: slice(head * head_dim, (head + 1) * head_dim) for head in heads}
+        vcols = {head: slice(width + head * head_dim, width + (head + 1) * head_dim) for head in heads}
+        full = {head: dot_t(q_position[:, cols[head]], rel[:, cols[head]]) for head in heads}
+        content = [dot_t(q_content[own[seg], cols[head]], kv[seg, :, cols[head]]) for head, seg in both]
+        position = [
+            pltpu.roll(full[head][own[seg]], WIDE - half + 1, 1, stride=1, stride_axis=0) for head, seg in both
+        ]
+        scores = [
+            (one + two) * root + mask[seg] for one, two, (_, seg) in zip(content, position, both)
+        ]
+        peaks = [jnp.max(score, 1, keepdims=True) for score in scores]
+        exponents = [jnp.exp(score - peak) for score, peak in zip(scores, peaks)]
+        totals = [jnp.sum(exponent, 1, keepdims=True) for exponent in exponents]
+        chosen = [low(exponent / total) for exponent, total in zip(exponents, totals)]
+        for value, (head, seg) in zip(chosen, both):
             if probs is not None:
-                probs[seg, head] = chosen
-            value = kv[seg, :, slice(width + head * head_dim, width + (head + 1) * head_dim)]
-            mixed[own, cols] = low(dot(chosen, value))
+                probs[seg, head] = value
+        outs = [dot(value, kv[seg, :, vcols[head]]) for value, (head, seg) in zip(chosen, both)]
+        for value, (head, seg) in zip(outs, both):
+            mixed[own[seg], cols[head]] = low(value)
+
+
+def mirror(values):
+    rows, wide = values[0].shape
+    lanes = 128
+    flip = lax.broadcasted_iota(jnp.int32, (lanes, lanes), 0) + lax.broadcasted_iota(jnp.int32, (lanes, lanes), 1)
+    flip = low(jnp.where(flip == lanes - 1, 1.0, 0.0))
+    starts = list(reversed(range(0, wide, lanes)))
+    turned = dot(jnp.concatenate([value[:, start : start + lanes] for value in values for start in starts], 0), flip)
+    count = len(starts)
+    return [
+        jnp.concatenate(
+            [turned[index * rows : (index + 1) * rows] for index in range(which * count, (which + 1) * count)], 1
+        )
+        for which in range(len(values))
+    ]
 
 
 def unskew(scores):
-    count = scores.shape[0]
-    moved = [
-        pltpu.roll(scores[start : start + 8], count - 8 - start, 1) if start < count - 8 else scores[start:]
-        for start in range(0, count, 8)
-    ]
-    scores = jnp.concatenate(moved, 0)
-    row = lax.broadcasted_iota(jnp.int32, scores.shape, 0)
-    for bit in range(3):
-        scores = jnp.where(((row >> bit) & 1) == 0, pltpu.roll(scores, 1 << bit, 1), scores)
-    return scores
+    half = scores[0].shape[0]
+    turned = [low(pltpu.roll(value, WIDE - half + 1, 1, stride=1, stride_axis=0)) for value in mirror(scores)]
+    return [low(value) for value in mirror(turned)]
 
 
 def attend_back(grad_mixed, q_content, q_position, kv, rel, probs, grad_content, grad_position, grad_kv, grad_rel):
-    heads = probs.shape[1]
-    head_dim = q_content.shape[1] // heads
+    head_dim = q_content.shape[1] // HEADS
     root = 1.0 / math.sqrt(head_dim)
     width = q_content.shape[1]
     half = probs.shape[2]
     past = WIDE - ROWS
-    for head in range(heads):
-        cols = slice(head * head_dim, (head + 1) * head_dim)
-        vcols = slice(width + head * head_dim, width + (head + 1) * head_dim)
-        total = None
-        for seg in range(2):
-            own = slice(seg * half, (seg + 1) * half)
-            grad_out = grad_mixed[own, cols]
+    own = [slice(seg * half, (seg + 1) * half) for seg in range(2)]
+    for first_head in range(0, HEADS, TOGETHER):
+        heads = range(first_head, first_head + TOGETHER)
+        both = [(head, seg) for head in heads for seg in range(2)]
+        cols = {head: slice(head * head_dim, (head + 1) * head_dim) for head in heads}
+        vcols = {head: slice(width + head * head_dim, width + (head + 1) * head_dim) for head in heads}
+        grad_outs = [grad_mixed[own[seg], cols[head]] for head, seg in both]
+        grad_probs = [dot_t(value, kv[seg, :, vcols[head]]) for value, (head, seg) in zip(grad_outs, both)]
+        wides = [probs[seg, head].astype(F32) for head, seg in both]
+        means = [jnp.sum(one * two, 1, keepdims=True) for one, two in zip(wides, grad_probs)]
+        scores = [low(one * (two - mean) * root) for one, two, mean in zip(wides, grad_probs, means)]
+        skewed = unskew(scores)
+        outs = [dot(score, kv[seg, :, cols[head]]) for score, (head, seg) in zip(scores, both)]
+        for value, (head, seg) in zip(outs, both):
+            grad_content[own[seg], cols[head]] = low(value)
+        for index, head in enumerate(heads):
+            pair = jnp.concatenate(skewed[2 * index : 2 * index + 2], 0)
+            grad_position[:, cols[head]] = low(dot(pair, rel[:, cols[head]]))
+            if grad_rel is not None:
+                grad_rel[:, cols[head]] = low(t_dot(pair, q_position[:, cols[head]]))
+        for score, value, (head, seg) in zip(scores, grad_outs, both):
             chosen = probs[seg, head]
-            wide = chosen.astype(F32)
-            grad_probs = low(dot_t(grad_out, kv[seg, :, vcols])).astype(F32)
-            scores = wide * (grad_probs - jnp.sum(wide * grad_probs, 1, keepdims=True)) * root
-            grad_scores = low(scores)
-            skewed = low(unskew(scores))
-            grad_content[own, cols] = low(dot(grad_scores, kv[seg, :, cols]))
-            grad_position[own, cols] = low(dot(skewed, rel[:, cols]))
             if grad_rel is None:
-                grad_kv[seg, :, cols] = low(t_dot(grad_scores[:, past:], q_content[own, cols]))[:half]
-                grad_kv[seg, :, vcols] = low(t_dot(chosen[:, past:], grad_out))[:half]
+                grad_kv[seg, :, cols[head]] = low(t_dot(score[:, past:], q_content[own[seg], cols[head]]))[:half]
+                grad_kv[seg, :, vcols[head]] = low(t_dot(chosen[:, past:], value))[:half]
             else:
-                grad_kv[seg, :, cols] = low(t_dot(grad_scores, q_content[own, cols]))
-                grad_kv[seg, :, vcols] = low(t_dot(chosen, grad_out))
-                term = t_dot(skewed, q_position[own, cols])
-                total = term if total is None else total + term
-        if grad_rel is not None:
-            grad_rel[:, cols] = low(total)
+                grad_kv[seg, :, cols[head]] = low(t_dot(score, q_content[own[seg], cols[head]]))
+                grad_kv[seg, :, vcols[head]] = low(t_dot(chosen, value))
 
 
 def queries_and_keys(entry, vec, w_in, waits, normed, q_content, q_position, kv):
@@ -199,8 +221,8 @@
     return cot.astype(F32) + norm_back(hat, scale, total * vec[1:2]), total, hat
 
 
-def stage_one(place, weights, past, rev, entry, vec, hidden_bias, mask, cot, kv, rel, output, early, w_in, w_out, w_rel, ff_in, ff_out,
-              normed, q_content, q_position, mixed, sems):
+def stage_one(place, weights, past, rev, entry, vec, hidden_bias, mask, cot, kv_hbm, rel_hbm, output, early, w_in, w_out, w_rel, ff_in, ff_out,
+              kv, rel, normed, q_content, q_position, mixed, sems):
     loads = Loads(sems)
     rows = w_in.shape[2]
     width = entry.shape[1]
@@ -231,8 +253,10 @@
             kv[seg, :past_len, side * width : (side + 1) * width] = low(
                 dot(past[seg], read_matrix(w_in.at[1 + side]))
             )
+    stores = [loads.start(kv.at[:, pl.ds(0, past_len), :], kv_hbm)]
     wait_rel.wait()
     rel[...] = low(dot(rev[...], read_matrix(w_rel)))
+    stores.append(loads.start(rel, rel_hbm))
 
     class Done:
         def wait(self):
@@ -248,11 +272,13 @@
     early[...] = jnp.where(place[1] == 1, normed_two, cot[...])
     total = feed_forward(normed_two, hidden_bias, ff_in, ff_out, waits_in, waits_out, None)
     output[...] = low(middle + total + vec[4:5])
+    for copy in stores:
+        copy.wait()
 
 
 def stage_two(place, weights, kv_past, rel_hbm, tokens, received, vec, hidden_bias, mask, cot,
-              entry, output, normed, q_content, q_position, kv_own, probs, mixed, middle_out, normed_two, pre, grad_low,
-              w_in, w_out, ff_in, ff_out, kv, rel, grad_mixed, grad_content, grad_position, grad_kv, sems):
+              probs_hbm, pre_hbm, entry, output, normed, q_content, q_position, kv_own, mixed, middle_out, normed_two, grad_low,
+              w_in, w_out, ff_in, ff_out, kv, rel, probs, pre, grad_mixed, grad_content, grad_position, grad_kv, sems):
     loads = Loads(sems)
     rows = w_in.shape[2]
     width = entry.shape[1]
@@ -264,7 +290,7 @@
         return loads.start(weights.at[:, pl.ds(index * rows, rows), :], target)
 
     waits = [part(index, w_in.at[index]) for index in range(3)]
-    wait_kv = loads.start(kv_past, kv)
+    wait_kv = loads.start(kv_past, kv.at[:, pl.ds(0, past_len), :])
     wait_rel = loads.start(rel_hbm, rel)
     wait_out = part(3, w_out)
     share = ff_out.shape[1]
@@ -278,12 +304,14 @@
             )
         )
     entry[...] = jnp.where(place[1] == 1, tokens[...], received[...])
+    kv[:, past_len + half :, :] = jnp.zeros((2, half, 2 * width), BF)
     wide_entry = entry[...].astype(F32)
     wait_kv.wait()
     queries_and_keys(wide_entry, vec, w_in, waits, normed, q_content, q_position, kv)
     kv_own[...] = kv[:, past_len : past_len + half, :]
     wait_rel.wait()
     attend(q_content, q_position, kv, rel, mask, probs, mixed)
+    stores = [loads.start(probs, probs_hbm)]
     wait_out.wait()
     middle = wide_entry + dot(mixed[...], read_matrix(w_out))
     middle_out[...] = middle
@@ -291,6 +319,7 @@
     flat = low(hat * vec[1:2] + vec[3:4])
     normed_two[...] = flat
     total = feed_forward(flat, hidden_bias, ff_in, ff_out, waits_in, waits_out, pre)
+    stores.append(loads.start(pre, pre_hbm))
     output[...] = low(middle_out[...] + total + vec[4:5])
 
     grad_middle, _, _ = middle_back(cot[...], middle_out[...], vec, ff_in, ff_out, None, None, pre)
@@ -304,6 +333,8 @@
     )
     hat_one, scale_one = normalise(entry[...].astype(F32))
     grad_low[...] = low(grad_middle + norm_back(hat_one, scale_one, grad_normed * vec[0:1]))
+    for copy in stores:
+        copy.wait()
 
 
 def place_of(dest, me, order):
@@ -354,9 +385,8 @@
         waits_in.append(loads.start(weights.at[:, pl.ds((5 + quarter) * rows, rows), :], ff_in.at[quarter]))
     wait_out = loads.start(weights.at[:, pl.ds(3 * rows, rows), :], w_out)
     others = [
-        loads.start(kv_past.at[:, pl.ds(0, past_len), :], kv.at[:, pl.ds(0, past_len), :]),
+        loads.start(kv_past, kv.at[:, pl.ds(0, past_len), :]),
         loads.start(kv_hbm, kv.at[:, pl.ds(past_len, half), :]),
-        loads.start(kv_past.at[:, pl.ds(past_len + half, half), :], kv.at[:, pl.ds(past_len + half, half), :]),
         loads.start(rel_hbm, rel),
         loads.start(probs_hbm, probs),
     ]
@@ -364,6 +394,7 @@
         loads.start(rev_hbm, rev),
         loads.start(past_hbm, rows_all.at[:, pl.ds(0, past_len), :]),
     ]
+    kv[:, past_len + half :, :] = jnp.zeros((2, half, 2 * width), BF)
     cot = jnp.where(place[1] == 1, returned[...], cot_out[...])
     wait_pre.wait()
     grad_middle, grad_two, hat = middle_back(cot, middle[...], vec, ff_in, ff_out, waits_in, waits_out, pre)
@@ -428,7 +459,7 @@
         copy.wait()
 
 
-def stage_five(weights, grad_kv_hbm, comp, mem, entry, grad_query, grad_middle, vec, grad_entry, sums,
+def stage_five(weights, grad_kv_hbm, comp, mem, entry, grad_query, grad_middle, vec, new_memory, grad_entry, sums,
                w_in, grad_kv, grad_normed, sems):
     loads = Loads(sems)
     rows = w_in.shape[2]
@@ -437,6 +468,10 @@
     past_len = WIDE - ROWS
     copies = [loads.start(grad_kv_hbm, grad_kv)] + [
         loads.start(weights.at[:, pl.ds(index * rows, rows), :], w_in.at[index]) for index in range(3)
+    ]
+    kept = mem.shape[1] - half
+    stores = [loads.start(mem.at[:, pl.ds(half, kept), :], new_memory.at[:, pl.ds(0, kept), :])] + [
+        loads.start(entry.at[pl.ds(seg * half, half), :], new_memory.at[seg, pl.ds(kept, half), :]) for seg in range(2)
     ]
     for copy in copies:
         copy.wait()
@@ -466,40 +501,69 @@
         )
         sums[1:2, cols] = jnp.sum(grad_past, 0, keepdims=True) + jnp.sum(grad_tok, 0, keepdims=True)
     grad_entry[...] = grad_middle[...] + norm_back(hat_tok, scale_tok, grad_normed[...] * vec[0:1])
-
-
-def stage_six(place, early, late, w_in, w_out, bias, grad_in, grad_out, grad_bias, rows_one, rows_two, total_in, sems):
+    for copy in stores:
+        copy.wait()
+
+
+def stage_six(place, weights, early, late, w_in, w_out, bias, hidden_bias, columns, keep, send, grad_out, grad_bias,
+              rows_one, rows_two, part_in, part_out, total_in, sems):
     size = rows_one.shape[0]
-    loads = Loads(sems)
-    one = loads.start(early, rows_one)
-    two = loads.start(late.at[:, pl.ds(0, ROWS), :], rows_two)
-    one.wait()
-    two.wait()
+    rows = part_in.shape[1]
+    quarters, width = hidden_bias.shape
+    share = size // quarters
     step = min(size, 4)
     is_first = place[1] == 1
-    bias_total = None
-    for start in range(0, size, step):
-        own = slice(start, start + step)
+    quarter = jnp.bitwise_and(place[0], quarters - 1)
+
+    def loads(index):
+        own = pl.ds(index * step, step)
+        return (
+            pltpu.make_async_copy(early.at[own], rows_one.at[own], sems.at[2 * index]),
+            pltpu.make_async_copy(late.at[own, pl.ds(0, ROWS), :], rows_two.at[own], sems.at[2 * index + 1]),
+        )
+
+    count = size // step
+    copies = (
+        pltpu.make_async_copy(
+            weights.at[:, pl.ds((5 + quarter) * rows, rows), :], part_in, sems.at[2 * count]
+        ),
+        pltpu.make_async_copy(
+            weights.at[pl.ds(quarter * share, share), pl.ds((5 + quarters) * rows, quarters * rows), :],
+            part_out,
+            sems.at[2 * count + 1],
+        ),
+    )
+    for copy in copies:
+        copy.start()
+    for index in range(count):
+        for copy in loads(index):
+            copy.start()
+    for copy in copies:
+        copy.wait()
+    total_in[...] = jnp.zeros(total_in.shape, F32)
+    grad_out[...] = jnp.zeros(grad_out.shape, F32)
+    grad_bias[...] = jnp.zeros(grad_bias.shape, F32)
+    part_bias = hidden_bias[pl.ds(quarter, 1), :]
+
+    def body(index, carry):
+        for copy in loads(index):
+            copy.wait()
+        own = pl.ds(index * step, step)
         value_one = read_matrix(rows_one.at[own])
         value_two = read_matrix(rows_two.at[own])
         normed = jnp.where(is_first, value_one, value_two)
         cot = jnp.where(is_first, value_two, value_one)
         pre = dot(normed, read_matrix(w_in)) + bias[...]
         grad_pre = low(dot_t(cot, w_out[...]) * gelu_slope(pre))
-        active = low(gelu(pre))
-        bias_term = jnp.sum(grad_pre.astype(F32), 0, keepdims=True)
-        out_term = t_dot(active, cot)
-        in_term = t_dot(grad_pre, normed)
-        if start == 0:
-            grad_out[...] = out_term
-            total_in[...] = in_term
-            bias_total = bias_term
-        else:
-            grad_out[...] += out_term
-            total_in[...] += in_term
-            bias_total = bias_total + bias_term
-    grad_bias[...] = bias_total
-    grad_in[...] = low(total_in[...].T)
+        grad_bias[...] += jnp.sum(grad_pre.astype(F32), 0, keepdims=True)
+        grad_out[...] += t_dot(low(gelu(pre)), cot)
+        pre = dot(normed, read_matrix(part_in)) + part_bias
+        grad_pre = low(dot_t(cot, read_matrix(part_out)) * gelu_slope(pre))
+        total_in[...] += t_dot(columns[pl.ds(index * step * ROWS, step * ROWS), :], grad_pre)
+        return carry
+
+    lax.fori_loop(0, count, body, 0)
+    store_blocks(keep, send, total_in[...], 0, place[0], 0, (1, 2))
 
 
 HBM = pl.BlockSpec(memory_space=pl.ANY)
@@ -588,6 +652,19 @@
 
     def last(self):
         return self.keep[0].astype(F32) + self.got[0].astype(F32)
+
+
+def relative_order(blocks, order):
+    size = lax.axis_size("stream")
+    me = lax.axis_index("stream")
+    index = []
+    for position in range(size):
+        value = 0
+        for place, bit in enumerate(order):
+            if (position >> (len(order) - 1 - place)) & 1:
+                value |= bit
+        index.append(value)
+    return blocks[jnp.array(index, jnp.int32) ^ me]
 
 
 def gather(shard):
@@ -656,7 +733,14 @@
     partial = dot(windows.reshape(-1, comp_rows), low(compress[0]))
     partial = low(partial).reshape(size, micro * CNEW, width)
     side_rows = micro * CNEW
-    partial = jnp.pad(partial, ((0, 0), (0, -side_rows % 16), (0, 0))).reshape(-1, width)
+    partial = jnp.pad(partial, ((0, 0), (0, -side_rows % 16), (0, 0)))
+    partial = relative_order(partial, order)
+    side_sum = Scatter(partial[: size // 2], partial[size // 2 :], order)
+    side_sum.move()
+    while side_sum.order:
+        side_sum.add()
+        side_sum.move()
+    squeezed = low(side_sum.last()[:side_rows] + small[5])
     windows = windows.reshape(-1, comp_rows)
 
     past = jnp.concatenate([compressed, memory], 1).astype(F32)
@@ -680,6 +764,7 @@
     flat_low = ((ROWS, width), BF)
     flat_wide = ((ROWS, width), F32)
     kv_all = ((micro, WIDE, 2 * width), BF)
+    kv_old = ((micro, past_len, 2 * width), BF)
     kv_tok = ((micro, seg_len, 2 * width), BF)
     rel_all = ((WIDE, width), BF)
     prob_all = ((micro, HEADS, seg_len, WIDE), BF)
@@ -693,30 +778,37 @@
         stage_one,
         "first_forward",
         [SMEM, HBM] + [VMEM] * 7,
-        [kv_all, rel_all, flat_low, flat_low],
-        [in_scratch, mat_scratch, mat_scratch, ff_in_scratch, ff_out_scratch] + [flat_low] * 4,
-        5 + 2 * quarters,
+        [kv_old, rel_all, flat_low, flat_low],
+        [in_scratch, mat_scratch, mat_scratch, ff_in_scratch, ff_out_scratch, kv_all, rel_all] + [flat_low] * 4,
+        7 + 2 * quarters,
         7_000_000_000,
         (place, weights, past_normed, rev, flat_tokens, vec, bias_rows, mask, flat_cot),
-        (partial,),
+        (squeezed,),
+        in_hbm=2,
     )
     early = gather(early)
     received = lax.ppermute(output, "section", [(0, 1)])
-    (entry, output, normed, q_content, q_position, kv_own, probs, mixed, middle, normed_two, pre, grad_low) = call(
+    quarter_cols = width // my_hidden
+    mine_in = lax.dynamic_slice(
+        weights, (0, (5 + me // quarter_cols) * rows, (me % quarter_cols) * my_hidden), (size, rows, my_hidden)
+    )
+    (probs, pre, entry, output, normed, q_content, q_position, kv_own, mixed, middle, normed_two, grad_low) = call(
         stage_two,
         "second_forward_and_back",
         [SMEM] + [HBM] * 3 + [VMEM] * 6,
-        [flat_low, flat_low, flat_low, flat_low, flat_low, kv_tok, prob_all, flat_low, flat_wide, flat_low,
-         pre_all_shape, flat_low],
-        [in_scratch, mat_scratch, ff_in_scratch, ff_out_scratch, kv_all, rel_all, flat_low, flat_low, flat_low, kv_tok],
-        6 + 2 * quarters,
+        [prob_all, pre_all_shape, flat_low, flat_low, flat_low, flat_low, flat_low, kv_tok, flat_low, flat_wide,
+         flat_low, flat_low],
+        [in_scratch, mat_scratch, ff_in_scratch, ff_out_scratch, kv_all, rel_all, prob_all, pre_all_shape, flat_low,
+         flat_low, flat_low, kv_tok],
+        8 + 2 * quarters,
         7_000_000_000,
         (place, weights, kv_past, rel, flat_tokens, received, vec, bias_rows, mask, flat_cot),
+        (mine_in,),
+        in_hbm=2,
     )
     returned = lax.ppermute(grad_low, "section", [(1, 0)])
     late = jnp.concatenate([jnp.where(first, returned, normed_two), side_pad], 0)
     late = gather(gate(late, early))
-    squeezed = lax.psum_scatter(gate(partial, late), "stream", scatter_dimension=0, tiled=True)
     half = size // 2
     other_order = order[:1] + order[2:] + order[1:2]
     wide = 5 * width // 2
@@ -748,61 +840,65 @@
     move_both()
     add_both()
     move_both()
-    grad_entry, more = call(
+    new_memory, grad_entry, more = call(
         stage_five,
         "entry_gradient",
         [HBM] * 2 + [VMEM] * 6,
-        [flat_wide, ((2, width), F32)],
+        [(memory.shape, BF), flat_wide, ((2, width), F32)],
         [in_scratch, kv_all, flat_wide],
-        4,
+        7,
         4_300_000_000,
         (weights, grad_kv, compressed, memory, entry, grad_query, grad_middle, vec),
         (one_sum.send, two_sum.send),
-    )
-
-    quarter_cols = width // my_hidden
-    mine_in = lax.dynamic_slice(
-        weights, (0, (5 + me // quarter_cols) * rows, (me % quarter_cols) * my_hidden), (size, rows, my_hidden)
-    )
-    grad_ff_in, grad_ff_out, grad_ff_bias = call(
+        in_hbm=1,
+    )
+
+    add_both(more)
+    move_both()
+
+    shared = quarters * rows
+    columns = [
+        lax.dynamic_slice(value, (0, 0, (me // quarters) * shared), (size, ROWS, shared)).reshape(-1, shared)
+        for value in (early, late)
+    ]
+    columns = jnp.where(first, columns[0], columns[1])
+    keep, send, grad_ff_out, grad_ff_bias = call(
         stage_six,
         "hidden_gradients",
-        [SMEM] + [HBM] * 2 + [VMEM] * 3,
-        [((width, my_hidden), BF), ((my_hidden, width), F32), ((1, my_hidden), F32)],
-        [((size, ROWS, width), BF), ((size, ROWS, width), BF), ((my_hidden, width), F32)],
-        2,
+        [SMEM] + [HBM] * 3 + [VMEM] * 5,
+        [((2, rows, width), BF)] * 2 + [((my_hidden, width), F32), ((1, my_hidden), F32)],
+        [((size, ROWS, width), BF), ((size, ROWS, width), BF), mat_scratch,
+         ((size // quarters, quarters * rows, width), BF), ((shared, width), F32)],
+        2 + 2 * (size // min(size, 4)),
         4_300_000_000,
-        (place, early, late, mine_in, low_ff_out, ff_bias_low),
-        (more,),
-    )
+        (place, weights, early, late, mine_in, low_ff_out, ff_bias_low, bias_rows, columns),
+        (one_sum.send, two_sum.send),
+    )
+    got = lax.ppermute(send, "stream", xor_pairs(size, 1))
+    far = lax.ppermute(jnp.concatenate([keep[1:], got[1:]], 0), "stream", xor_pairs(size, 2))
+    grad_ff_in = jnp.concatenate([keep[:1], got[:1], far], 0)
+    grad_ff_in = grad_ff_in[jnp.arange(quarters, dtype=me.dtype) ^ (me % quarters)]
+    grad_ff_in = grad_ff_in.transpose(1, 0, 2).reshape(rows, hidden_cols).astype(F32)
     vectors = jnp.stack(
         [more[0], sums[1], more[1], sums[3], sums[4], jnp.sum(cot_comp.astype(F32), (0, 1)), sums[6], sums[7]]
     )
-    vectors = low(vectors.reshape(8, size, rows).transpose(1, 0, 2))
-    vectors = jnp.pad(vectors, ((0, 0), (0, 8), (0, my_hidden - rows)))
-    moved = jnp.concatenate([grad_ff_in.reshape(size, rows, my_hidden), vectors], 1)
-    moved = lax.all_to_all(moved, "stream", 0, 0, tiled=True)
-
-    add_both(grad_ff_bias)
-    move_both()
+    vectors = vectors.reshape(8, size, rows).transpose(1, 0, 2)
+    vectors = jnp.sum(lax.all_to_all(vectors, "stream", 0, 0, tiled=True), 0)
     while one_sum.order:
-        add_both(squeezed)
+        one_sum.add(grad_ff_bias)
+        two_sum.add(one_sum.send)
         move_both()
     one, two = one_sum.last(), two_sum.last()
-    vectors = jnp.sum(moved[:, rows : rows + 8, :rows].astype(F32), 0)
-    grad_ff_in = moved[:, :rows].transpose(1, 0, 2).reshape(rows, hidden_cols).astype(F32)
     side_all = late[:, ROWS : ROWS + side_rows].reshape(-1, width)
     grad_compress = t_dot(windows, side_all)
     both = jnp.concatenate([one, two], 1)
     grad_attn_in = both[:, : 3 * width]
     grad_rel = both[:, 3 * width : 4 * width]
     grad_attn_out = both[:, 4 * width :]
-    entry = entry.reshape(tokens.shape)
     grad_entry = grad_entry.reshape(tokens.shape)
 
     activations = low(output).reshape(tokens.shape)
-    new_memory = jnp.concatenate([memory[:, seg_len:], entry], 1)
-    squeezed = low(squeezed[:side_rows].astype(F32) + small[5]).reshape(micro, CNEW, width)
+    squeezed = squeezed.reshape(micro, CNEW, width)
     new_compressed = jnp.concatenate([compressed[:, CNEW:], squeezed], 1)
     return tuple(
         value[None]

time: 416 us -> 386 us (0.928)
  Pallas kernels: 126 us -> 113 us
  waiting for transfers between devices: 160 us -> 148 us
    ppermute x8 -> x12, waiting for transfers between devices: 34 us -> 72 us  [move(): lax.ppermute(self.send, 'stream', xor_pairs(lax.axis_size('stream'), bit))]
    all_gather x3, waiting for transfers between devices: 99.5 us -> 63.2 us  [gather(): return lax.all_gather(shard, 'stream', axis=0, tiled=False)]
    pallas_call x5, Pallas kernels: 116 us -> 104 us  [call(): pl.pallas_call(kernel, name=name, in_specs=in_specs + [HBM] * len(after),...]
    reduce_scatter x1 -> x0, waiting for transfers between devices: 6.42 us -> none  [per_device(): lax.psum_scatter(gate(partial, late), 'stream', scatter_dimension=0, tile...]
    all_to_all x1, waiting for transfers between devices: 5.22 us -> 0.01 us  [per_device(): vectors = jnp.sum(lax.all_to_all(vectors, 'stream', 0, 0, tiled=True), 0)]
    pallas_call x6 -> x9, Pallas kernels: 10.1 us -> 8.72 us  [add_halves(): pl.pallas_call(kernel, name='add_halves', grid=(half,), in_specs=specs +...]
    ppermute x8 -> x12, starting transfers between devices: 11.7 us -> 11.1 us  [move(): lax.ppermute(self.send, 'stream', xor_pairs(lax.axis_size('stream'), bit))]
  transfers between devices with their start and end apart: 16 -> 21, of which waited for: 10 -> 13; matrix products, arithmetic and copies ran while one was open for 10% -> 9% of each run, Pallas kernels for 25% -> 25%
where the time goes in v4:
time: 386 us; the launch traced here: 381 us
  waiting for transfers between devices  148 us (38%)
  Pallas kernels  113 us (29%)
  blocking collectives  29.1 us (8%)
  starting transfers between devices  28.4 us (7%)
  local copies, waits for them, and re-layouts  24.5 us (6%)
  other arithmetic  19.2 us (5%)
  between operations  14.9 us (4%)
  matrix products  4.47 us (1%)
    pallas_call x5, Pallas kernels, call(): pl.pallas_call(kernel, name=name, in_specs=in_specs + [HBM] * len(after),...  104 us
    ppermute x12, waiting for transfers between devices, move(): lax.ppermute(self.send, 'stream', xor_pairs(lax.axis_size('stream'), bit))  72 us
    all_gather x3, waiting for transfers between devices, gather(): return lax.all_gather(shard, 'stream', axis=0, tiled=False)  63.2 us
    all_gather x1, blocking collectives, gather(): return lax.all_gather(shard, 'stream', axis=0, tiled=False)  29.1 us
    ppermute x12, starting transfers between devices, move(): lax.ppermute(self.send, 'stream', xor_pairs(lax.axis_size('stream'), bit))  11.1 us
    pallas_call x9, Pallas kernels, add_halves(): pl.pallas_call(kernel, name='add_halves', grid=(half,), in_specs=specs +...  8.72 us
    ppermute x1, waiting for transfers between devices, per_device(): returned = lax.ppermute(grad_low, 'section', [(1, 0)])  8.42 us
    unnamed x62, local copies, waits for them, and re-layouts  7.86 us
  transfers between devices with their start and end apart: 21, of which 13 were waited for; matrix products, arithmetic and copies ran while one was open for 9% of the time, Pallas kernels for 25%

profile of v4, /device:TPU:0, one launch (start us, length us, event | category | flops | bytes accessed | tf_op | source)
XLA Modules:
  0.0 380.7 jit_solution(16774139414058518194)
XLA Ops:
  13.5 7.5 %all-to-all-start = ((bf16[16,42,192]{2,1,0:T(8,128)(2,1)}), bf16[16,42,192]{2,1,0:T(8,128)(2,1)S(1)}, u32[]{:S(2)}, u32[]{:S(2)}) async-start(bf16[16,42,192]{2,1,0:T(8,128)(2,1)} %bitcast.92), calls=%async_computation | async-start | bytes 786432 | tf_op jit(solution)/shard_map/all_to_all | solution.py:732
  21.2 29.1 %all-gather.4 = bf16[16,12,64]{2,1,0:T(8,128)(2,1)S(1)} all-gather(bf16[1,12,64]{2,1,0:T(8,128)(2,1)S(1)} %maximum_bitcast_fusion.1), channel_id=3, replica_groups=mesh['section'=2,'stream'=16] {'stream'}, dimensions={0}, use_global_device_ids=true | all-gather | bytes 26112 | tf_op jit(solution)/shard_map/all_gather | solution.py:671
  59.8 3.6 fusion.14
  68.6 15.3 %collective-permute-done.1.refs_2_.refs_3_ = bf16[4,48,1024]{2,1,0:T(8,128)(2,1)S(1)} collective-permute-done((bf16[4,48,1024]{2,1,0:T(8,128)(2,1)S(1)}, bf16[4,48,1024]{2,1,0:T(8,128)(2,1)S(1)}, u32[]{:S(2)}, u32[]{:S(2)}) %collective-permute-start.1) | collective-permute-done | bytes 393248 | tf_op jit(solution)/shard_map/ppermute | solution.py:647
  85.2 10.6 %collective-permute-done.2.refs_2_.refs_3_ = bf16[2,48,1024]{2,1,0:T(8,128)(2,1)S(1)} collective-permute-done((bf16[2,48,1024]{2,1,0:T(8,128)(2,1)S(1)}, bf16[2,48,1024]{2,1,0:T(8,128)(2,1)S(1)}, u32[]{:S(2)}, u32[]{:S(2)}) %collective-permute-start.2) | collective-permute-done | bytes 196640 | tf_op jit(solution)/shard_map/ppermute | solution.py:647
  96.5 8.8 %collective-permute-done.3 = bf16[1,48,1024]{2,1,0:T(8,128)(2,1)S(1)} collective-permute-done((bf16[1,48,1024]{2,1,0:T(8,128)(2,1)S(1)}, bf16[1,48,1024]{2,1,0:T(8,128)(2,1)S(1)}, u32[]{:S(2)}, u32[]{:S(2)}) %collective-permute-start.3) | collective-permute-done | bytes 98336 | tf_op jit(solution)/shard_map/ppermute | solution.py:647
  106.0 60.4 %all-gather.9.cloned.1.call-done = bf16[13312,1024]{1,0:T(8,128)(2,1)} async-done(((bf16[832,1024]{1,0:T(8,128)(2,1)}), bf16[13312,1024]{1,0:T(8,128)(2,1)}) %all-gather.9.cloned.1.call-update) | async-done | bytes 27262992 | tf_op jit(solution)/shard_map/all_gather | solution.py:671
  166.3 16.9 %first_forward.1 = (bf16[2,384,2048]{2,1,0:T(8,128)(2,1)}, bf16[512,1024]{1,0:T(8,128)(2,1)}, bf16[128,1024]{1,0:T(8,128)(2,1)}, bf16[128,1024]{1,0:T(8,128)(2,1)}) custom-call(s32[2]{0:T(128)} %pad_add_fusion.refs_0_, bf16[16,832,1024]{2,1,0:T(8,128)(2,1)} %bitcast.93, bf16[2,384,1024]{2,1,0:T(8,128)(2,1)} %fusion.5.refs_2_.refs_7_, ...), custom_call_target="tpu_custom_call" | custom-call | flops 7000000 | bytes 100000 | tf_op jit(solution)/shard_map/first_forward/pallas_call | solution.py:578
  183.3 3.9 %collective-permute-start.4 = (bf16[128,1024]{1,0:T(8,128)(2,1)}, bf16[128,1024]{1,0:T(8,128)(2,1)S(1)}, u32[]{:S(2)}, u32[]{:S(2)}) collective-permute-start(bf16[128,1024]{1,0:T(8,128)(2,1)} %get-tuple-element.71), channel_id=1, source_target_pairs={{0,16},{1,17},{2,18},{3,19},{4,20},{5,21},{6,22},{7,23},{8,24},{9,... | collective-permute-start | bytes 786440 | tf_op jit(solution)/shard_map/ppermute | solution.py:790
  189.2 3.8 %collective-permute-done.4.refs_5_ = bf16[128,1024]{1,0:T(8,128)(2,1)S(1)} collective-permute-done((bf16[128,1024]{1,0:T(8,128)(2,1)}, bf16[128,1024]{1,0:T(8,128)(2,1)S(1)}, u32[]{:S(2)}, u32[]{:S(2)}) %collective-permute-start.4) | collective-permute-done | bytes 262176 | tf_op jit(solution)/shard_map/ppermute | solution.py:790
  193.7 27.1 %second_forward_and_back.1 = (bf16[2,8,64,512]{3,2,1,0:T(8,128)(2,1)}, f32[4,128,1024]{2,1,0:T(8,128)}, bf16[128,1024]{1,0:T(8,128)(2,1)}, bf16[128,1024]{1,0:T(...) custom-call(s32[2]{0:T(128)} %pad_add_fusion.refs_0_, ...), custom_call_target="tpu_custom_call" | custom-call | flops 7000000 | bytes 100000 | tf_op jit(solution)/shard_map/second_forward_and_back/pallas_call | solution.py:578
  222.2 8.4 %collective-permute-done.5.refs_9_ = bf16[128,1024]{1,0:T(8,128)(2,1)S(1)} collective-permute-done((bf16[128,1024]{1,0:T(8,128)(2,1)}, bf16[128,1024]{1,0:T(8,128)(2,1)S(1)}, u32[]{:S(2)}, u32[]{:S(2)}) %collective-permute-start.5) | collective-permute-done | bytes 262176 | tf_op jit(solution)/shard_map/ppermute | solution.py:809
  231.5 2.8 all-gather.11.cloned.1.call-done
  234.3 25.7 %shared_gradients.1 = (bf16[2,512,2048]{2,1,0:T(8,128)(2,1)}, bf16[8,64,2560]{2,1,0:T(8,128)(2,1)}, bf16[8,64,2560]{2,1,0:T(8,128)(2,1)}, bf16[8,64,2560]{2,1,0:...) custom-call(s32[2]{0:T(128)} %pad_add_fusion.refs_0_, ...), custom_call_target="tpu_custom_call" | custom-call | flops 7000000 | bytes 100000 | tf_op jit(solution)/shard_map/shared_gradients/pallas_call | solution.py:578
  260.7 4.6 %collective-permute-done.6.refs_2_.refs_3_ = bf16[8,64,2560]{2,1,0:T(8,128)(2,1)S(1)} collective-permute-done((bf16[8,64,2560]{2,1,0:T(8,128)(2,1)}, bf16[8,64,2560]{2,1,0:T(8,128)(2,1)S(1)}, u32[]{:S(2)}, u32[]{:S(2)}) %collective-permute-start.6) | collective-permute-done | bytes 2621472 | tf_op jit(solution)/shard_map/ppermute | solution.py:647
  275.8 12.9 %entry_gradient.1 = (bf16[2,256,1024]{2,1,0:T(8,128)(2,1)}, f32[128,1024]{1,0:T(8,128)}, f32[2,1024]{1,0:T(2,128)}) custom-call(bf16[16,832,1024]{2,1,0:T(8,128)(2,1)} %bitcast.97, bf16[2,512,2048]{2,1,0:T(8,128)(2,1)} %get-tuple-element.82.refs_1_, bf16[2,128,1024]{2,1,0:T(8,128)(2,1)} %bitcast.107, bf16[2,256,1024]{2,1,0:T(8,128)(2,1)} %bitcast.102, ...), custom_call_target="tpu_custom_call" | custom-call | flops 4300000 | bytes 100000 | tf_op jit(solution)/shard_map/entry_gradient/pallas_call | solution.py:578
  290.4 3.8 all-to-all-start.1
  294.2 15.7 %collective-permute-done.8.refs_2_.refs_3_ = bf16[4,64,2560]{2,1,0:T(8,128)(2,1)} collective-permute-done((bf16[4,64,2560]{2,1,0:T(8,128)(2,1)}, bf16[4,64,2560]{2,1,0:T(8,128)(2,1)}, u32[]{:S(2)}, u32[]{:S(2)}) %collective-permute-start.8) | collective-permute-done | bytes 1310752 | tf_op jit(solution)/shard_map/ppermute | solution.py:647
  314.1 3.6 collective-permute-done.10.refs_2_.refs_3_
  319.9 2.4 collective-permute-start.12
  325.6 2.8 dynamic-slice_select_fusion
  328.5 21.2 %hidden_gradients.1 = (bf16[2,64,1024]{2,1,0:T(8,128)(2,1)}, bf16[2,64,1024]{2,1,0:T(8,128)(2,1)}, f32[256,1024]{1,0:T(8,128)}, f32[1,256]{1,0:T(1,128)}) custom-call(s32[2]{0:T(128)} %pad_add_fusion.refs_0_, bf16[16,832,1024]{2,1,0:T(8,128)(2,1)} %bitcast.98, bf16[16,128,1024]{2,1,0:T(8,128)(2,1)} %bitcast.101, bf16[16,176,1024]{2,1,0:T(8,128)(2,1)} %bitcast.113, ...), custom_call_target="tpu_custom_call" | custom-call | flops 4300000 | bytes 100000 | tf_op jit(solution)/shard_map/hidden_gradients/pallas_call | solution.py:578
  353.1 2.8 fusion.10
  356.8 11.9 %collective-permute-done.11 = bf16[1,64,2560]{2,1,0:T(8,128)(2,1)S(1)} collective-permute-done((bf16[1,64,2560]{2,1,0:T(8,128)(2,1)S(1)}, bf16[1,64,2560]{2,1,0:T(8,128)(2,1)S(1)}, u32[]{:S(2)}, u32[]{:S(2)}) %collective-permute-start.11) | collective-permute-done | bytes 327712 | tf_op jit(solution)/shard_map/ppermute | solution.py:647
  (188 shorter events, 60.2 us)
Async XLA Ops:
  7.2 159.1 %all-gather.9.cloned.1.call-start = ((), (), s32[]{:S(2)}) async-start(), calls=%async_computation.2 | async-start | bytes 28966912 | tf_op jit(solution)/shard_map/all_gather | solution.py:671
  12.1 38.2 %copy-start.25 = (s32[16]{0:T(128)S(1)}, s32[16]{0:T(128)}, u32[]{:S(2)}) copy-start(s32[16]{0:T(128)} %constant.78.clone) | copy-start | bytes 196
  12.1 38.3 %copy-start.5 = (bf16[1,2,128,1024]{3,2,1,0:T(8,128)(2,1)S(1)}, bf16[1,2,128,1024]{3,2,1,0:T(8,128)(2,1)}, u32[]{:S(2)}) copy-start(bf16[1,2,128,1024]{3,2,1,0:T(8,128)(2,1)} %param.20) | copy-start | bytes 1572868
  13.5 38.9 %copy-start.20 = (s32[2,448]{1,0:T(2,128)S(1)}, s32[2,448]{1,0:T(2,128)}, u32[]{:S(2)}) copy-start(s32[2,448]{1,0:T(2,128)} %param.18) | copy-start | bytes 10756
  13.5 39.5 %all-to-all-start = ((bf16[16,42,192]{2,1,0:T(8,128)(2,1)}), bf16[16,42,192]{2,1,0:T(8,128)(2,1)S(1)}, u32[]{:S(2)}, u32[]{:S(2)}) async-start(bf16[16,42,192]{2,1,0:T(8,128)(2,1)} %bitcast.92), calls=%async_computation | async-start | bytes 786432 | tf_op jit(solution)/shard_map/all_to_all | solution.py:732
  21.0 213.3 %all-gather.11.cloned.1.call-start = ((), (), s32[]{:S(2)}) async-start(), calls=%async_computation.3 | async-start | bytes 4456448 | tf_op jit(solution)/shard_map/all_gather | solution.py:671
  59.2 4.2 %collective-permute-start = (bf16[8,48,1024]{2,1,0:T(8,128)(2,1)S(1)}, bf16[8,48,1024]{2,1,0:T(8,128)(2,1)S(1)}, u32[]{:S(2)}, u32[]{:S(2)}) collective-permute-start(bf16[8,48,1024]{2,1,0:T(8,128)(2,1)S(1)} %get-tuple-element.119), channel_id=1, source_target_pairs={{0,1},{1,0},{2,3},{3,2},{4,5},{5,4},{6,7},{7,6},{8,9},{9,8},{10,11... | collective-permute-start | bytes 2359304 | tf_op jit(solution)/shard_map/ppermute | solution.py:647
  63.7 20.2 %collective-permute-start.1 = (bf16[4,48,1024]{2,1,0:T(8,128)(2,1)S(1)}, bf16[4,48,1024]{2,1,0:T(8,128)(2,1)S(1)}, u32[]{:S(2)}, u32[]{:S(2)}) collective-permute-start(bf16[4,48,1024]{2,1,0:T(8,128)(2,1)S(1)} %get-tuple-element.64), channel_id=1, source_target_pairs={{0,2},{1,3},{2,0},{3,1},{4,6},{5,7},{6,4},{7,5},{8,10},{9,11},{10,... | collective-permute-start | bytes 1179656 | tf_op jit(solution)/shard_map/ppermute | solution.py:647
  84.3 11.5 %collective-permute-start.2 = (bf16[2,48,1024]{2,1,0:T(8,128)(2,1)S(1)}, bf16[2,48,1024]{2,1,0:T(8,128)(2,1)S(1)}, u32[]{:S(2)}, u32[]{:S(2)}) collective-permute-start(bf16[2,48,1024]{2,1,0:T(8,128)(2,1)S(1)} %get-tuple-element.66), channel_id=1, source_target_pairs={{0,4},{1,5},{2,6},{3,7},{4,0},{5,1},{6,2},{7,3},{8,12},{9,13},{10,... | collective-permute-start | bytes 589832 | tf_op jit(solution)/shard_map/ppermute | solution.py:647
  95.8 9.5 %collective-permute-start.3 = (bf16[1,48,1024]{2,1,0:T(8,128)(2,1)S(1)}, bf16[1,48,1024]{2,1,0:T(8,128)(2,1)S(1)}, u32[]{:S(2)}, u32[]{:S(2)}) collective-permute-start(bf16[1,48,1024]{2,1,0:T(8,128)(2,1)S(1)} %get-tuple-element.68), channel_id=1, source_target_pairs={{0,8},{1,9},{2,10},{3,11},{4,12},{5,13},{6,14},{7,15},{8,0},{9,1},... | collective-permute-start | bytes 294920 | tf_op jit(solution)/shard_map/ppermute | solution.py:647
  183.3 142.3 %all-gather.13.cloned.1.call-start = ((), (), s32[]{:S(2)}) async-start(), calls=%async_computation.4 | async-start | bytes 6127616 | tf_op jit(solution)/shard_map/all_gather | solution.py:671
  183.3 9.7 %collective-permute-start.4 = (bf16[128,1024]{1,0:T(8,128)(2,1)}, bf16[128,1024]{1,0:T(8,128)(2,1)S(1)}, u32[]{:S(2)}, u32[]{:S(2)}) collective-permute-start(bf16[128,1024]{1,0:T(8,128)(2,1)} %get-tuple-element.71), channel_id=1, source_target_pairs={{0,16},{1,17},{2,18},{3,19},{4,20},{5,21},{6,22},{7,23},{8,24},{9,... | collective-permute-start | bytes 786440 | tf_op jit(solution)/shard_map/ppermute | solution.py:790
  220.8 9.8 %collective-permute-start.5 = (bf16[128,1024]{1,0:T(8,128)(2,1)}, bf16[128,1024]{1,0:T(8,128)(2,1)S(1)}, u32[]{:S(2)}, u32[]{:S(2)}) collective-permute-start(bf16[128,1024]{1,0:T(8,128)(2,1)} %get-tuple-element.76), channel_id=1, source_target_pairs={{16,0},{17,1},{18,2},{19,3},{20,4},{21,5},{22,6},{23,7},{24,8},{25... | collective-permute-start | bytes 786440 | tf_op jit(solution)/shard_map/ppermute | solution.py:809
  260.1 5.2 %collective-permute-start.6 = (bf16[8,64,2560]{2,1,0:T(8,128)(2,1)}, bf16[8,64,2560]{2,1,0:T(8,128)(2,1)S(1)}, u32[]{:S(2)}, u32[]{:S(2)}) collective-permute-start(bf16[8,64,2560]{2,1,0:T(8,128)(2,1)} %get-tuple-element.87), channel_id=1, source_target_pairs={{0,1},{1,0},{2,3},{3,2},{4,5},{5,4},{6,7},{7,6},{8,9},{9,8},{10,11... | collective-permute-start | bytes 7864328 | tf_op jit(solution)/shard_map/ppermute | solution.py:647
  260.4 10.2 %collective-permute-start.7 = (bf16[8,64,2560]{2,1,0:T(8,128)(2,1)}, bf16[8,64,2560]{2,1,0:T(8,128)(2,1)S(1)}, u32[]{:S(2)}, u32[]{:S(2)}) collective-permute-start(bf16[8,64,2560]{2,1,0:T(8,128)(2,1)} %get-tuple-element.90), channel_id=1, source_target_pairs={{0,1},{1,0},{2,3},{3,2},{4,5},{5,4},{6,7},{7,6},{8,9},{9,8},{10,11... | collective-permute-start | bytes 7864328 | tf_op jit(solution)/shard_map/ppermute | solution.py:647
  268.8 41.1 %collective-permute-start.8 = (bf16[4,64,2560]{2,1,0:T(8,128)(2,1)}, bf16[4,64,2560]{2,1,0:T(8,128)(2,1)}, u32[]{:S(2)}, u32[]{:S(2)}) collective-permute-start(bf16[4,64,2560]{2,1,0:T(8,128)(2,1)} %get-tuple-element.88.refs_8_), channel_id=1, source_target_pairs={{0,2},{1,3},{2,0},{3,1},{4,6},{5,7},{6,4},{7,5},{8,10},{9,11},{10,... | collective-permute-start | bytes 3932168 | tf_op jit(solution)/shard_map/ppermute | solution.py:647
  272.4 45.3 %collective-permute-start.10 = (bf16[4,64,2560]{2,1,0:T(8,128)(2,1)}, bf16[4,64,2560]{2,1,0:T(8,128)(2,1)}, u32[]{:S(2)}, u32[]{:S(2)}) collective-permute-start(bf16[4,64,2560]{2,1,0:T(8,128)(2,1)} %get-tuple-element.91.refs_9_), channel_id=1, source_target_pairs={{0,4},{1,5},{2,6},{3,7},{4,0},{5,1},{6,2},{7,3},{8,12},{9,13},{10,... | collective-permute-start | bytes 3932168 | tf_op jit(solution)/shard_map/ppermute | solution.py:647
  290.4 32.7 %all-to-all-start.1 = ((f32[16,1,512]{2,1,0:T(1,128)}), f32[16,1,512]{2,1,0:T(1,128)S(1)}, u32[]{:S(2)}, u32[]{:S(2)}) async-start(f32[16,1,512]{2,1,0:T(1,128)} %reshape.243), calls=%async_computation.1 | async-start | bytes 65536 | tf_op jit(solution)/shard_map/all_to_all | solution.py:886
  312.6 37.1 %collective-permute-start.9 = (bf16[2,64,2560]{2,1,0:T(8,128)(2,1)}, bf16[2,64,2560]{2,1,0:T(8,128)(2,1)S(1)}, u32[]{:S(2)}, u32[]{:S(2)}) collective-permute-start(bf16[2,64,2560]{2,1,0:T(8,128)(2,1)} %get-tuple-element.97.refs_9_), channel_id=1, source_target_pairs={{0,4},{1,5},{2,6},{3,7},{4,0},{5,1},{6,2},{7,3},{8,12},{9,13},{10,... | collective-permute-start | bytes 1966088 | tf_op jit(solution)/shard_map/ppermute | solution.py:647
  319.9 31.7 %collective-permute-start.12 = (bf16[2,64,2560]{2,1,0:T(8,128)(2,1)}, bf16[2,64,2560]{2,1,0:T(8,128)(2,1)S(1)}, u32[]{:S(2)}, u32[]{:S(2)}) collective-permute-start(bf16[2,64,2560]{2,1,0:T(8,128)(2,1)} %get-tuple-element.101.refs_10_), channel_id=1, source_target_pairs={{0,8},{1,9},{2,10},{3,11},{4,12},{5,13},{6,14},{7,15},{8,0},{9,1},... | collective-permute-start | bytes 1966088 | tf_op jit(solution)/shard_map/ppermute | solution.py:647
  349.6 6.3 %collective-permute-start.14 = (bf16[2,64,1024]{2,1,0:T(8,128)(2,1)}, bf16[2,64,1024]{2,1,0:T(8,128)(2,1)S(1)}, u32[]{:S(2)}, u32[]{:S(2)}) collective-permute-start(bf16[2,64,1024]{2,1,0:T(8,128)(2,1)} %get-tuple-element.109), channel_id=1, source_target_pairs={{0,1},{1,0},{2,3},{3,2},{4,5},{5,4},{6,7},{7,6},{8,9},{9,8},{10,11... | collective-permute-start | bytes 786440 | tf_op jit(solution)/shard_map/ppermute | solution.py:877
  350.6 18.1 %collective-permute-start.11 = (bf16[1,64,2560]{2,1,0:T(8,128)(2,1)S(1)}, bf16[1,64,2560]{2,1,0:T(8,128)(2,1)S(1)}, u32[]{:S(2)}, u32[]{:S(2)}) collective-permute-start(bf16[1,64,2560]{2,1,0:T(8,128)(2,1)S(1)} %get-tuple-element.104.refs_4_), channel_id=1, source_target_pairs={{0,8},{1,9},{2,10},{3,11},{4,12},{5,13},{6,14},{7,15},{8,0},{9,1},... | collective-permute-start | bytes 983048 | tf_op jit(solution)/shard_map/ppermute | solution.py:647
  351.7 17.0 %collective-permute-start.13 = (bf16[1,64,2560]{2,1,0:T(8,128)(2,1)S(1)}, bf16[1,64,2560]{2,1,0:T(8,128)(2,1)S(1)}, u32[]{:S(2)}, u32[]{:S(2)}) collective-permute-start(bf16[1,64,2560]{2,1,0:T(8,128)(2,1)S(1)} %get-tuple-element.107), channel_id=1, source_target_pairs={{0,2},{1,3},{2,0},{3,1},{4,6},{5,7},{6,4},{7,5},{8,10},{9,11},{10,... | collective-permute-start | bytes 983048 | tf_op jit(solution)/shard_map/ppermute | solution.py:647
  356.1 14.5 %collective-permute-start.15 = (bf16[2,64,1024]{2,1,0:T(8,128)(2,1)S(1)}, bf16[2,64,1024]{2,1,0:T(8,128)(2,1)S(1)}, u32[]{:S(2)}, u32[]{:S(2)}) collective-permute-start(bf16[2,64,1024]{2,1,0:T(8,128)(2,1)S(1)} %pad_maximum_fusion.3), channel_id=1, source_target_pairs={{0,2},{1,3},{2,0},{3,1},{4,6},{5,7},{6,4},{7,5},{8,10},{9,11},{10,... | collective-permute-start | bytes 786440 | tf_op jit(solution)/shard_map/ppermute | solution.py:878
  (24 other events, 124.3 us)
Sparse Core Ops, SparseCore 0:
  12.2 154.1 all-gather.8
  183.4 50.8 all-gather.10
  236.6 71.1 all-gather.12

commit v5 on v4

--- a/solution.py
+++ b/solution.py
@@ -44,15 +44,25 @@
     return scale * (grad_hat - first - hat * second)
 
 
+GELU_RATE = 0.7978845608028654
+GELU_CUBE = 0.044715
+
+
+def gelu_inner(values):
+    square = values * values
+    return square, jnp.tanh(values * (GELU_RATE + GELU_RATE * GELU_CUBE * square))
+
+
 def gelu(values):
-    return 0.5 * values * (1.0 + jnp.tanh(0.7978845608028654 * (values + 0.044715 * values * values * values)))
+    _, inner = gelu_inner(values)
+    half = 0.5 * values
+    return half + half * inner
 
 
 def gelu_slope(values):
-    inner = jnp.tanh(0.7978845608028654 * (values + 0.044715 * values * values * values))
-    return 0.5 * (1.0 + inner) + 0.5 * values * (1.0 - inner * inner) * 0.7978845608028654 * (
-        1.0 + 3.0 * 0.044715 * values * values
-    )
+    square, inner = gelu_inner(values)
+    rise = values * (0.5 * GELU_RATE + 1.5 * GELU_RATE * GELU_CUBE * square)
+    return 0.5 + 0.5 * inner + rise * (1.0 - inner * inner)
 
 
 def sinusoid(key_count, model_width):
@@ -221,7 +231,7 @@
     return cot.astype(F32) + norm_back(hat, scale, total * vec[1:2]), total, hat
 
 
-def stage_one(place, weights, past, rev, entry, vec, hidden_bias, mask, cot, kv_hbm, rel_hbm, output, early, w_in, w_out, w_rel, ff_in, ff_out,
+def stage_one(place, weights, past, rev, entry, vec, hidden_bias, mask, cot, side_rows, kv_hbm, rel_hbm, output, early, w_in, w_out, w_rel, ff_in, ff_out,
               kv, rel, normed, q_content, q_position, mixed, sems):
     loads = Loads(sems)
     rows = w_in.shape[2]
@@ -269,7 +279,8 @@
     middle = wide_entry + dot(mixed[...], read_matrix(w_out))
     hat, _ = normalise(middle)
     normed_two = low(hat * vec[1:2] + vec[3:4])
-    early[...] = jnp.where(place[1] == 1, normed_two, cot[...])
+    early[:ROWS] = jnp.where(place[1] == 1, normed_two, cot[...])
+    early[ROWS:] = side_rows[...]
     total = feed_forward(normed_two, hidden_bias, ff_in, ff_out, waits_in, waits_out, None)
     output[...] = low(middle + total + vec[4:5])
     for copy in stores:
@@ -277,7 +288,7 @@
 
 
 def stage_two(place, weights, kv_past, rel_hbm, tokens, received, vec, hidden_bias, mask, cot,
-              probs_hbm, pre_hbm, entry, output, normed, q_content, q_position, kv_own, mixed, middle_out, normed_two, grad_low,
+              probs_hbm, pre_hbm, entry, normed, q_content, q_position, kv_own, mixed, middle_out, normed_two, grad_low,
               w_in, w_out, ff_in, ff_out, kv, rel, probs, pre, grad_mixed, grad_content, grad_position, grad_kv, sems):
     loads = Loads(sems)
     rows = w_in.shape[2]
@@ -318,11 +329,12 @@
     hat, _ = normalise(middle)
     flat = low(hat * vec[1:2] + vec[3:4])
     normed_two[...] = flat
-    total = feed_forward(flat, hidden_bias, ff_in, ff_out, waits_in, waits_out, pre)
+    for quarter in range(quarters):
+        waits_in[quarter].wait()
+        pre[quarter] = dot(flat, read_matrix(ff_in.at[quarter])) + hidden_bias[quarter : quarter + 1]
     stores.append(loads.start(pre, pre_hbm))
-    output[...] = low(middle_out[...] + total + vec[4:5])
-
-    grad_middle, _, _ = middle_back(cot[...], middle_out[...], vec, ff_in, ff_out, None, None, pre)
+
+    grad_middle, _, _ = middle_back(cot[...], middle_out[...], vec, ff_in, ff_out, None, waits_out, pre)
     grad_mixed[...] = low(dot_t(low(grad_middle), read_matrix(w_out)))
     attend_back(grad_mixed, q_content, q_position, kv, rel, probs, grad_content, grad_position, grad_kv, None)
     grad_query = low(grad_content[...].astype(F32) + grad_position[...].astype(F32))
@@ -459,8 +471,8 @@
         copy.wait()
 
 
-def stage_five(weights, grad_kv_hbm, comp, mem, entry, grad_query, grad_middle, vec, new_memory, grad_entry, sums,
-               w_in, grad_kv, grad_normed, sems):
+def stage_five(weights, grad_kv_hbm, pre_hbm, comp, mem, entry, grad_query, grad_middle, vec, middle, new_memory,
+               grad_entry, sums, output, w_in, grad_kv, grad_normed, pre, ff_out, sems):
     loads = Loads(sems)
     rows = w_in.shape[2]
     width = entry.shape[1]
@@ -468,6 +480,16 @@
     past_len = WIDE - ROWS
     copies = [loads.start(grad_kv_hbm, grad_kv)] + [
         loads.start(weights.at[:, pl.ds(index * rows, rows), :], w_in.at[index]) for index in range(3)
+    ]
+    quarters = ff_out.shape[0]
+    share = ff_out.shape[1]
+    wait_pre = loads.start(pre_hbm, pre)
+    waits_out = [
+        loads.start(
+            weights.at[pl.ds(quarter * share, share), pl.ds((5 + quarters) * rows, quarters * rows), :],
+            ff_out.at[quarter],
+        )
+        for quarter in range(quarters)
     ]
     kept = mem.shape[1] - half
     stores = [loads.start(mem.at[:, pl.ds(half, kept), :], new_memory.at[:, pl.ds(0, kept), :])] + [
@@ -501,16 +523,24 @@
         )
         sums[1:2, cols] = jnp.sum(grad_past, 0, keepdims=True) + jnp.sum(grad_tok, 0, keepdims=True)
     grad_entry[...] = grad_middle[...] + norm_back(hat_tok, scale_tok, grad_normed[...] * vec[0:1])
+    wait_pre.wait()
+    total = middle[...] + vec[4:5]
+    for quarter in range(quarters):
+        waits_out[quarter].wait()
+        total = total + dot(low(gelu(pre[quarter])), read_matrix(ff_out.at[quarter]))
+    output[...] = low(total)
     for copy in stores:
         copy.wait()
 
 
-def stage_six(place, weights, early, late, w_in, w_out, bias, hidden_bias, columns, keep, send, grad_out, grad_bias,
-              rows_one, rows_two, part_in, part_out, total_in, sems):
+def stage_six(columns_given, place, weights, early, late, w_in, w_out, bias, hidden_bias, *refs):
+    columns = refs[0] if columns_given else None
+    (keep, send, grad_out, grad_bias, rows_one, rows_two, part_in, part_out, total_in, sems) = refs[-10:]
     size = rows_one.shape[0]
     rows = part_in.shape[1]
     quarters, width = hidden_bias.shape
     share = size // quarters
+    shared = quarters * rows
     step = min(size, 4)
     is_first = place[1] == 1
     quarter = jnp.bitwise_and(place[0], quarters - 1)
@@ -518,8 +548,8 @@
     def loads(index):
         own = pl.ds(index * step, step)
         return (
-            pltpu.make_async_copy(early.at[own], rows_one.at[own], sems.at[2 * index]),
-            pltpu.make_async_copy(late.at[own, pl.ds(0, ROWS), :], rows_two.at[own], sems.at[2 * index + 1]),
+            pltpu.make_async_copy(early.at[own, pl.ds(0, ROWS), :], rows_one.at[own], sems.at[2 * index]),
+            pltpu.make_async_copy(late.at[own], rows_two.at[own], sems.at[2 * index + 1]),
         )
 
     count = size // step
@@ -533,13 +563,11 @@
             sems.at[2 * count + 1],
         ),
     )
-    for copy in copies:
+    for copy in loads(0) + copies:
         copy.start()
-    for index in range(count):
+    for index in range(1, count):
         for copy in loads(index):
             copy.start()
-    for copy in copies:
-        copy.wait()
     total_in[...] = jnp.zeros(total_in.shape, F32)
     grad_out[...] = jnp.zeros(grad_out.shape, F32)
     grad_bias[...] = jnp.zeros(grad_bias.shape, F32)
@@ -557,13 +585,51 @@
         grad_pre = low(dot_t(cot, w_out[...]) * gelu_slope(pre))
         grad_bias[...] += jnp.sum(grad_pre.astype(F32), 0, keepdims=True)
         grad_out[...] += t_dot(low(gelu(pre)), cot)
+
+        @pl.when(index == 0)
+        def _():
+            for copy in copies:
+                copy.wait()
+
+        if columns is None:
+            cols = pl.ds(pl.multiple_of((place[0] // quarters) * shared, 128), shared)
+            left = jnp.where(is_first, read_matrix(rows_one.at[own, :, cols]), read_matrix(rows_two.at[own, :, cols]))
+        else:
+            left = columns[pl.ds(index * step * ROWS, step * ROWS), :]
         pre = dot(normed, read_matrix(part_in)) + part_bias
         grad_pre = low(dot_t(cot, read_matrix(part_out)) * gelu_slope(pre))
-        total_in[...] += t_dot(columns[pl.ds(index * step * ROWS, step * ROWS), :], grad_pre)
+        total_in[...] += t_dot(left, grad_pre)
         return carry
 
     lax.fori_loop(0, count, body, 0)
     store_blocks(keep, send, total_in[...], 0, place[0], 0, (1, 2))
+
+
+def pack(attn_in, attn_out, rel_proj, ff_in, ff_out, shard):
+    rows, width = attn_out.shape
+    start = 0
+    for value in (attn_in, attn_out, rel_proj, ff_in):
+        for column in range(0, value.shape[1], width):
+            shard[start : start + rows, :] = low(value[:, column : column + width])
+            start += rows
+    shard[start:, :] = low(ff_out[...])
+
+
+def finish(place, keep_one, got_one, keep_two, got_two, own, near, far, grad_attn_in, grad_attn_out, grad_rel,
+           grad_ff_in):
+    width = grad_rel.shape[1]
+    wide = keep_one.shape[2]
+    one = keep_one[0].astype(F32) + got_one[0].astype(F32)
+    two = keep_two[0].astype(F32) + got_two[0].astype(F32)
+    rest = 3 * width - wide
+    grad_attn_in[:, :wide] = one
+    grad_attn_in[:, wide:] = two[:, :rest]
+    grad_rel[...] = two[:, rest : rest + width]
+    grad_attn_out[...] = two[:, rest + width :]
+    quarters = grad_ff_in.shape[1] // width
+    for index, value in enumerate((own[0], near[0], far[0], far[1])):
+        column = jnp.bitwise_xor(jnp.bitwise_and(place[0], quarters - 1), index)
+        grad_ff_in[:, pl.ds(pl.multiple_of(column * width, width), width)] = value.astype(F32)
 
 
 HBM = pl.BlockSpec(memory_space=pl.ANY)
@@ -573,7 +639,8 @@
 
 def call(body, name, in_specs, outs, scratch, copies, flops, args, after=(), in_hbm=0):
     def kernel(*refs):
-        body(*refs[: len(args)], *refs[len(args) + len(after) :])
+        stop = len(refs) if copies else -1
+        body(*refs[: len(args)], *refs[len(args) + len(after) : stop])
 
     return pl.pallas_call(
         kernel,
@@ -581,7 +648,7 @@
         in_specs=in_specs + [HBM] * len(after),
         out_specs=[HBM] * in_hbm + [VMEM] * (len(outs) - in_hbm),
         out_shape=[jax.ShapeDtypeStruct(shape, dtype) for shape, dtype in outs],
-        scratch_shapes=[pltpu.VMEM(shape, dtype) for shape, dtype in scratch] + [pltpu.SemaphoreType.DMA((copies,))],
+        scratch_shapes=[pltpu.VMEM(shape, dtype) for shape, dtype in scratch] + [pltpu.SemaphoreType.DMA((max(copies, 1),))],
         compiler_params=pltpu.CompilerParams(vmem_limit_bytes=VMEM_BYTES),
         cost_estimate=pl.CostEstimate(flops=flops // 1000, bytes_accessed=100_000, transcendentals=0),
     )(*args, *after)
@@ -714,14 +781,17 @@
     ff_bias_low = low(ff_bias[0]).astype(F32).reshape(1, my_hidden)
     hidden_bias = small[8:].reshape(quarters, size, rows).transpose(1, 0, 2).reshape(hidden_cols)
 
-    low_in, low_ff_in, low_ff_out = low(attn_in[0]), low(ff_in[0]), low(ff_out[0])
-    shard = jnp.concatenate(
-        [low_in[:, i * width : (i + 1) * width] for i in range(3)]
-        + [low(attn_out[0]), low(rel_proj[0])]
-        + [low_ff_in[:, i * width : (i + 1) * width] for i in range(quarters)]
-        + [low_ff_out],
+    (shard,) = call(
+        pack,
+        "pack",
+        [VMEM] * 5,
+        [(((5 + 2 * quarters) * rows, width), BF)],
+        [],
         0,
-    )
+        1000,
+        (attn_in[0], attn_out[0], rel_proj[0], ff_in[0], ff_out[0]),
+    )
+    low_ff_out = shard[(5 + quarters) * rows :]
     weights = gather(shard)
 
     def part(start, count=1):
@@ -777,12 +847,12 @@
     kv_past, rel, output, early = call(
         stage_one,
         "first_forward",
-        [SMEM, HBM] + [VMEM] * 7,
-        [kv_old, rel_all, flat_low, flat_low],
+        [SMEM, HBM] + [VMEM] * 8,
+        [kv_old, rel_all, flat_low, ((ROWS + side_pad.shape[0], width), BF)],
         [in_scratch, mat_scratch, mat_scratch, ff_in_scratch, ff_out_scratch, kv_all, rel_all] + [flat_low] * 4,
         7 + 2 * quarters,
         7_000_000_000,
-        (place, weights, past_normed, rev, flat_tokens, vec, bias_rows, mask, flat_cot),
+        (place, weights, past_normed, rev, flat_tokens, vec, bias_rows, mask, flat_cot, side_pad),
         (squeezed,),
         in_hbm=2,
     )
@@ -792,11 +862,11 @@
     mine_in = lax.dynamic_slice(
         weights, (0, (5 + me // quarter_cols) * rows, (me % quarter_cols) * my_hidden), (size, rows, my_hidden)
     )
-    (probs, pre, entry, output, normed, q_content, q_position, kv_own, mixed, middle, normed_two, grad_low) = call(
+    (probs, pre, entry, normed, q_content, q_position, kv_own, mixed, middle, normed_two, grad_low) = call(
         stage_two,
         "second_forward_and_back",
         [SMEM] + [HBM] * 3 + [VMEM] * 6,
-        [prob_all, pre_all_shape, flat_low, flat_low, flat_low, flat_low, flat_low, kv_tok, flat_low, flat_wide,
+        [prob_all, pre_all_shape, flat_low, flat_low, flat_low, flat_low, kv_tok, flat_low, flat_wide,
          flat_low, flat_low],
         [in_scratch, mat_scratch, ff_in_scratch, ff_out_scratch, kv_all, rel_all, prob_all, pre_all_shape, flat_low,
          flat_low, flat_low, kv_tok],
@@ -807,8 +877,8 @@
         in_hbm=2,
     )
     returned = lax.ppermute(grad_low, "section", [(1, 0)])
-    late = jnp.concatenate([jnp.where(first, returned, normed_two), side_pad], 0)
-    late = gather(gate(late, early))
+    late = jnp.where(first, returned, normed_two)
+    late = gather(late)
     half = size // 2
     other_order = order[:1] + order[2:] + order[1:2]
     wide = 5 * width // 2
@@ -840,16 +910,16 @@
     move_both()
     add_both()
     move_both()
-    new_memory, grad_entry, more = call(
+    new_memory, grad_entry, more, output = call(
         stage_five,
         "entry_gradient",
-        [HBM] * 2 + [VMEM] * 6,
-        [(memory.shape, BF), flat_wide, ((2, width), F32)],
-        [in_scratch, kv_all, flat_wide],
-        7,
-        4_300_000_000,
-        (weights, grad_kv, compressed, memory, entry, grad_query, grad_middle, vec),
-        (one_sum.send, two_sum.send),
+        [HBM] * 3 + [VMEM] * 7,
+        [(memory.shape, BF), flat_wide, ((2, width), F32), flat_low],
+        [in_scratch, kv_all, flat_wide, pre_all_shape, ff_out_scratch],
+        8 + quarters,
+        15_000_000_000_000,
+        (weights, grad_kv, pre, compressed, memory, entry, grad_query, grad_middle, vec, middle),
+        (one_sum.send, two_sum.send, early[0, :16, :128]),
         in_hbm=1,
     )
 
@@ -857,28 +927,27 @@
     move_both()
 
     shared = quarters * rows
-    columns = [
-        lax.dynamic_slice(value, (0, 0, (me // quarters) * shared), (size, ROWS, shared)).reshape(-1, shared)
-        for value in (early, late)
-    ]
-    columns = jnp.where(first, columns[0], columns[1])
+    columns = []
+    if shared % 128:
+        columns = [
+            lax.dynamic_slice(value, (0, 0, (me // quarters) * shared), (size, ROWS, shared)).reshape(-1, shared)
+            for value in (early, late)
+        ]
+        columns = [jnp.where(first, columns[0], columns[1])]
     keep, send, grad_ff_out, grad_ff_bias = call(
-        stage_six,
+        functools.partial(stage_six, bool(columns)),
         "hidden_gradients",
-        [SMEM] + [HBM] * 3 + [VMEM] * 5,
+        [SMEM] + [HBM] * 3 + [VMEM] * (4 + len(columns)),
         [((2, rows, width), BF)] * 2 + [((my_hidden, width), F32), ((1, my_hidden), F32)],
         [((size, ROWS, width), BF), ((size, ROWS, width), BF), mat_scratch,
          ((size // quarters, quarters * rows, width), BF), ((shared, width), F32)],
         2 + 2 * (size // min(size, 4)),
-        4_300_000_000,
-        (place, weights, early, late, mine_in, low_ff_out, ff_bias_low, bias_rows, columns),
+        20_000_000_000_000,
+        (place, weights, early, late, mine_in, low_ff_out, ff_bias_low, bias_rows) + tuple(columns),
         (one_sum.send, two_sum.send),
     )
     got = lax.ppermute(send, "stream", xor_pairs(size, 1))
     far = lax.ppermute(jnp.concatenate([keep[1:], got[1:]], 0), "stream", xor_pairs(size, 2))
-    grad_ff_in = jnp.concatenate([keep[:1], got[:1], far], 0)
-    grad_ff_in = grad_ff_in[jnp.arange(quarters, dtype=me.dtype) ^ (me % quarters)]
-    grad_ff_in = grad_ff_in.transpose(1, 0, 2).reshape(rows, hidden_cols).astype(F32)
     vectors = jnp.stack(
         [more[0], sums[1], more[1], sums[3], sums[4], jnp.sum(cot_comp.astype(F32), (0, 1)), sums[6], sums[7]]
     )
@@ -888,13 +957,18 @@
         one_sum.add(grad_ff_bias)
         two_sum.add(one_sum.send)
         move_both()
-    one, two = one_sum.last(), two_sum.last()
-    side_all = late[:, ROWS : ROWS + side_rows].reshape(-1, width)
+    grad_attn_in, grad_attn_out, grad_rel, grad_ff_in = call(
+        finish,
+        "finish",
+        [SMEM] + [VMEM] * 7,
+        [((rows, 3 * width), F32), ((rows, width), F32), ((rows, width), F32), ((rows, hidden_cols), F32)],
+        [],
+        0,
+        1000,
+        (place, one_sum.keep, one_sum.got, two_sum.keep, two_sum.got, keep[:1], got[:1], far),
+    )
+    side_all = early[:, ROWS : ROWS + side_rows].reshape(-1, width)
     grad_compress = t_dot(windows, side_all)
-    both = jnp.concatenate([one, two], 1)
-    grad_attn_in = both[:, : 3 * width]
-    grad_rel = both[:, 3 * width : 4 * width]
-    grad_attn_out = both[:, 4 * width :]
     grad_entry = grad_entry.reshape(tokens.shape)
 
     activations = low(output).reshape(tokens.shape)

time: 386 us -> 379 us (0.982)
  waiting for transfers between devices: 148 us -> 137 us
  Pallas kernels: 113 us -> 122 us
  other arithmetic: 19.2 us -> 13.8 us
    ppermute x12, waiting for transfers between devices: 72 us -> 61.1 us  [move(): lax.ppermute(self.send, 'stream', xor_pairs(lax.axis_size('stream'), bit))]
    pallas_call x5 -> x7, Pallas kernels: 104 us -> 110 us  [call(): pl.pallas_call(kernel, name=name, in_specs=in_specs + [HBM] * len(after),...]
    ppermute x1, waiting for transfers between devices: 0.01 us -> 3.88 us  [per_device(): lax.ppermute(jnp.concatenate([keep[1:], got[1:]], 0), 'stream', xor_pairs...]
    unnamed x62 -> x59, local copies, waits for them, and re-layouts: 7.86 us -> 5.52 us
  transfers between devices with their start and end apart: 21 -> 21, of which waited for: 13 -> 11; matrix products, arithmetic and copies ran while one was open for 9% -> 10% of each run, Pallas kernels for 25% -> 26%
where the time goes in v5:
time: 379 us; the launch traced here: 374 us
  waiting for transfers between devices  137 us (36%)
  Pallas kernels  122 us (32%)
  blocking collectives  29 us (8%)
  starting transfers between devices  28.9 us (8%)
  local copies, waits for them, and re-layouts  23.6 us (6%)
  between operations  14.8 us (4%)
  other arithmetic  13.8 us (4%)
  matrix products  4.48 us (1%)
    pallas_call x7, Pallas kernels, call(): pl.pallas_call(kernel, name=name, in_specs=in_specs + [HBM] * len(after),...  110 us
    ppermute x12, waiting for transfers between devices, move(): lax.ppermute(self.send, 'stream', xor_pairs(lax.axis_size('stream'), bit))  61.1 us
    all_gather x3, waiting for transfers between devices, gather(): return lax.all_gather(shard, 'stream', axis=0, tiled=False)  59.9 us
    all_gather x1, blocking collectives, gather(): return lax.all_gather(shard, 'stream', axis=0, tiled=False)  29 us
    pallas_call x9, Pallas kernels, add_halves(): pl.pallas_call(kernel, name='add_halves', grid=(half,), in_specs=specs +...  11.9 us
    ppermute x12, starting transfers between devices, move(): lax.ppermute(self.send, 'stream', xor_pairs(lax.axis_size('stream'), bit))  11.2 us
    ppermute x1, waiting for transfers between devices, per_device(): returned = lax.ppermute(grad_low, 'section', [(1, 0)])  8.52 us
  transfers between devices with their start and end apart: 21, of which 11 were waited for; matrix products, arithmetic and copies ran while one was open for 10% of the time, Pallas kernels for 26%

profile of v5, /device:TPU:0, one launch (start us, length us, event | category | flops | bytes accessed | tf_op | source)
XLA Modules:
  0.0 373.9 jit_solution(12718692498989308227)
XLA Ops:
  7.2 3.4 pack.1
  12.0 7.4 %all-to-all-start = ((bf16[16,42,192]{2,1,0:T(8,128)(2,1)}), bf16[16,42,192]{2,1,0:T(8,128)(2,1)S(1)}, u32[]{:S(2)}, u32[]{:S(2)}) async-start(bf16[16,42,192]{2,1,0:T(8,128)(2,1)} %bitcast.77), calls=%async_computation | async-start | bytes 786432 | tf_op jit(solution)/shard_map/all_to_all | solution.py:802
  19.6 29.0 %all-gather.4 = bf16[16,12,64]{2,1,0:T(8,128)(2,1)S(1)} all-gather(bf16[1,12,64]{2,1,0:T(8,128)(2,1)S(1)} %maximum_bitcast_fusion.1), channel_id=3, replica_groups=mesh['section'=2,'stream'=16] {'stream'}, dimensions={0}, use_global_device_ids=true | all-gather | bytes 26112 | tf_op jit(solution)/shard_map/all_gather | solution.py:738
  59.0 3.6 fusion.14
  67.6 15.4 %collective-permute-done.1.refs_2_.refs_3_ = bf16[4,48,1024]{2,1,0:T(8,128)(2,1)S(1)} collective-permute-done((bf16[4,48,1024]{2,1,0:T(8,128)(2,1)S(1)}, bf16[4,48,1024]{2,1,0:T(8,128)(2,1)S(1)}, u32[]{:S(2)}, u32[]{:S(2)}) %collective-permute-start.1) | collective-permute-done | bytes 393248 | tf_op jit(solution)/shard_map/ppermute | solution.py:714
  84.3 10.6 %collective-permute-done.2.refs_2_.refs_3_ = bf16[2,48,1024]{2,1,0:T(8,128)(2,1)S(1)} collective-permute-done((bf16[2,48,1024]{2,1,0:T(8,128)(2,1)S(1)}, bf16[2,48,1024]{2,1,0:T(8,128)(2,1)S(1)}, u32[]{:S(2)}, u32[]{:S(2)}) %collective-permute-start.2) | collective-permute-done | bytes 196640 | tf_op jit(solution)/shard_map/ppermute | solution.py:714
  95.7 8.7 %collective-permute-done.3 = bf16[1,48,1024]{2,1,0:T(8,128)(2,1)S(1)} collective-permute-done((bf16[1,48,1024]{2,1,0:T(8,128)(2,1)S(1)}, bf16[1,48,1024]{2,1,0:T(8,128)(2,1)S(1)}, u32[]{:S(2)}, u32[]{:S(2)}) %collective-permute-start.3) | collective-permute-done | bytes 98336 | tf_op jit(solution)/shard_map/ppermute | solution.py:714
  105.1 59.9 %all-gather.9.cloned.1.call-done = bf16[13312,1024]{1,0:T(8,128)(2,1)} async-done(((bf16[832,1024]{1,0:T(8,128)(2,1)}), bf16[13312,1024]{1,0:T(8,128)(2,1)}) %all-gather.9.cloned.1.call-update) | async-done | bytes 27262992 | tf_op jit(solution)/shard_map/all_gather | solution.py:738
  165.0 17.1 %first_forward.1 = (bf16[2,384,2048]{2,1,0:T(8,128)(2,1)}, bf16[512,1024]{1,0:T(8,128)(2,1)}, bf16[128,1024]{1,0:T(8,128)(2,1)}, bf16[176,1024]{1,0:T(8,128)(2,1)}) custom-call(s32[2]{0:T(128)} %pad_add_fusion.refs_0_, bf16[16,832,1024]{2,1,0:T(8,128)(2,1)} %bitcast.78, bf16[2,384,1024]{2,1,0:T(8,128)(2,1)} %fusion.5.refs_2_.refs_7_, ...), custom_call_target="tpu_custom_call" | custom-call | flops 7000000 | bytes 100000 | tf_op jit(solution)/shard_map/first_forward/pallas_call | solution.py:645
  182.1 3.8 %collective-permute-start.4 = (bf16[128,1024]{1,0:T(8,128)(2,1)}, bf16[128,1024]{1,0:T(8,128)(2,1)S(1)}, u32[]{:S(2)}, u32[]{:S(2)}) collective-permute-start(bf16[128,1024]{1,0:T(8,128)(2,1)} %get-tuple-element.75), channel_id=1, source_target_pairs={{0,16},{1,17},{2,18},{3,19},{4,20},{5,21},{6,22},{7,23},{8,24},{9,... | collective-permute-start | bytes 786440 | tf_op jit(solution)/shard_map/ppermute | solution.py:860
  187.9 3.9 %collective-permute-done.4.refs_5_ = bf16[128,1024]{1,0:T(8,128)(2,1)S(1)} collective-permute-done((bf16[128,1024]{1,0:T(8,128)(2,1)}, bf16[128,1024]{1,0:T(8,128)(2,1)S(1)}, u32[]{:S(2)}, u32[]{:S(2)}) %collective-permute-start.4) | collective-permute-done | bytes 262176 | tf_op jit(solution)/shard_map/ppermute | solution.py:860
  192.5 25.6 %second_forward_and_back.1 = (bf16[2,8,64,512]{3,2,1,0:T(8,128)(2,1)}, f32[4,128,1024]{2,1,0:T(8,128)}, bf16[128,1024]{1,0:T(8,128)(2,1)}, bf16[128,1024]{1,0:T(...) custom-call(s32[2]{0:T(128)} %pad_add_fusion.refs_0_, ...), custom_call_target="tpu_custom_call" | custom-call | flops 7000000 | bytes 100000 | tf_op jit(solution)/shard_map/second_forward_and_back/pallas_call | solution.py:645
  219.4 8.5 %collective-permute-done.5.refs_9_ = bf16[128,1024]{1,0:T(8,128)(2,1)S(1)} collective-permute-done((bf16[128,1024]{1,0:T(8,128)(2,1)}, bf16[128,1024]{1,0:T(8,128)(2,1)S(1)}, u32[]{:S(2)}, u32[]{:S(2)}) %collective-permute-start.5) | collective-permute-done | bytes 262176 | tf_op jit(solution)/shard_map/ppermute | solution.py:879
  228.8 25.8 %shared_gradients.1 = (bf16[2,512,2048]{2,1,0:T(8,128)(2,1)}, bf16[8,64,2560]{2,1,0:T(8,128)(2,1)}, bf16[8,64,2560]{2,1,0:T(8,128)(2,1)}, bf16[8,64,2560]{2,1,0:...) custom-call(s32[2]{0:T(128)} %pad_add_fusion.refs_0_, ...), custom_call_target="tpu_custom_call" | custom-call | flops 7000000 | bytes 100000 | tf_op jit(solution)/shard_map/shared_gradients/pallas_call | solution.py:645
  261.1 4.0 %add_halves.13 = (bf16[4,64,2560]{2,1,0:T(8,128)(2,1)S(1)}, bf16[4,64,2560]{2,1,0:T(8,128)(2,1)}) custom-call(bf16[8,64,2560]{2,1,0:T(8,128)(2,1)S(1)} %copy-done.1, bf16[8,64,2560]{2,1,0:T(8,128)(2,1)S(1)} %copy-done.1, bf16[8,64,2560]{2,1,0:T(8,128)(2,1)} %collective-permute-done.7.refs_2_.refs_3_, bf16[8,64,2560]{2,1,0:T(8,128)(2,1)} %collective-permute-done.7.refs_2_.refs_3_), custom_call_target="tpu_custom_call" | custom-call | flops 1000 | bytes 100000 | tf_op jit(solution)/shard_map/add_halves/pallas_call | solution.py:682
  267.5 3.8 %add_halves.12 = (bf16[4,64,2560]{2,1,0:T(8,128)(2,1)S(1)}, bf16[4,64,2560]{2,1,0:T(8,128)(2,1)}) custom-call(bf16[8,64,2560]{2,1,0:T(8,128)(2,1)S(1)} %copy-done, bf16[8,64,2560]{2,1,0:T(8,128)(2,1)S(1)} %copy-done, bf16[8,64,2560]{2,1,0:T(8,128)(2,1)} %collective-permute-done.6.refs_2_.refs_3_, bf16[8,64,2560]{2,1,0:T(8,128)(2,1)} %collective-permute-done.6.refs_2_.refs_3_), custom_call_target="tpu_custom_call" | custom-call | flops 1000 | bytes 100000 | tf_op jit(solution)/shard_map/add_halves/pallas_call | solution.py:682
  274.1 14.9 %entry_gradient.1 = (bf16[2,256,1024]{2,1,0:T(8,128)(2,1)}, f32[128,1024]{1,0:T(8,128)}, f32[2,1024]{1,0:T(2,128)}, bf16[128,1024]{1,0:T(8,128)(2,1)}) custom-call(bf16[16,832,1024]{2,1,0:T(8,128)(2,1)} %bitcast.82, bf16[2,512,2048]{2,1,0:T(8,128)(2,1)} %get-tuple-element.85.refs_1_, f32[4,128,1024]{2,1,0:T(8,128)} %get-tuple-element.78.refs_6_.refs_2_, ...), custom_call_target="tpu_custom_call" | custom-call | flops 15000000512 | bytes 100000 | tf_op jit(solution)/shard_map/entry_gradient/pallas_call | solution.py:645
  290.7 4.4 %all-to-all-start.1 = ((f32[16,1,512]{2,1,0:T(1,128)}), f32[16,1,512]{2,1,0:T(1,128)S(1)}, u32[]{:S(2)}, u32[]{:S(2)}) async-start(f32[16,1,512]{2,1,0:T(1,128)} %reshape.190), calls=%async_computation.1 | async-start | bytes 65536 | tf_op jit(solution)/shard_map/all_to_all | solution.py:955
  295.1 15.7 %collective-permute-done.8.refs_2_.refs_3_ = bf16[4,64,2560]{2,1,0:T(8,128)(2,1)} collective-permute-done((bf16[4,64,2560]{2,1,0:T(8,128)(2,1)}, bf16[4,64,2560]{2,1,0:T(8,128)(2,1)}, u32[]{:S(2)}, u32[]{:S(2)}) %collective-permute-start.8) | collective-permute-done | bytes 1310752 | tf_op jit(solution)/shard_map/ppermute | solution.py:714
  318.6 20.4 %hidden_gradients.1 = (bf16[2,64,1024]{2,1,0:T(8,128)(2,1)}, bf16[2,64,1024]{2,1,0:T(8,128)(2,1)}, f32[256,1024]{1,0:T(8,128)}, f32[1,256]{1,0:T(1,128)}) custom-call(s32[2]{0:T(128)} %pad_add_fusion.refs_0_, bf16[16,832,1024]{2,1,0:T(8,128)(2,1)} %bitcast.83, bf16[16,176,1024]{2,1,0:T(8,128)(2,1)} %bitcast.109, bf16[16,128,1024]{2,1,0:T(8,128)(2,1)} %bitcast.111, ...), custom_call_target="tpu_custom_call" | custom-call | flops 20000000000 | bytes 100000 | tf_op jit(solution)/shard_map/hidden_gradients/pallas_call | solution.py:645
  339.1 2.8 fusion.10
  349.9 3.9 %collective-permute-done.15.refs_7_ = bf16[2,64,1024]{2,1,0:T(8,128)(2,1)S(1)} collective-permute-done((bf16[2,64,1024]{2,1,0:T(8,128)(2,1)S(1)}, bf16[2,64,1024]{2,1,0:T(8,128)(2,1)S(1)}, u32[]{:S(2)}, u32[]{:S(2)}) %collective-permute-start.15) | collective-permute-done | bytes 262176 | tf_op jit(solution)/shard_map/ppermute | solution.py:950
  353.8 6.6 %collective-permute-done.13.refs_4_ = bf16[1,64,2560]{2,1,0:T(8,128)(2,1)S(1)} collective-permute-done((bf16[1,64,2560]{2,1,0:T(8,128)(2,1)S(1)}, bf16[1,64,2560]{2,1,0:T(8,128)(2,1)S(1)}, u32[]{:S(2)}, u32[]{:S(2)}) %collective-permute-start.13) | collective-permute-done | bytes 327712 | tf_op jit(solution)/shard_map/ppermute | solution.py:714
  364.0 2.9 finish.1
  (171 shorter events, 56.9 us)
Async XLA Ops:
  7.2 157.8 %all-gather.9.cloned.1.call-start = ((), (), s32[]{:S(2)}) async-start(), calls=%async_computation.2 | async-start | bytes 28966912 | tf_op jit(solution)/shard_map/all_gather | solution.py:738
  10.7 38.2 %copy-start.9 = (bf16[1,2,128,1024]{3,2,1,0:T(8,128)(2,1)S(1)}, bf16[1,2,128,1024]{3,2,1,0:T(8,128)(2,1)}, u32[]{:S(2)}) copy-start(bf16[1,2,128,1024]{3,2,1,0:T(8,128)(2,1)} %param.20) | copy-start | bytes 1572868
  10.7 40.0 %copy-start.22 = (s32[2,448]{1,0:T(2,128)S(1)}, s32[2,448]{1,0:T(2,128)}, u32[]{:S(2)}) copy-start(s32[2,448]{1,0:T(2,128)} %param.18) | copy-start | bytes 10756
  10.7 40.0 %copy-start.14 = (bf16[1,2,21,1024]{3,1,2,0:T(2,128)(2,1)S(1)}, bf16[1,2,21,1024]{3,1,2,0:T(2,128)(2,1)}, u32[]{:S(2)}) copy-start(bf16[1,2,21,1024]{3,1,2,0:T(2,128)(2,1)} %param.22) | copy-start | bytes 258052
  12.0 40.0 %all-to-all-start = ((bf16[16,42,192]{2,1,0:T(8,128)(2,1)}), bf16[16,42,192]{2,1,0:T(8,128)(2,1)S(1)}, u32[]{:S(2)}, u32[]{:S(2)}) async-start(bf16[16,42,192]{2,1,0:T(8,128)(2,1)} %bitcast.77), calls=%async_computation | async-start | bytes 786432 | tf_op jit(solution)/shard_map/all_to_all | solution.py:802
  19.4 253.4 %all-gather.11.cloned.1.call-start = ((), (), s32[]{:S(2)}) async-start(), calls=%async_computation.3 | async-start | bytes 6127616 | tf_op jit(solution)/shard_map/all_gather | solution.py:738
  58.3 4.3 %collective-permute-start = (bf16[8,48,1024]{2,1,0:T(8,128)(2,1)S(1)}, bf16[8,48,1024]{2,1,0:T(8,128)(2,1)S(1)}, u32[]{:S(2)}, u32[]{:S(2)}) collective-permute-start(bf16[8,48,1024]{2,1,0:T(8,128)(2,1)S(1)} %get-tuple-element.125), channel_id=1, source_target_pairs={{0,1},{1,0},{2,3},{3,2},{4,5},{5,4},{6,7},{7,6},{8,9},{9,8},{10,11... | collective-permute-start | bytes 2359304 | tf_op jit(solution)/shard_map/ppermute | solution.py:714
  62.9 20.2 %collective-permute-start.1 = (bf16[4,48,1024]{2,1,0:T(8,128)(2,1)S(1)}, bf16[4,48,1024]{2,1,0:T(8,128)(2,1)S(1)}, u32[]{:S(2)}, u32[]{:S(2)}) collective-permute-start(bf16[4,48,1024]{2,1,0:T(8,128)(2,1)S(1)} %get-tuple-element.68), channel_id=1, source_target_pairs={{0,2},{1,3},{2,0},{3,1},{4,6},{5,7},{6,4},{7,5},{8,10},{9,11},{10,... | collective-permute-start | bytes 1179656 | tf_op jit(solution)/shard_map/ppermute | solution.py:714
  83.4 11.5 %collective-permute-start.2 = (bf16[2,48,1024]{2,1,0:T(8,128)(2,1)S(1)}, bf16[2,48,1024]{2,1,0:T(8,128)(2,1)S(1)}, u32[]{:S(2)}, u32[]{:S(2)}) collective-permute-start(bf16[2,48,1024]{2,1,0:T(8,128)(2,1)S(1)} %get-tuple-element.70), channel_id=1, source_target_pairs={{0,4},{1,5},{2,6},{3,7},{4,0},{5,1},{6,2},{7,3},{8,12},{9,13},{10,... | collective-permute-start | bytes 589832 | tf_op jit(solution)/shard_map/ppermute | solution.py:714
  95.0 9.4 %collective-permute-start.3 = (bf16[1,48,1024]{2,1,0:T(8,128)(2,1)S(1)}, bf16[1,48,1024]{2,1,0:T(8,128)(2,1)S(1)}, u32[]{:S(2)}, u32[]{:S(2)}) collective-permute-start(bf16[1,48,1024]{2,1,0:T(8,128)(2,1)S(1)} %get-tuple-element.72), channel_id=1, source_target_pairs={{0,8},{1,9},{2,10},{3,11},{4,12},{5,13},{6,14},{7,15},{8,0},{9,1},... | collective-permute-start | bytes 294920 | tf_op jit(solution)/shard_map/ppermute | solution.py:714
  182.1 136.5 %all-gather.13.cloned.1.call-start = ((), (), s32[]{:S(2)}) async-start(), calls=%async_computation.4 | async-start | bytes 4456448 | tf_op jit(solution)/shard_map/all_gather | solution.py:738
  182.1 9.7 %collective-permute-start.4 = (bf16[128,1024]{1,0:T(8,128)(2,1)}, bf16[128,1024]{1,0:T(8,128)(2,1)S(1)}, u32[]{:S(2)}, u32[]{:S(2)}) collective-permute-start(bf16[128,1024]{1,0:T(8,128)(2,1)} %get-tuple-element.75), channel_id=1, source_target_pairs={{0,16},{1,17},{2,18},{3,19},{4,20},{5,21},{6,22},{7,23},{8,24},{9,... | collective-permute-start | bytes 786440 | tf_op jit(solution)/shard_map/ppermute | solution.py:860
  218.1 9.8 %collective-permute-start.5 = (bf16[128,1024]{1,0:T(8,128)(2,1)}, bf16[128,1024]{1,0:T(8,128)(2,1)S(1)}, u32[]{:S(2)}, u32[]{:S(2)}) collective-permute-start(bf16[128,1024]{1,0:T(8,128)(2,1)} %get-tuple-element.79), channel_id=1, source_target_pairs={{16,0},{17,1},{18,2},{19,3},{20,4},{21,5},{22,6},{23,7},{24,8},{25... | collective-permute-start | bytes 786440 | tf_op jit(solution)/shard_map/ppermute | solution.py:879
  254.6 6.5 %collective-permute-start.7 = (bf16[8,64,2560]{2,1,0:T(8,128)(2,1)}, bf16[8,64,2560]{2,1,0:T(8,128)(2,1)}, u32[]{:S(2)}, u32[]{:S(2)}) collective-permute-start(bf16[8,64,2560]{2,1,0:T(8,128)(2,1)} %get-tuple-element.93), channel_id=1, source_target_pairs={{0,1},{1,0},{2,3},{3,2},{4,5},{5,4},{6,7},{7,6},{8,9},{9,8},{10,11... | collective-permute-start | bytes 7864328 | tf_op jit(solution)/shard_map/ppermute | solution.py:714
  254.7 12.8 %collective-permute-start.6 = (bf16[8,64,2560]{2,1,0:T(8,128)(2,1)}, bf16[8,64,2560]{2,1,0:T(8,128)(2,1)}, u32[]{:S(2)}, u32[]{:S(2)}) collective-permute-start(bf16[8,64,2560]{2,1,0:T(8,128)(2,1)} %get-tuple-element.90), channel_id=1, source_target_pairs={{0,1},{1,0},{2,3},{3,2},{4,5},{5,4},{6,7},{7,6},{8,9},{9,8},{10,11... | collective-permute-start | bytes 7864328 | tf_op jit(solution)/shard_map/ppermute | solution.py:714
  266.1 49.1 %collective-permute-start.10 = (bf16[4,64,2560]{2,1,0:T(8,128)(2,1)}, bf16[4,64,2560]{2,1,0:T(8,128)(2,1)S(1)}, u32[]{:S(2)}, u32[]{:S(2)}) collective-permute-start(bf16[4,64,2560]{2,1,0:T(8,128)(2,1)} %get-tuple-element.94.refs_11_), channel_id=1, source_target_pairs={{0,4},{1,5},{2,6},{3,7},{4,0},{5,1},{6,2},{7,3},{8,12},{9,13},{10,... | collective-permute-start | bytes 3932168 | tf_op jit(solution)/shard_map/ppermute | solution.py:714
  271.3 39.5 %collective-permute-start.8 = (bf16[4,64,2560]{2,1,0:T(8,128)(2,1)}, bf16[4,64,2560]{2,1,0:T(8,128)(2,1)}, u32[]{:S(2)}, u32[]{:S(2)}) collective-permute-start(bf16[4,64,2560]{2,1,0:T(8,128)(2,1)} %get-tuple-element.91.refs_10_), channel_id=1, source_target_pairs={{0,2},{1,3},{2,0},{3,1},{4,6},{5,7},{6,4},{7,5},{8,10},{9,11},{10,... | collective-permute-start | bytes 3932168 | tf_op jit(solution)/shard_map/ppermute | solution.py:714
  290.7 51.9 %all-to-all-start.1 = ((f32[16,1,512]{2,1,0:T(1,128)}), f32[16,1,512]{2,1,0:T(1,128)S(1)}, u32[]{:S(2)}, u32[]{:S(2)}) async-start(f32[16,1,512]{2,1,0:T(1,128)} %reshape.190), calls=%async_computation.1 | async-start | bytes 65536 | tf_op jit(solution)/shard_map/all_to_all | solution.py:955
  313.7 31.6 %collective-permute-start.9 = (bf16[2,64,2560]{2,1,0:T(8,128)(2,1)}, bf16[2,64,2560]{2,1,0:T(8,128)(2,1)S(1)}, u32[]{:S(2)}, u32[]{:S(2)}) collective-permute-start(bf16[2,64,2560]{2,1,0:T(8,128)(2,1)} %get-tuple-element.102.refs_8_), channel_id=1, source_target_pairs={{0,4},{1,5},{2,6},{3,7},{4,0},{5,1},{6,2},{7,3},{8,12},{9,13},{10,... | collective-permute-start | bytes 1966088 | tf_op jit(solution)/shard_map/ppermute | solution.py:714
  316.2 31.1 %collective-permute-start.12 = (bf16[2,64,2560]{2,1,0:T(8,128)(2,1)}, bf16[2,64,2560]{2,1,0:T(8,128)(2,1)S(1)}, u32[]{:S(2)}, u32[]{:S(2)}) collective-permute-start(bf16[2,64,2560]{2,1,0:T(8,128)(2,1)} %get-tuple-element.105.refs_9_), channel_id=1, source_target_pairs={{0,8},{1,9},{2,10},{3,11},{4,12},{5,13},{6,14},{7,15},{8,0},{9,1},... | collective-permute-start | bytes 1966088 | tf_op jit(solution)/shard_map/ppermute | solution.py:714
  339.0 4.9 %collective-permute-start.14 = (bf16[2,64,1024]{2,1,0:T(8,128)(2,1)}, bf16[2,64,1024]{2,1,0:T(8,128)(2,1)S(1)}, u32[]{:S(2)}, u32[]{:S(2)}) collective-permute-start(bf16[2,64,1024]{2,1,0:T(8,128)(2,1)} %get-tuple-element.113), channel_id=1, source_target_pairs={{0,1},{1,0},{2,3},{3,2},{4,5},{5,4},{6,7},{7,6},{8,9},{9,8},{10,11... | collective-permute-start | bytes 786440 | tf_op jit(solution)/shard_map/ppermute | solution.py:949
  344.6 9.2 %collective-permute-start.15 = (bf16[2,64,1024]{2,1,0:T(8,128)(2,1)S(1)}, bf16[2,64,1024]{2,1,0:T(8,128)(2,1)S(1)}, u32[]{:S(2)}, u32[]{:S(2)}) collective-permute-start(bf16[2,64,1024]{2,1,0:T(8,128)(2,1)S(1)} %pad_maximum_fusion.1), channel_id=1, source_target_pairs={{0,2},{1,3},{2,0},{3,1},{4,6},{5,7},{6,4},{7,5},{8,10},{9,11},{10,... | collective-permute-start | bytes 786440 | tf_op jit(solution)/shard_map/ppermute | solution.py:950
  345.4 17.8 %collective-permute-start.11 = (bf16[1,64,2560]{2,1,0:T(8,128)(2,1)S(1)}, bf16[1,64,2560]{2,1,0:T(8,128)(2,1)S(1)}, u32[]{:S(2)}, u32[]{:S(2)}) collective-permute-start(bf16[1,64,2560]{2,1,0:T(8,128)(2,1)S(1)} %get-tuple-element.108.refs_4_), channel_id=1, source_target_pairs={{0,8},{1,9},{2,10},{3,11},{4,12},{5,13},{6,14},{7,15},{8,0},{9,1},... | collective-permute-start | bytes 983048 | tf_op jit(solution)/shard_map/ppermute | solution.py:714
  348.2 12.2 %collective-permute-start.13 = (bf16[1,64,2560]{2,1,0:T(8,128)(2,1)S(1)}, bf16[1,64,2560]{2,1,0:T(8,128)(2,1)S(1)}, u32[]{:S(2)}, u32[]{:S(2)}) collective-permute-start(bf16[1,64,2560]{2,1,0:T(8,128)(2,1)S(1)} %get-tuple-element.111), channel_id=1, source_target_pairs={{0,2},{1,3},{2,0},{3,1},{4,6},{5,7},{6,4},{7,5},{8,10},{9,11},{10,... | collective-permute-start | bytes 983048 | tf_op jit(solution)/shard_map/ppermute | solution.py:714
  (26 other events, 226.7 us)
Sparse Core Ops, SparseCore 0:
  10.8 154.1 all-gather.8
  182.2 59.3 all-gather.10
  243.7 60.6 all-gather.12

commit v6 on v5

--- a/solution.py
+++ b/solution.py
@@ -108,7 +108,7 @@
         both = [(head, seg) for head in heads for seg in range(2)]
         cols = {head: slice(head * head_dim, (head + 1) * head_dim) for head in heads}
         vcols = {head: slice(width + head * head_dim, width + (head + 1) * head_dim) for head in heads}
-        full = {head: dot_t(q_position[:, cols[head]], rel[:, cols[head]]) for head in heads}
+        full = {head: dot(q_position[:, cols[head]], rel[cols[head], :]) for head in heads}
         content = [dot_t(q_content[own[seg], cols[head]], kv[seg, :, cols[head]]) for head, seg in both]
         position = [
             pltpu.roll(full[head][own[seg]], WIDE - half + 1, 1, stride=1, stride_axis=0) for head, seg in both
@@ -173,7 +173,7 @@
             grad_content[own[seg], cols[head]] = low(value)
         for index, head in enumerate(heads):
             pair = jnp.concatenate(skewed[2 * index : 2 * index + 2], 0)
-            grad_position[:, cols[head]] = low(dot(pair, rel[:, cols[head]]))
+            grad_position[:, cols[head]] = low(dot_t(pair, rel[cols[head], :]))
             if grad_rel is not None:
                 grad_rel[:, cols[head]] = low(t_dot(pair, q_position[:, cols[head]]))
         for score, value, (head, seg) in zip(scores, grad_outs, both):
@@ -231,8 +231,8 @@
     return cot.astype(F32) + norm_back(hat, scale, total * vec[1:2]), total, hat
 
 
-def stage_one(place, weights, past, rev, entry, vec, hidden_bias, mask, cot, side_rows, kv_hbm, rel_hbm, output, early, w_in, w_out, w_rel, ff_in, ff_out,
-              kv, rel, normed, q_content, q_position, mixed, sems):
+def stage_one(place, weights, past, rel, entry, vec, hidden_bias, mask, cot, side_rows, kv_hbm, output, early, w_in, w_out, ff_in, ff_out,
+              kv, normed, q_content, q_position, mixed, sems):
     loads = Loads(sems)
     rows = w_in.shape[2]
     width = entry.shape[1]
@@ -242,16 +242,15 @@
         return loads.start(weights.at[:, pl.ds(index * rows, rows), :], target)
 
     key_value = [part(1, w_in.at[1]), part(2, w_in.at[2])]
-    wait_rel = part(4, w_rel)
     wait_query = part(0, w_in.at[0])
     wait_out = part(3, w_out)
     share = ff_out.shape[1]
     waits_in, waits_out = [], []
     for quarter in range(quarters):
-        waits_in.append(part(5 + quarter, ff_in.at[quarter]))
+        waits_in.append(part(4 + quarter, ff_in.at[quarter]))
         waits_out.append(
             loads.start(
-                weights.at[pl.ds(quarter * share, share), pl.ds((5 + quarters) * rows, quarters * rows), :],
+                weights.at[pl.ds(quarter * share, share), pl.ds((4 + quarters) * rows, quarters * rows), :],
                 ff_out.at[quarter],
             )
         )
@@ -264,9 +263,6 @@
                 dot(past[seg], read_matrix(w_in.at[1 + side]))
             )
     stores = [loads.start(kv.at[:, pl.ds(0, past_len), :], kv_hbm)]
-    wait_rel.wait()
-    rel[...] = low(dot(rev[...], read_matrix(w_rel)))
-    stores.append(loads.start(rel, rel_hbm))
 
     class Done:
         def wait(self):
@@ -307,10 +303,10 @@
     share = ff_out.shape[1]
     waits_in, waits_out = [], []
     for quarter in range(quarters):
-        waits_in.append(part(5 + quarter, ff_in.at[quarter]))
+        waits_in.append(part(4 + quarter, ff_in.at[quarter]))
         waits_out.append(
             loads.start(
-                weights.at[pl.ds(quarter * share, share), pl.ds((5 + quarters) * rows, quarters * rows), :],
+                weights.at[pl.ds(quarter * share, share), pl.ds((4 + quarters) * rows, quarters * rows), :],
                 ff_out.at[quarter],
             )
         )
@@ -390,11 +386,11 @@
     for quarter in range(quarters):
         waits_out.append(
             loads.start(
-                weights.at[pl.ds(quarter * share, share), pl.ds((5 + quarters) * rows, quarters * rows), :],
+                weights.at[pl.ds(quarter * share, share), pl.ds((4 + quarters) * rows, quarters * rows), :],
                 ff_out.at[quarter],
             )
         )
-        waits_in.append(loads.start(weights.at[:, pl.ds((5 + quarter) * rows, rows), :], ff_in.at[quarter]))
+        waits_in.append(loads.start(weights.at[:, pl.ds((4 + quarter) * rows, rows), :], ff_in.at[quarter]))
     wait_out = loads.start(weights.at[:, pl.ds(3 * rows, rows), :], w_out)
     others = [
         loads.start(kv_past, kv.at[:, pl.ds(0, past_len), :]),
@@ -486,7 +482,7 @@
     wait_pre = loads.start(pre_hbm, pre)
     waits_out = [
         loads.start(
-            weights.at[pl.ds(quarter * share, share), pl.ds((5 + quarters) * rows, quarters * rows), :],
+            weights.at[pl.ds(quarter * share, share), pl.ds((4 + quarters) * rows, quarters * rows), :],
             ff_out.at[quarter],
         )
         for quarter in range(quarters)
@@ -555,10 +551,10 @@
     count = size // step
     copies = (
         pltpu.make_async_copy(
-            weights.at[:, pl.ds((5 + quarter) * rows, rows), :], part_in, sems.at[2 * count]
+            weights.at[:, pl.ds((4 + quarter) * rows, rows), :], part_in, sems.at[2 * count]
         ),
         pltpu.make_async_copy(
-            weights.at[pl.ds(quarter * share, share), pl.ds((5 + quarters) * rows, quarters * rows), :],
+            weights.at[pl.ds(quarter * share, share), pl.ds((4 + quarters) * rows, quarters * rows), :],
             part_out,
             sems.at[2 * count + 1],
         ),
@@ -605,10 +601,10 @@
     store_blocks(keep, send, total_in[...], 0, place[0], 0, (1, 2))
 
 
-def pack(attn_in, attn_out, rel_proj, ff_in, ff_out, shard):
+def pack(attn_in, attn_out, ff_in, ff_out, shard):
     rows, width = attn_out.shape
     start = 0
-    for value in (attn_in, attn_out, rel_proj, ff_in):
+    for value in (attn_in, attn_out, ff_in):
         for column in range(0, value.shape[1], width):
             shard[start : start + rows, :] = low(value[:, column : column + width])
             start += rows
@@ -784,14 +780,14 @@
     (shard,) = call(
         pack,
         "pack",
-        [VMEM] * 5,
-        [(((5 + 2 * quarters) * rows, width), BF)],
+        [VMEM] * 4,
+        [(((4 + 2 * quarters) * rows, width), BF)],
         [],
         0,
         1000,
-        (attn_in[0], attn_out[0], rel_proj[0], ff_in[0], ff_out[0]),
-    )
-    low_ff_out = shard[(5 + quarters) * rows :]
+        (attn_in[0], attn_out[0], ff_in[0], ff_out[0]),
+    )
+    low_ff_out = shard[(4 + quarters) * rows :]
     weights = gather(shard)
 
     def part(start, count=1):
@@ -816,6 +812,14 @@
     past = jnp.concatenate([compressed, memory], 1).astype(F32)
     past_normed = low(normalise(past)[0] * gain_one + bias_one)
     rev = jnp.pad(sinusoid(key_len, width), ((0, WIDE - key_len), (0, 0)))
+    rel_cols = low(rel_proj[0]).reshape(rows, size, rows).transpose(1, 0, 2)
+    rel_cols = lax.all_to_all(rel_cols, "stream", 0, 0, tiled=True).reshape(width, rows)
+    rel = low(lax.dot_general(rel_cols, rev, (((0,), (1,)), ((), ())), preferred_element_type=F32))[None]
+    spread = order[::-1]
+    for bit in spread:
+        rel = jnp.concatenate([rel, lax.ppermute(rel, "stream", xor_pairs(size, bit))], 0)
+    apart = jnp.arange(size, dtype=me.dtype) ^ me
+    rel = rel[sum(((apart // bit) % 2) << index for index, bit in enumerate(spread))].reshape(width, WIDE)
     keys = jnp.pad(doc_ids, ((0, 0), (0, WIDE - key_len)), constant_values=-1)
     allowed = (jnp.arange(WIDE)[None, :] <= jnp.arange(seg_len)[:, None] + past_len) & (
         keys[:, None, :] == doc_ids[:, past_len:, None]
@@ -837,6 +841,7 @@
     kv_old = ((micro, past_len, 2 * width), BF)
     kv_tok = ((micro, seg_len, 2 * width), BF)
     rel_all = ((WIDE, width), BF)
+    rel_turned = ((width, WIDE), BF)
     prob_all = ((micro, HEADS, seg_len, WIDE), BF)
     pre_all_shape = ((quarters, ROWS, width), F32)
 
@@ -844,23 +849,23 @@
     flat_cot = cot_out.reshape(-1, width)
     side = cot_comp.reshape(micro * CNEW, width)
     side_pad = jnp.pad(side, ((0, -side_rows % 16), (0, 0)))
-    kv_past, rel, output, early = call(
+    kv_past, output, early = call(
         stage_one,
         "first_forward",
         [SMEM, HBM] + [VMEM] * 8,
-        [kv_old, rel_all, flat_low, ((ROWS + side_pad.shape[0], width), BF)],
-        [in_scratch, mat_scratch, mat_scratch, ff_in_scratch, ff_out_scratch, kv_all, rel_all] + [flat_low] * 4,
-        7 + 2 * quarters,
+        [kv_old, flat_low, ((ROWS + side_pad.shape[0], width), BF)],
+        [in_scratch, mat_scratch, ff_in_scratch, ff_out_scratch, kv_all] + [flat_low] * 4,
+        5 + 2 * quarters,
         7_000_000_000,
-        (place, weights, past_normed, rev, flat_tokens, vec, bias_rows, mask, flat_cot, side_pad),
+        (place, weights, past_normed, rel, flat_tokens, vec, bias_rows, mask, flat_cot, side_pad),
         (squeezed,),
-        in_hbm=2,
+        in_hbm=1,
     )
     early = gather(early)
     received = lax.ppermute(output, "section", [(0, 1)])
     quarter_cols = width // my_hidden
     mine_in = lax.dynamic_slice(
-        weights, (0, (5 + me // quarter_cols) * rows, (me % quarter_cols) * my_hidden), (size, rows, my_hidden)
+        weights, (0, (4 + me // quarter_cols) * rows, (me % quarter_cols) * my_hidden), (size, rows, my_hidden)
     )
     (probs, pre, entry, normed, q_content, q_position, kv_own, mixed, middle, normed_two, grad_low) = call(
         stage_two,
@@ -868,7 +873,7 @@
         [SMEM] + [HBM] * 3 + [VMEM] * 6,
         [prob_all, pre_all_shape, flat_low, flat_low, flat_low, flat_low, kv_tok, flat_low, flat_wide,
          flat_low, flat_low],
-        [in_scratch, mat_scratch, ff_in_scratch, ff_out_scratch, kv_all, rel_all, prob_all, pre_all_shape, flat_low,
+        [in_scratch, mat_scratch, ff_in_scratch, ff_out_scratch, kv_all, rel_turned, prob_all, pre_all_shape, flat_low,
          flat_low, flat_low, kv_tok],
         8 + 2 * quarters,
         7_000_000_000,
@@ -888,7 +893,7 @@
         "shared_gradients",
         [SMEM] + [HBM] * 8 + [VMEM] * 8,
         [kv_all] + [part_shape] * 4 + [flat_low, flat_wide, ((8, width), F32)],
-        [mat_scratch, ff_in_scratch, ff_out_scratch, pre_all_shape, kv_all, rel_all, prob_all,
+        [mat_scratch, ff_in_scratch, ff_out_scratch, pre_all_shape, kv_all, rel_turned, prob_all,
          ((micro, WIDE, width), BF), rel_all, kv_all, flat_low, flat_low, flat_low, rel_all,
          ((2, 2, half, rows, wide), BF)],
         24 + 2 * quarters,

time: 379 us -> 375 us (0.989)
  waiting for transfers between devices: 137 us -> 110 us
  local copies, waits for them, and re-layouts: 23.6 us -> 41.5 us
  blocking collectives: 29 us -> 22.3 us
  starting transfers between devices: 28.9 us -> 35.2 us
  other arithmetic: 13.8 us -> 18.4 us
    all_gather x3, waiting for transfers between devices: 59.9 us -> 16.1 us  [gather(): return lax.all_gather(shard, 'stream', axis=0, tiled=False)]
    all_to_all x1, waiting for transfers between devices: 0.01 us -> 10.9 us  [per_device(): windows = lax.all_to_all(windows, 'stream', 0, 0, tiled=True)]
    ppermute x0 -> x4, waiting for transfers between devices: none -> 10.4 us  [per_device(): lax.ppermute(rel, 'stream', xor_pairs(size, bit))]
    all_to_all x0 -> x1, starting transfers between devices: none -> 7.52 us  [per_device(): lax.all_to_all(rel_cols, 'stream', 0, 0, tiled=True).reshape(width, rows)]
    all_gather x1, blocking collectives: 29 us -> 22.3 us  [gather(): return lax.all_gather(shard, 'stream', axis=0, tiled=False)]
    ppermute x12, waiting for transfers between devices: 61.1 us -> 55.8 us  [move(): lax.ppermute(self.send, 'stream', xor_pairs(lax.axis_size('stream'), bit))]
    unnamed x59 -> x78, local copies, waits for them, and re-layouts: 5.52 us -> 10.1 us
    all_to_all x1, starting transfers between devices: 7.39 us -> 3.56 us  [per_device(): windows = lax.all_to_all(windows, 'stream', 0, 0, tiled=True)]
  transfers between devices with their start and end apart: 21 -> 26, of which waited for: 11 -> 14; matrix products, arithmetic and copies ran while one was open for 10% -> 17% of each run, Pallas kernels for 26% -> 27%
where the time goes in v6:
time: 375 us; the launch traced here: 369 us
  Pallas kernels  121 us (32%)
  waiting for transfers between devices  110 us (29%)
  local copies, waits for them, and re-layouts  41.5 us (11%)
  starting transfers between devices  35.2 us (9%)
  blocking collectives  22.3 us (6%)
  other arithmetic  18.4 us (5%)
  between operations  14.9 us (4%)
  matrix products  6.62 us (2%)
    pallas_call x7, Pallas kernels, call(): pl.pallas_call(kernel, name=name, in_specs=in_specs + [HBM] * len(after),...  109 us
    ppermute x12, waiting for transfers between devices, move(): lax.ppermute(self.send, 'stream', xor_pairs(lax.axis_size('stream'), bit))  55.8 us
    all_gather x1, blocking collectives, gather(): return lax.all_gather(shard, 'stream', axis=0, tiled=False)  22.3 us
    all_gather x3, waiting for transfers between devices, gather(): return lax.all_gather(shard, 'stream', axis=0, tiled=False)  16.1 us
    pallas_call x9, Pallas kernels, add_halves(): pl.pallas_call(kernel, name='add_halves', grid=(half,), in_specs=specs +...  11.9 us
    all_to_all x1, waiting for transfers between devices, per_device(): windows = lax.all_to_all(windows, 'stream', 0, 0, tiled=True)  10.9 us
    ppermute x4, waiting for transfers between devices, per_device(): lax.ppermute(rel, 'stream', xor_pairs(size, bit))  10.4 us
    unnamed x78, local copies, waits for them, and re-layouts  10.1 us
  transfers between devices with their start and end apart: 26, of which 14 were waited for; matrix products, arithmetic and copies ran while one was open for 17% of the time, Pallas kernels for 27%

profile of v6, /device:TPU:0, one launch (start us, length us, event | category | flops | bytes accessed | tf_op | source)
XLA Modules:
  0.0 369.1 jit_solution(7479668951195829254)
XLA Ops:
  11.7 7.5 %all-to-all-start = ((bf16[16,2,2048]{2,1,0:T(2,128)(2,1)}), bf16[16,2,2048]{2,1,0:T(2,128)(2,1)S(1)}, u32[]{:S(2)}, u32[]{:S(2)}) async-start(bf16[16,2,2048]{2,1,0:T(2,128)(2,1)} %reshape.469), calls=%async_computation | async-start | bytes 262144 | tf_op jit(solution)/shard_map/all_to_all | solution.py:816
  19.4 22.3 %all-gather.4 = bf16[16,12,64]{2,1,0:T(8,128)(2,1)S(1)} all-gather(bf16[1,12,64]{2,1,0:T(8,128)(2,1)S(1)} %maximum_bitcast_fusion.1), channel_id=3, replica_groups=mesh['section'=2,'stream'=16] {'stream'}, dimensions={0}, use_global_device_ids=true | all-gather | bytes 26112 | tf_op jit(solution)/shard_map/all_gather | solution.py:734
  42.7 3.6 fusion.15
  50.1 3.6 all-to-all-start.1
  61.7 10.9 %all-to-all-done.1 = bf16[16,42,192]{2,1,0:T(8,128)(2,1)S(1)} async-done(((bf16[16,42,192]{2,1,0:T(8,128)(2,1)}), bf16[16,42,192]{2,1,0:T(8,128)(2,1)S(1)}, u32[]{:S(2)}, u32[]{:S(2)}) %all-to-all-start.1) | async-done | bytes 258080 | tf_op jit(solution)/shard_map/all_to_all | solution.py:798
  97.9 9.9 %collective-permute-done.2 = bf16[4,64,512]{2,1,0:T(8,128)(2,1)S(1)} collective-permute-done((bf16[4,64,512]{2,1,0:T(8,128)(2,1)S(1)}, bf16[4,64,512]{2,1,0:T(8,128)(2,1)S(1)}, u32[]{:S(2)}, u32[]{:S(2)}) %collective-permute-start.2) | collective-permute-done | bytes 262176 | tf_op jit(solution)/shard_map/ppermute | solution.py:820
  109.4 14.9 %collective-permute-done.5.refs_2_.refs_3_ = bf16[4,48,1024]{2,1,0:T(8,128)(2,1)S(1)} collective-permute-done((bf16[4,48,1024]{2,1,0:T(8,128)(2,1)S(1)}, bf16[4,48,1024]{2,1,0:T(8,128)(2,1)S(1)}, u32[]{:S(2)}, u32[]{:S(2)}) %collective-permute-start.5) | collective-permute-done | bytes 393248 | tf_op jit(solution)/shard_map/ppermute | solution.py:710
  125.9 10.0 %collective-permute-done.6.refs_2_.refs_3_ = bf16[2,48,1024]{2,1,0:T(8,128)(2,1)S(1)} collective-permute-done((bf16[2,48,1024]{2,1,0:T(8,128)(2,1)S(1)}, bf16[2,48,1024]{2,1,0:T(8,128)(2,1)S(1)}, u32[]{:S(2)}, u32[]{:S(2)}) %collective-permute-start.6) | collective-permute-done | bytes 196640 | tf_op jit(solution)/shard_map/ppermute | solution.py:710
  139.7 5.5 %collective-permute-done.7 = bf16[1,48,1024]{2,1,0:T(8,128)(2,1)S(1)} collective-permute-done((bf16[1,48,1024]{2,1,0:T(8,128)(2,1)S(1)}, bf16[1,48,1024]{2,1,0:T(8,128)(2,1)S(1)}, u32[]{:S(2)}, u32[]{:S(2)}) %collective-permute-start.7) | collective-permute-done | bytes 98336 | tf_op jit(solution)/shard_map/ppermute | solution.py:710
  145.9 16.1 %all-gather.9.cloned.1.call-done = bf16[12288,1024]{1,0:T(8,128)(2,1)} async-done(((bf16[768,1024]{1,0:T(8,128)(2,1)}), bf16[12288,1024]{1,0:T(8,128)(2,1)}) %all-gather.9.cloned.1.call-update) | async-done | bytes 25165840 | tf_op jit(solution)/shard_map/all_gather | solution.py:734
  162.0 15.7 %first_forward.1 = (bf16[2,384,2048]{2,1,0:T(8,128)(2,1)}, bf16[128,1024]{1,0:T(8,128)(2,1)}, bf16[176,1024]{1,0:T(8,128)(2,1)}) custom-call(s32[2]{0:T(128)} %pad_add_fusion.refs_0_, bf16[16,768,1024]{2,1,0:T(8,128)(2,1)} %bitcast.93, bf16[2,384,1024]{2,1,0:T(8,128)(2,1)} %fusion.5.refs_2_.refs_7_, bf16[1024,512]{1,0:T(8,128)(2,1)} %bitcast.99, ...), custom_call_target="tpu_custom_call" | custom-call | flops 7000000 | bytes 100000 | tf_op jit(solution)/shard_map/first_forward/pallas_call | solution.py:641
  177.8 3.9 %collective-permute-start.8 = (bf16[128,1024]{1,0:T(8,128)(2,1)}, bf16[128,1024]{1,0:T(8,128)(2,1)S(1)}, u32[]{:S(2)}, u32[]{:S(2)}) collective-permute-start(bf16[128,1024]{1,0:T(8,128)(2,1)} %get-tuple-element.73), channel_id=1, source_target_pairs={{0,16},{1,17},{2,18},{3,19},{4,20},{5,21},{6,22},{7,23},{8,24},{9,... | collective-permute-start | bytes 786440 | tf_op jit(solution)/shard_map/ppermute | solution.py:865
  183.6 3.9 %collective-permute-done.8.refs_5_ = bf16[128,1024]{1,0:T(8,128)(2,1)S(1)} collective-permute-done((bf16[128,1024]{1,0:T(8,128)(2,1)}, bf16[128,1024]{1,0:T(8,128)(2,1)S(1)}, u32[]{:S(2)}, u32[]{:S(2)}) %collective-permute-start.8) | collective-permute-done | bytes 262176 | tf_op jit(solution)/shard_map/ppermute | solution.py:865
  188.2 25.8 %second_forward_and_back.1 = (bf16[2,8,64,512]{3,2,1,0:T(8,128)(2,1)}, f32[4,128,1024]{2,1,0:T(8,128)}, bf16[128,1024]{1,0:T(8,128)(2,1)}, bf16[128,1024]{1,0:T(...) custom-call(s32[2]{0:T(128)} %pad_add_fusion.refs_0_, ...), custom_call_target="tpu_custom_call" | custom-call | flops 7000000 | bytes 100000 | tf_op jit(solution)/shard_map/second_forward_and_back/pallas_call | solution.py:641
  215.3 8.5 %collective-permute-done.9.refs_9_ = bf16[128,1024]{1,0:T(8,128)(2,1)S(1)} collective-permute-done((bf16[128,1024]{1,0:T(8,128)(2,1)}, bf16[128,1024]{1,0:T(8,128)(2,1)S(1)}, u32[]{:S(2)}, u32[]{:S(2)}) %collective-permute-start.9) | collective-permute-done | bytes 262176 | tf_op jit(solution)/shard_map/ppermute | solution.py:884
  224.7 25.8 %shared_gradients.1 = (bf16[2,512,2048]{2,1,0:T(8,128)(2,1)}, bf16[8,64,2560]{2,1,0:T(8,128)(2,1)}, bf16[8,64,2560]{2,1,0:T(8,128)(2,1)}, bf16[8,64,2560]{2,1,0:...) custom-call(s32[2]{0:T(128)} %pad_add_fusion.refs_0_, ...), custom_call_target="tpu_custom_call" | custom-call | flops 7000000 | bytes 100000 | tf_op jit(solution)/shard_map/shared_gradients/pallas_call | solution.py:641
  257.0 4.0 %add_halves.13 = (bf16[4,64,2560]{2,1,0:T(8,128)(2,1)S(1)}, bf16[4,64,2560]{2,1,0:T(8,128)(2,1)}) custom-call(bf16[8,64,2560]{2,1,0:T(8,128)(2,1)S(1)} %copy-done.1, bf16[8,64,2560]{2,1,0:T(8,128)(2,1)S(1)} %copy-done.1, bf16[8,64,2560]{2,1,0:T(8,128)(2,1)} %collective-permute-done.11.refs_2_.refs_3_, ...), custom_call_target="tpu_custom_call" | custom-call | flops 1000 | bytes 100000 | tf_op jit(solution)/shard_map/add_halves/pallas_call | solution.py:678
  262.1 4.0 %add_halves.12 = (bf16[4,64,2560]{2,1,0:T(8,128)(2,1)S(1)}, bf16[4,64,2560]{2,1,0:T(8,128)(2,1)}) custom-call(bf16[8,64,2560]{2,1,0:T(8,128)(2,1)S(1)} %copy-done, bf16[8,64,2560]{2,1,0:T(8,128)(2,1)S(1)} %copy-done, bf16[8,64,2560]{2,1,0:T(8,128)(2,1)} %collective-permute-done.10.refs_2_.refs_3_, bf16[8,64,2560]{2,1,0:T(8,128)(2,1)} %collective-permute-done.10.refs_2_.refs_3_), custom_call_target="tpu_custom_call" | custom-call | flops 1000 | bytes 100000 | tf_op jit(solution)/shard_map/add_halves/pallas_call | solution.py:678
  268.4 14.8 %entry_gradient.1 = (bf16[2,256,1024]{2,1,0:T(8,128)(2,1)}, f32[128,1024]{1,0:T(8,128)}, f32[2,1024]{1,0:T(2,128)}, bf16[128,1024]{1,0:T(8,128)(2,1)}) custom-call(bf16[16,768,1024]{2,1,0:T(8,128)(2,1)} %bitcast.97, bf16[2,512,2048]{2,1,0:T(8,128)(2,1)} %get-tuple-element.83.refs_1_, f32[4,128,1024]{2,1,0:T(8,128)} %get-tuple-element.76.refs_6_.refs_2_, ...), custom_call_target="tpu_custom_call" | custom-call | flops 15000000512 | bytes 100000 | tf_op jit(solution)/shard_map/entry_gradient/pallas_call | solution.py:641
  285.0 6.3 %all-to-all-start.2 = ((f32[16,1,512]{2,1,0:T(1,128)}), f32[16,1,512]{2,1,0:T(1,128)S(1)}, u32[]{:S(2)}, u32[]{:S(2)}) async-start(f32[16,1,512]{2,1,0:T(1,128)} %reshape.471), calls=%async_computation.2 | async-start | bytes 65536 | tf_op jit(solution)/shard_map/all_to_all | solution.py:960
  291.3 14.7 %collective-permute-done.12.refs_2_.refs_3_ = bf16[4,64,2560]{2,1,0:T(8,128)(2,1)} collective-permute-done((bf16[4,64,2560]{2,1,0:T(8,128)(2,1)}, bf16[4,64,2560]{2,1,0:T(8,128)(2,1)}, u32[]{:S(2)}, u32[]{:S(2)}) %collective-permute-start.12) | collective-permute-done | bytes 1310752 | tf_op jit(solution)/shard_map/ppermute | solution.py:710
  313.8 20.4 %hidden_gradients.1 = (bf16[2,64,1024]{2,1,0:T(8,128)(2,1)}, bf16[2,64,1024]{2,1,0:T(8,128)(2,1)}, f32[256,1024]{1,0:T(8,128)}, f32[1,256]{1,0:T(1,128)}) custom-call(s32[2]{0:T(128)} %pad_add_fusion.refs_0_, bf16[16,768,1024]{2,1,0:T(8,128)(2,1)} %bitcast.98, bf16[16,176,1024]{2,1,0:T(8,128)(2,1)} %bitcast.128, bf16[16,128,1024]{2,1,0:T(8,128)(2,1)} %bitcast.130, ...), custom_call_target="tpu_custom_call" | custom-call | flops 20000000000 | bytes 100000 | tf_op jit(solution)/shard_map/hidden_gradients/pallas_call | solution.py:641
  345.2 3.9 %collective-permute-done.19.refs_7_ = bf16[2,64,1024]{2,1,0:T(8,128)(2,1)S(1)} collective-permute-done((bf16[2,64,1024]{2,1,0:T(8,128)(2,1)S(1)}, bf16[2,64,1024]{2,1,0:T(8,128)(2,1)S(1)}, u32[]{:S(2)}, u32[]{:S(2)}) %collective-permute-start.19) | collective-permute-done | bytes 262176 | tf_op jit(solution)/shard_map/ppermute | solution.py:955
  349.1 6.6 %collective-permute-done.17.refs_4_ = bf16[1,64,2560]{2,1,0:T(8,128)(2,1)S(1)} collective-permute-done((bf16[1,64,2560]{2,1,0:T(8,128)(2,1)S(1)}, bf16[1,64,2560]{2,1,0:T(8,128)(2,1)S(1)}, u32[]{:S(2)}, u32[]{:S(2)}) %collective-permute-start.17) | collective-permute-done | bytes 327712 | tf_op jit(solution)/shard_map/ppermute | solution.py:710
  (213 shorter events, 91.5 us)
Async XLA Ops:
  7.2 154.8 %all-gather.9.cloned.1.call-start = ((), (), s32[]{:S(2)}) async-start(), calls=%async_computation.3 | async-start | bytes 26738688 | tf_op jit(solution)/shard_map/all_gather | solution.py:734
  11.7 38.5 %all-to-all-start = ((bf16[16,2,2048]{2,1,0:T(2,128)(2,1)}), bf16[16,2,2048]{2,1,0:T(2,128)(2,1)S(1)}, u32[]{:S(2)}, u32[]{:S(2)}) async-start(bf16[16,2,2048]{2,1,0:T(2,128)(2,1)} %reshape.469), calls=%async_computation | async-start | bytes 262144 | tf_op jit(solution)/shard_map/all_to_all | solution.py:816
  50.1 22.5 %all-to-all-start.1 = ((bf16[16,42,192]{2,1,0:T(8,128)(2,1)}), bf16[16,42,192]{2,1,0:T(8,128)(2,1)S(1)}, u32[]{:S(2)}, u32[]{:S(2)}) async-start(bf16[16,42,192]{2,1,0:T(8,128)(2,1)} %bitcast.92), calls=%async_computation.1 | async-start | bytes 786432 | tf_op jit(solution)/shard_map/all_to_all | solution.py:798
  53.7 213.5 %all-gather.11.cloned.1.call-start = ((), (), s32[]{:S(2)}) async-start(), calls=%async_computation.4 | async-start | bytes 6127616 | tf_op jit(solution)/shard_map/all_gather | solution.py:734
  59.0 24.1 %collective-permute-start = (bf16[1,64,512]{2,1,0:T(8,128)(2,1)S(1)}, bf16[1,64,512]{2,1,0:T(8,128)(2,1)S(1)}, u32[]{:S(2)}, u32[]{:S(2)}) collective-permute-start(bf16[1,64,512]{2,1,0:T(8,128)(2,1)S(1)} %get-tuple-element.136), channel_id=1, source_target_pairs={{0,8},{1,9},{2,10},{3,11},{4,12},{5,13},{6,14},{7,15},{8,0},{9,1},... | collective-permute-start | bytes 196616 | tf_op jit(solution)/shard_map/ppermute | solution.py:820
  82.5 13.0 %collective-permute-start.4 = (bf16[8,48,1024]{2,1,0:T(8,128)(2,1)}, bf16[8,48,1024]{2,1,0:T(8,128)(2,1)S(1)}, u32[]{:S(2)}, u32[]{:S(2)}) collective-permute-start(bf16[8,48,1024]{2,1,0:T(8,128)(2,1)} %get-tuple-element.123), channel_id=1, source_target_pairs={{0,1},{1,0},{2,3},{3,2},{4,5},{5,4},{6,7},{7,6},{8,9},{9,8},{10,11... | collective-permute-start | bytes 2359304 | tf_op jit(solution)/shard_map/ppermute | solution.py:710
  83.7 9.2 %collective-permute-start.1 = (bf16[2,64,512]{2,1,0:T(8,128)(2,1)}, bf16[2,64,512]{2,1,0:T(8,128)(2,1)S(1)}, u32[]{:S(2)}, u32[]{:S(2)}) collective-permute-start(bf16[2,64,512]{2,1,0:T(8,128)(2,1)} %pad_maximum_fusion.4), channel_id=1, source_target_pairs={{0,4},{1,5},{2,6},{3,7},{4,0},{5,1},{6,2},{7,3},{8,12},{9,13},{10,... | collective-permute-start | bytes 393224 | tf_op jit(solution)/shard_map/ppermute | solution.py:820
  92.9 14.8 %collective-permute-start.2 = (bf16[4,64,512]{2,1,0:T(8,128)(2,1)S(1)}, bf16[4,64,512]{2,1,0:T(8,128)(2,1)S(1)}, u32[]{:S(2)}, u32[]{:S(2)}) collective-permute-start(bf16[4,64,512]{2,1,0:T(8,128)(2,1)S(1)} %pad_maximum_fusion.2), channel_id=1, source_target_pairs={{0,2},{1,3},{2,0},{3,1},{4,6},{5,7},{6,4},{7,5},{8,10},{9,11},{10,... | collective-permute-start | bytes 786440 | tf_op jit(solution)/shard_map/ppermute | solution.py:820
  95.8 28.5 %collective-permute-start.5 = (bf16[4,48,1024]{2,1,0:T(8,128)(2,1)S(1)}, bf16[4,48,1024]{2,1,0:T(8,128)(2,1)S(1)}, u32[]{:S(2)}, u32[]{:S(2)}) collective-permute-start(bf16[4,48,1024]{2,1,0:T(8,128)(2,1)S(1)} %get-tuple-element.67), channel_id=1, source_target_pairs={{0,2},{1,3},{2,0},{3,1},{4,6},{5,7},{6,4},{7,5},{8,10},{9,11},{10,... | collective-permute-start | bytes 1179656 | tf_op jit(solution)/shard_map/ppermute | solution.py:710
  107.8 28.2 %collective-permute-start.3 = (bf16[8,64,512]{2,1,0:T(8,128)(2,1)S(1)}, bf16[8,64,512]{2,1,0:T(8,128)(2,1)S(1)}, u32[]{:S(2)}, u32[]{:S(2)}) collective-permute-start(bf16[8,64,512]{2,1,0:T(8,128)(2,1)S(1)} %pad_maximum_fusion.1), channel_id=1, source_target_pairs={{0,1},{1,0},{2,3},{3,2},{4,5},{5,4},{6,7},{7,6},{8,9},{9,8},{10,11... | collective-permute-start | bytes 1572872 | tf_op jit(solution)/shard_map/ppermute | solution.py:820
  124.4 11.4 %collective-permute-start.6 = (bf16[2,48,1024]{2,1,0:T(8,128)(2,1)S(1)}, bf16[2,48,1024]{2,1,0:T(8,128)(2,1)S(1)}, u32[]{:S(2)}, u32[]{:S(2)}) collective-permute-start(bf16[2,48,1024]{2,1,0:T(8,128)(2,1)S(1)} %get-tuple-element.69), channel_id=1, source_target_pairs={{0,4},{1,5},{2,6},{3,7},{4,0},{5,1},{6,2},{7,3},{8,12},{9,13},{10,... | collective-permute-start | bytes 589832 | tf_op jit(solution)/shard_map/ppermute | solution.py:710
  135.9 9.3 %collective-permute-start.7 = (bf16[1,48,1024]{2,1,0:T(8,128)(2,1)S(1)}, bf16[1,48,1024]{2,1,0:T(8,128)(2,1)S(1)}, u32[]{:S(2)}, u32[]{:S(2)}) collective-permute-start(bf16[1,48,1024]{2,1,0:T(8,128)(2,1)S(1)} %get-tuple-element.71), channel_id=1, source_target_pairs={{0,8},{1,9},{2,10},{3,11},{4,12},{5,13},{6,14},{7,15},{8,0},{9,1},... | collective-permute-start | bytes 294920 | tf_op jit(solution)/shard_map/ppermute | solution.py:710
  177.7 136.1 %all-gather.13.cloned.1.call-start = ((), (), s32[]{:S(2)}) async-start(), calls=%async_computation.5 | async-start | bytes 4456448 | tf_op jit(solution)/shard_map/all_gather | solution.py:734
  177.8 9.7 %collective-permute-start.8 = (bf16[128,1024]{1,0:T(8,128)(2,1)}, bf16[128,1024]{1,0:T(8,128)(2,1)S(1)}, u32[]{:S(2)}, u32[]{:S(2)}) collective-permute-start(bf16[128,1024]{1,0:T(8,128)(2,1)} %get-tuple-element.73), channel_id=1, source_target_pairs={{0,16},{1,17},{2,18},{3,19},{4,20},{5,21},{6,22},{7,23},{8,24},{9,... | collective-permute-start | bytes 786440 | tf_op jit(solution)/shard_map/ppermute | solution.py:865
  214.0 9.8 %collective-permute-start.9 = (bf16[128,1024]{1,0:T(8,128)(2,1)}, bf16[128,1024]{1,0:T(8,128)(2,1)S(1)}, u32[]{:S(2)}, u32[]{:S(2)}) collective-permute-start(bf16[128,1024]{1,0:T(8,128)(2,1)} %get-tuple-element.77), channel_id=1, source_target_pairs={{16,0},{17,1},{18,2},{19,3},{20,4},{21,5},{22,6},{23,7},{24,8},{25... | collective-permute-start | bytes 786440 | tf_op jit(solution)/shard_map/ppermute | solution.py:884
  250.6 11.6 %collective-permute-start.10 = (bf16[8,64,2560]{2,1,0:T(8,128)(2,1)}, bf16[8,64,2560]{2,1,0:T(8,128)(2,1)}, u32[]{:S(2)}, u32[]{:S(2)}) collective-permute-start(bf16[8,64,2560]{2,1,0:T(8,128)(2,1)} %get-tuple-element.88), channel_id=1, source_target_pairs={{0,1},{1,0},{2,3},{3,2},{4,5},{5,4},{6,7},{7,6},{8,9},{9,8},{10,11... | collective-permute-start | bytes 7864328 | tf_op jit(solution)/shard_map/ppermute | solution.py:710
  262.1 48.3 %collective-permute-start.14 = (bf16[4,64,2560]{2,1,0:T(8,128)(2,1)}, bf16[4,64,2560]{2,1,0:T(8,128)(2,1)S(1)}, u32[]{:S(2)}, u32[]{:S(2)}) collective-permute-start(bf16[4,64,2560]{2,1,0:T(8,128)(2,1)} %get-tuple-element.92.refs_11_), channel_id=1, source_target_pairs={{0,4},{1,5},{2,6},{3,7},{4,0},{5,1},{6,2},{7,3},{8,12},{9,13},{10,... | collective-permute-start | bytes 3932168 | tf_op jit(solution)/shard_map/ppermute | solution.py:710
  266.1 39.9 %collective-permute-start.12 = (bf16[4,64,2560]{2,1,0:T(8,128)(2,1)}, bf16[4,64,2560]{2,1,0:T(8,128)(2,1)}, u32[]{:S(2)}, u32[]{:S(2)}) collective-permute-start(bf16[4,64,2560]{2,1,0:T(8,128)(2,1)} %get-tuple-element.89.refs_10_), channel_id=1, source_target_pairs={{0,2},{1,3},{2,0},{3,1},{4,6},{5,7},{6,4},{7,5},{8,10},{9,11},{10,... | collective-permute-start | bytes 3932168 | tf_op jit(solution)/shard_map/ppermute | solution.py:710
  285.0 52.8 %all-to-all-start.2 = ((f32[16,1,512]{2,1,0:T(1,128)}), f32[16,1,512]{2,1,0:T(1,128)S(1)}, u32[]{:S(2)}, u32[]{:S(2)}) async-start(f32[16,1,512]{2,1,0:T(1,128)} %reshape.471), calls=%async_computation.2 | async-start | bytes 65536 | tf_op jit(solution)/shard_map/all_to_all | solution.py:960
  308.9 31.6 %collective-permute-start.13 = (bf16[2,64,2560]{2,1,0:T(8,128)(2,1)}, bf16[2,64,2560]{2,1,0:T(8,128)(2,1)S(1)}, u32[]{:S(2)}, u32[]{:S(2)}) collective-permute-start(bf16[2,64,2560]{2,1,0:T(8,128)(2,1)} %get-tuple-element.100.refs_8_), channel_id=1, source_target_pairs={{0,4},{1,5},{2,6},{3,7},{4,0},{5,1},{6,2},{7,3},{8,12},{9,13},{10,... | collective-permute-start | bytes 1966088 | tf_op jit(solution)/shard_map/ppermute | solution.py:710
  311.4 31.1 %collective-permute-start.16 = (bf16[2,64,2560]{2,1,0:T(8,128)(2,1)}, bf16[2,64,2560]{2,1,0:T(8,128)(2,1)S(1)}, u32[]{:S(2)}, u32[]{:S(2)}) collective-permute-start(bf16[2,64,2560]{2,1,0:T(8,128)(2,1)} %get-tuple-element.103.refs_9_), channel_id=1, source_target_pairs={{0,8},{1,9},{2,10},{3,11},{4,12},{5,13},{6,14},{7,15},{8,0},{9,1},... | collective-permute-start | bytes 1966088 | tf_op jit(solution)/shard_map/ppermute | solution.py:710
  339.9 9.2 %collective-permute-start.19 = (bf16[2,64,1024]{2,1,0:T(8,128)(2,1)S(1)}, bf16[2,64,1024]{2,1,0:T(8,128)(2,1)S(1)}, u32[]{:S(2)}, u32[]{:S(2)}) collective-permute-start(bf16[2,64,1024]{2,1,0:T(8,128)(2,1)S(1)} %pad_maximum_fusion.3), channel_id=1, source_target_pairs={{0,2},{1,3},{2,0},{3,1},{4,6},{5,7},{6,4},{7,5},{8,10},{9,11},{10,... | collective-permute-start | bytes 786440 | tf_op jit(solution)/shard_map/ppermute | solution.py:955
  340.7 17.8 %collective-permute-start.15 = (bf16[1,64,2560]{2,1,0:T(8,128)(2,1)S(1)}, bf16[1,64,2560]{2,1,0:T(8,128)(2,1)S(1)}, u32[]{:S(2)}, u32[]{:S(2)}) collective-permute-start(bf16[1,64,2560]{2,1,0:T(8,128)(2,1)S(1)} %get-tuple-element.106.refs_4_), channel_id=1, source_target_pairs={{0,8},{1,9},{2,10},{3,11},{4,12},{5,13},{6,14},{7,15},{8,0},{9,1},... | collective-permute-start | bytes 983048 | tf_op jit(solution)/shard_map/ppermute | solution.py:710
  343.4 12.2 %collective-permute-start.17 = (bf16[1,64,2560]{2,1,0:T(8,128)(2,1)S(1)}, bf16[1,64,2560]{2,1,0:T(8,128)(2,1)S(1)}, u32[]{:S(2)}, u32[]{:S(2)}) collective-permute-start(bf16[1,64,2560]{2,1,0:T(8,128)(2,1)S(1)} %get-tuple-element.109), channel_id=1, source_target_pairs={{0,2},{1,3},{2,0},{3,1},{4,6},{5,7},{6,4},{7,5},{8,10},{9,11},{10,... | collective-permute-start | bytes 983048 | tf_op jit(solution)/shard_map/ppermute | solution.py:710
  (39 other events, 393.0 us)
Sparse Core Ops, SparseCore 0:
  10.7 151.2 all-gather.8
  177.9 59.0 all-gather.10
  239.1 59.7 all-gather.12

commit v7 on v6

--- a/solution.py
+++ b/solution.py
@@ -803,10 +803,7 @@
     partial = relative_order(partial, order)
     side_sum = Scatter(partial[: size // 2], partial[size // 2 :], order)
     side_sum.move()
-    while side_sum.order:
-        side_sum.add()
-        side_sum.move()
-    squeezed = low(side_sum.last()[:side_rows] + small[5])
+    side_sum.add()
     windows = windows.reshape(-1, comp_rows)
 
     past = jnp.concatenate([compressed, memory], 1).astype(F32)
@@ -858,11 +855,12 @@
         5 + 2 * quarters,
         7_000_000_000,
         (place, weights, past_normed, rel, flat_tokens, vec, bias_rows, mask, flat_cot, side_pad),
-        (squeezed,),
+        (side_sum.send, low_ff_out),
         in_hbm=1,
     )
     early = gather(early)
     received = lax.ppermute(output, "section", [(0, 1)])
+    side_sum.send = gate(side_sum.send, output)
     quarter_cols = width // my_hidden
     mine_in = lax.dynamic_slice(
         weights, (0, (4 + me // quarter_cols) * rows, (me % quarter_cols) * my_hidden), (size, rows, my_hidden)
@@ -881,7 +879,9 @@
         (mine_in,),
         in_hbm=2,
     )
-    returned = lax.ppermute(grad_low, "section", [(1, 0)])
+    side_sum.move()
+    returned = lax.ppermute(gate(grad_low, side_sum.got), "section", [(1, 0)])
+    side_sum.add()
     late = jnp.where(first, returned, normed_two)
     late = gather(late)
     half = size // 2
@@ -900,6 +900,7 @@
         7_000_000_000,
         (place, weights, kv_past, kv_own, rel, probs, pre, past_normed, rev, returned, flat_cot, vec, normed, q_content,
          q_position, mixed, middle),
+        (side_sum.send,),
         in_hbm=5,
     )
     one_sum, two_sum = Scatter(keep_one, send_one, order), Scatter(keep_two, send_two, other_order)
@@ -913,8 +914,12 @@
         two_sum.add(*after)
 
     move_both()
-    add_both()
+    side_sum.move()
+    one_sum.add(side_sum.got)
+    two_sum.add()
     move_both()
+    side_sum.add(two_sum.send)
+    side_sum.move()
     new_memory, grad_entry, more, output = call(
         stage_five,
         "entry_gradient",
@@ -977,7 +982,10 @@
     grad_entry = grad_entry.reshape(tokens.shape)
 
     activations = low(output).reshape(tokens.shape)
-    squeezed = squeezed.reshape(micro, CNEW, width)
+    while side_sum.order:
+        side_sum.add()
+        side_sum.move()
+    squeezed = low(side_sum.last()[:side_rows] + small[5]).reshape(micro, CNEW, width)
     new_compressed = jnp.concatenate([compressed[:, CNEW:], squeezed], 1)
     return tuple(
         value[None]

time: 375 us -> 375 us (level)
  starting transfers between devices: 35.2 us -> 40.8 us
  other arithmetic: 18.4 us -> 13 us
  Pallas kernels: 121 us -> 117 us
    all_gather x3, waiting for transfers between devices: 16.1 us -> 49 us  [gather(): return lax.all_gather(shard, 'stream', axis=0, tiled=False)]
    ppermute x12, waiting for transfers between devices: 55.8 us -> 24.1 us  [move(): lax.ppermute(self.send, 'stream', xor_pairs(lax.axis_size('stream'), bit))]
    ppermute x4, waiting for transfers between devices: 10.4 us -> 25.9 us  [per_device(): lax.ppermute(rel, 'stream', xor_pairs(size, bit))]
    all_to_all x1, waiting for transfers between devices: 10.9 us -> 0.01 us  [per_device(): windows = lax.all_to_all(windows, 'stream', 0, 0, tiled=True)]
    unnamed x78 -> x76, local copies, waits for them, and re-layouts: 10.1 us -> 17.2 us
    ppermute x12, starting transfers between devices: 8.94 us -> 14.4 us  [move(): lax.ppermute(self.send, 'stream', xor_pairs(lax.axis_size('stream'), bit))]
  transfers between devices with their start and end apart: 26 -> 26, of which waited for: 14 -> 13; matrix products, arithmetic and copies ran while one was open for 17% -> 13% of each run, Pallas kernels for 27% -> 26%
where the time goes in v7:
time: 375 us; the launch traced here: 369 us
  Pallas kernels  117 us (31%)
  waiting for transfers between devices  113 us (30%)
  local copies, waits for them, and re-layouts  42 us (11%)
  starting transfers between devices  40.8 us (11%)
  blocking collectives  22.3 us (6%)
  between operations  14.9 us (4%)
  other arithmetic  13 us (3%)
  matrix products  5.56 us (1%)
    pallas_call x7, Pallas kernels, call(): pl.pallas_call(kernel, name=name, in_specs=in_specs + [HBM] * len(after),...  109 us
    all_gather x3, waiting for transfers between devices, gather(): return lax.all_gather(shard, 'stream', axis=0, tiled=False)  49 us
    ppermute x4, waiting for transfers between devices, per_device(): lax.ppermute(rel, 'stream', xor_pairs(size, bit))  25.9 us
    ppermute x12, waiting for transfers between devices, move(): lax.ppermute(self.send, 'stream', xor_pairs(lax.axis_size('stream'), bit))  24.1 us
    all_gather x1, blocking collectives, gather(): return lax.all_gather(shard, 'stream', axis=0, tiled=False)  22.3 us
    unnamed x76, local copies, waits for them, and re-layouts  17.2 us
    ppermute x12, starting transfers between devices, move(): lax.ppermute(self.send, 'stream', xor_pairs(lax.axis_size('stream'), bit))  14.4 us
    pallas_call x9, Pallas kernels, add_halves(): pl.pallas_call(kernel, name='add_halves', grid=(half,), in_specs=specs +...  8.28 us
  transfers between devices with their start and end apart: 26, of which 13 were waited for; matrix products, arithmetic and copies ran while one was open for 13% of the time, Pallas kernels for 26%

profile of v7, /device:TPU:0, one launch (start us, length us, event | category | flops | bytes accessed | tf_op | source)
XLA Modules:
  0.0 369.0 jit_solution(14091736150293995899)
XLA Ops:
  11.7 7.4 %all-to-all-start = ((bf16[16,2,2048]{2,1,0:T(2,128)(2,1)}), bf16[16,2,2048]{2,1,0:T(2,128)(2,1)S(1)}, u32[]{:S(2)}, u32[]{:S(2)}) async-start(bf16[16,2,2048]{2,1,0:T(2,128)(2,1)} %reshape.469), calls=%async_computation | async-start | bytes 262144 | tf_op jit(solution)/shard_map/all_to_all | solution.py:813
  19.2 22.3 %all-gather.4 = bf16[16,12,64]{2,1,0:T(8,128)(2,1)S(1)} all-gather(bf16[1,12,64]{2,1,0:T(8,128)(2,1)S(1)} %maximum_bitcast_fusion.1), channel_id=3, replica_groups=mesh['section'=2,'stream'=16] {'stream'}, dimensions={0}, use_global_device_ids=true | all-gather | bytes 26112 | tf_op jit(solution)/shard_map/all_gather | solution.py:734
  43.4 3.6 fusion.15
  49.7 3.7 all-to-all-start.1
  57.9 16.6 %collective-permute-done = bf16[1,64,512]{2,1,0:T(8,128)(2,1)S(1)} collective-permute-done((bf16[1,64,512]{2,1,0:T(8,128)(2,1)S(1)}, bf16[1,64,512]{2,1,0:T(8,128)(2,1)S(1)}, u32[]{:S(2)}, u32[]{:S(2)}) %collective-permute-start) | collective-permute-done | bytes 65568 | tf_op jit(solution)/shard_map/ppermute | solution.py:817
  79.4 3.9 %collective-permute-done.1 = bf16[2,64,512]{2,1,0:T(8,128)(2,1)S(1)} collective-permute-done((bf16[2,64,512]{2,1,0:T(8,128)(2,1)S(1)}, bf16[2,64,512]{2,1,0:T(8,128)(2,1)S(1)}, u32[]{:S(2)}, u32[]{:S(2)}) %collective-permute-start.1) | collective-permute-done | bytes 131104 | tf_op jit(solution)/shard_map/ppermute | solution.py:817
  92.9 5.4 %collective-permute-done.2 = bf16[4,64,512]{2,1,0:T(8,128)(2,1)S(1)} collective-permute-done((bf16[4,64,512]{2,1,0:T(8,128)(2,1)}, bf16[4,64,512]{2,1,0:T(8,128)(2,1)S(1)}, u32[]{:S(2)}, u32[]{:S(2)}) %collective-permute-start.2) | collective-permute-done | bytes 262176 | tf_op jit(solution)/shard_map/ppermute | solution.py:817
  105.9 49.0 %all-gather.9.cloned.1.call-done = bf16[12288,1024]{1,0:T(8,128)(2,1)} async-done(((bf16[768,1024]{1,0:T(8,128)(2,1)}), bf16[12288,1024]{1,0:T(8,128)(2,1)}) %all-gather.9.cloned.1.call-update) | async-done | bytes 25165840 | tf_op jit(solution)/shard_map/all_gather | solution.py:734
  154.9 15.7 %first_forward.1 = (bf16[2,384,2048]{2,1,0:T(8,128)(2,1)}, bf16[128,1024]{1,0:T(8,128)(2,1)}, bf16[176,1024]{1,0:T(8,128)(2,1)}) custom-call(s32[2]{0:T(128)} %pad_add_fusion.refs_0_, bf16[16,768,1024]{2,1,0:T(8,128)(2,1)} %bitcast.93, bf16[2,384,1024]{2,1,0:T(8,128)(2,1)} %fusion.5.refs_2_.refs_7_, bf16[1024,512]{1,0:T(8,128)(2,1)} %bitcast.99, ...), custom_call_target="tpu_custom_call" | custom-call | flops 7000000 | bytes 100000 | tf_op jit(solution)/shard_map/first_forward/pallas_call | solution.py:641
  172.1 3.8 %collective-permute-start.5 = (bf16[128,1024]{1,0:T(8,128)(2,1)}, bf16[128,1024]{1,0:T(8,128)(2,1)S(1)}, u32[]{:S(2)}, u32[]{:S(2)}) collective-permute-start(bf16[128,1024]{1,0:T(8,128)(2,1)} %get-tuple-element.68.refs_1_), channel_id=1, source_target_pairs={{0,16},{1,17},{2,18},{3,19},{4,20},{5,21},{6,22},{7,23},{8,24},{9,... | collective-permute-start | bytes 786440 | tf_op jit(solution)/shard_map/ppermute | solution.py:862
  177.9 3.6 collective-permute-done.5.refs_5_
  182.2 25.9 %second_forward_and_back.1 = (bf16[2,8,64,512]{3,2,1,0:T(8,128)(2,1)}, f32[4,128,1024]{2,1,0:T(8,128)}, bf16[128,1024]{1,0:T(8,128)(2,1)}, bf16[128,1024]{1,0:T(...) custom-call(s32[2]{0:T(128)} %pad_add_fusion.refs_0_, ...), custom_call_target="tpu_custom_call" | custom-call | flops 7000000 | bytes 100000 | tf_op jit(solution)/shard_map/second_forward_and_back/pallas_call | solution.py:641
  210.1 8.2 %collective-permute-done.7.refs_9_ = bf16[128,1024]{1,0:T(8,128)(2,1)S(1)} collective-permute-done((bf16[128,1024]{1,0:T(8,128)(2,1)}, bf16[128,1024]{1,0:T(8,128)(2,1)S(1)}, u32[]{:S(2)}, u32[]{:S(2)}) %collective-permute-start.7) | collective-permute-done | bytes 262176 | tf_op jit(solution)/shard_map/ppermute | solution.py:883
  220.9 25.6 %shared_gradients.1 = (bf16[2,512,2048]{2,1,0:T(8,128)(2,1)}, bf16[8,64,2560]{2,1,0:T(8,128)(2,1)}, bf16[8,64,2560]{2,1,0:T(8,128)(2,1)}, bf16[8,64,2560]{2,1,0:...) custom-call(s32[2]{0:T(128)} %pad_add_fusion.refs_0_, ...), custom_call_target="tpu_custom_call" | custom-call | flops 7000000 | bytes 100000 | tf_op jit(solution)/shard_map/shared_gradients/pallas_call | solution.py:641
  259.3 3.3 collective-permute-start.11
  265.3 3.8 %add_halves.11 = (bf16[4,64,2560]{2,1,0:T(8,128)(2,1)S(1)}, bf16[4,64,2560]{2,1,0:T(8,128)(2,1)}) custom-call(bf16[8,64,2560]{2,1,0:T(8,128)(2,1)S(1)} %copy-done.1, bf16[8,64,2560]{2,1,0:T(8,128)(2,1)S(1)} %copy-done.1, bf16[8,64,2560]{2,1,0:T(8,128)(2,1)} %collective-permute-done.8.refs_2_.refs_3_, ...), custom_call_target="tpu_custom_call" | custom-call | flops 1000 | bytes 100000 | tf_op jit(solution)/shard_map/add_halves/pallas_call | solution.py:678
  269.4 3.4 collective-permute-done.11
  276.1 15.0 %entry_gradient.1 = (bf16[2,256,1024]{2,1,0:T(8,128)(2,1)}, f32[128,1024]{1,0:T(8,128)}, f32[2,1024]{1,0:T(2,128)}, bf16[128,1024]{1,0:T(8,128)(2,1)}) custom-call(bf16[16,768,1024]{2,1,0:T(8,128)(2,1)} %bitcast.97, bf16[2,512,2048]{2,1,0:T(8,128)(2,1)} %get-tuple-element.80.refs_1_, f32[4,128,1024]{2,1,0:T(8,128)} %get-tuple-element.71.refs_6_.refs_2_, ...), custom_call_target="tpu_custom_call" | custom-call | flops 15000000512 | bytes 100000 | tf_op jit(solution)/shard_map/entry_gradient/pallas_call | solution.py:641
  292.8 3.9 %all-to-all-start.2 = ((f32[16,1,512]{2,1,0:T(1,128)}), f32[16,1,512]{2,1,0:T(1,128)S(1)}, u32[]{:S(2)}, u32[]{:S(2)}) async-start(f32[16,1,512]{2,1,0:T(1,128)} %reshape.471), calls=%async_computation.2 | async-start | bytes 65536 | tf_op jit(solution)/shard_map/all_to_all | solution.py:965
  296.7 4.1 %collective-permute-done.12.refs_2_.refs_3_ = bf16[4,64,2560]{2,1,0:T(8,128)(2,1)} collective-permute-done((bf16[4,64,2560]{2,1,0:T(8,128)(2,1)}, bf16[4,64,2560]{2,1,0:T(8,128)(2,1)}, u32[]{:S(2)}, u32[]{:S(2)}) %collective-permute-start.12) | collective-permute-done | bytes 1310752 | tf_op jit(solution)/shard_map/ppermute | solution.py:710
  305.1 3.7 collective-permute-done.14.refs_2_.refs_3_
  312.0 20.4 %hidden_gradients.1 = (bf16[2,64,1024]{2,1,0:T(8,128)(2,1)}, bf16[2,64,1024]{2,1,0:T(8,128)(2,1)}, f32[256,1024]{1,0:T(8,128)}, f32[1,256]{1,0:T(1,128)}) custom-call(s32[2]{0:T(128)} %pad_add_fusion.refs_0_, bf16[16,768,1024]{2,1,0:T(8,128)(2,1)} %bitcast.98, bf16[16,176,1024]{2,1,0:T(8,128)(2,1)} %bitcast.128, bf16[16,128,1024]{2,1,0:T(8,128)(2,1)} %bitcast.130, ...), custom_call_target="tpu_custom_call" | custom-call | flops 20000000000 | bytes 100000 | tf_op jit(solution)/shard_map/hidden_gradients/pallas_call | solution.py:641
  347.3 6.6 %collective-permute-done.17.refs_4_ = bf16[1,64,2560]{2,1,0:T(8,128)(2,1)S(1)} collective-permute-done((bf16[1,64,2560]{2,1,0:T(8,128)(2,1)S(1)}, bf16[1,64,2560]{2,1,0:T(8,128)(2,1)S(1)}, u32[]{:S(2)}, u32[]{:S(2)}) %collective-permute-start.17) | collective-permute-done | bytes 327712 | tf_op jit(solution)/shard_map/ppermute | solution.py:710
  353.9 4.4 %collective-permute-done.15.refs_2_ = bf16[1,64,2560]{2,1,0:T(8,128)(2,1)S(1)} collective-permute-done((bf16[1,64,2560]{2,1,0:T(8,128)(2,1)S(1)}, bf16[1,64,2560]{2,1,0:T(8,128)(2,1)S(1)}, u32[]{:S(2)}, u32[]{:S(2)}) %collective-permute-start.15) | collective-permute-done | bytes 327712 | tf_op jit(solution)/shard_map/ppermute | solution.py:710
  (212 shorter events, 90.7 us)
Async XLA Ops:
  7.2 147.7 %all-gather.9.cloned.1.call-start = ((), (), s32[]{:S(2)}) async-start(), calls=%async_computation.3 | async-start | bytes 26738688 | tf_op jit(solution)/shard_map/all_gather | solution.py:734
  11.7 38.0 %all-to-all-start = ((bf16[16,2,2048]{2,1,0:T(2,128)(2,1)}), bf16[16,2,2048]{2,1,0:T(2,128)(2,1)S(1)}, u32[]{:S(2)}, u32[]{:S(2)}) async-start(bf16[16,2,2048]{2,1,0:T(2,128)(2,1)} %reshape.469), calls=%async_computation | async-start | bytes 262144 | tf_op jit(solution)/shard_map/all_to_all | solution.py:813
  49.7 35.8 %all-to-all-start.1 = ((bf16[16,42,192]{2,1,0:T(8,128)(2,1)}), bf16[16,42,192]{2,1,0:T(8,128)(2,1)S(1)}, u32[]{:S(2)}, u32[]{:S(2)}) async-start(bf16[16,42,192]{2,1,0:T(8,128)(2,1)} %bitcast.92), calls=%async_computation.1 | async-start | bytes 786432 | tf_op jit(solution)/shard_map/all_to_all | solution.py:798
  53.4 221.4 %all-gather.11.cloned.1.call-start = ((), (), s32[]{:S(2)}) async-start(), calls=%async_computation.4 | async-start | bytes 6127616 | tf_op jit(solution)/shard_map/all_gather | solution.py:734
  55.2 19.4 %collective-permute-start = (bf16[1,64,512]{2,1,0:T(8,128)(2,1)S(1)}, bf16[1,64,512]{2,1,0:T(8,128)(2,1)S(1)}, u32[]{:S(2)}, u32[]{:S(2)}) collective-permute-start(bf16[1,64,512]{2,1,0:T(8,128)(2,1)S(1)} %get-tuple-element.136), channel_id=1, source_target_pairs={{0,8},{1,9},{2,10},{3,11},{4,12},{5,13},{6,14},{7,15},{8,0},{9,1},... | collective-permute-start | bytes 196616 | tf_op jit(solution)/shard_map/ppermute | solution.py:817
  74.6 8.7 %collective-permute-start.1 = (bf16[2,64,512]{2,1,0:T(8,128)(2,1)S(1)}, bf16[2,64,512]{2,1,0:T(8,128)(2,1)S(1)}, u32[]{:S(2)}, u32[]{:S(2)}) collective-permute-start(bf16[2,64,512]{2,1,0:T(8,128)(2,1)S(1)} %pad_maximum_fusion.4), channel_id=1, source_target_pairs={{0,4},{1,5},{2,6},{3,7},{4,0},{5,1},{6,2},{7,3},{8,12},{9,13},{10,... | collective-permute-start | bytes 393224 | tf_op jit(solution)/shard_map/ppermute | solution.py:817
  84.0 14.2 %collective-permute-start.2 = (bf16[4,64,512]{2,1,0:T(8,128)(2,1)}, bf16[4,64,512]{2,1,0:T(8,128)(2,1)S(1)}, u32[]{:S(2)}, u32[]{:S(2)}) collective-permute-start(bf16[4,64,512]{2,1,0:T(8,128)(2,1)} %pad_maximum_fusion.2), channel_id=1, source_target_pairs={{0,2},{1,3},{2,0},{3,1},{4,6},{5,7},{6,4},{7,5},{8,10},{9,11},{10,... | collective-permute-start | bytes 786440 | tf_op jit(solution)/shard_map/ppermute | solution.py:817
  92.9 12.0 %collective-permute-start.4 = (bf16[8,48,1024]{2,1,0:T(8,128)(2,1)}, bf16[8,48,1024]{2,1,0:T(8,128)(2,1)S(1)}, u32[]{:S(2)}, u32[]{:S(2)}) collective-permute-start(bf16[8,48,1024]{2,1,0:T(8,128)(2,1)} %get-tuple-element.123), channel_id=1, source_target_pairs={{0,1},{1,0},{2,3},{3,2},{4,5},{5,4},{6,7},{7,6},{8,9},{9,8},{10,11... | collective-permute-start | bytes 2359304 | tf_op jit(solution)/shard_map/ppermute | solution.py:710
  170.7 141.3 %all-gather.13.cloned.1.call-start = ((), (), s32[]{:S(2)}) async-start(), calls=%async_computation.5 | async-start | bytes 4456448 | tf_op jit(solution)/shard_map/all_gather | solution.py:734
  170.7 37.3 %collective-permute-start.6 = (bf16[4,48,1024]{2,1,0:T(8,128)(2,1)}, bf16[4,48,1024]{2,1,0:T(8,128)(2,1)S(1)}, u32[]{:S(2)}, u32[]{:S(2)}) collective-permute-start(bf16[4,48,1024]{2,1,0:T(8,128)(2,1)} %gate.2), channel_id=1, source_target_pairs={{0,2},{1,3},{2,0},{3,1},{4,6},{5,7},{6,4},{7,5},{8,10},{9,11},{10,... | collective-permute-start | bytes 1179656 | tf_op jit(solution)/shard_map/ppermute | solution.py:710
  172.1 9.4 %collective-permute-start.5 = (bf16[128,1024]{1,0:T(8,128)(2,1)}, bf16[128,1024]{1,0:T(8,128)(2,1)S(1)}, u32[]{:S(2)}, u32[]{:S(2)}) collective-permute-start(bf16[128,1024]{1,0:T(8,128)(2,1)} %get-tuple-element.68.refs_1_), channel_id=1, source_target_pairs={{0,16},{1,17},{2,18},{3,19},{4,20},{5,21},{6,22},{7,23},{8,24},{9,... | collective-permute-start | bytes 786440 | tf_op jit(solution)/shard_map/ppermute | solution.py:862
  208.8 9.4 %collective-permute-start.7 = (bf16[128,1024]{1,0:T(8,128)(2,1)}, bf16[128,1024]{1,0:T(8,128)(2,1)S(1)}, u32[]{:S(2)}, u32[]{:S(2)}) collective-permute-start(bf16[128,1024]{1,0:T(8,128)(2,1)} %gate.3), channel_id=1, source_target_pairs={{16,0},{17,1},{18,2},{19,3},{20,4},{21,5},{22,6},{23,7},{24,8},{25... | collective-permute-start | bytes 786440 | tf_op jit(solution)/shard_map/ppermute | solution.py:883
  246.5 8.2 %collective-permute-start.10 = (bf16[8,64,2560]{2,1,0:T(8,128)(2,1)}, bf16[8,64,2560]{2,1,0:T(8,128)(2,1)S(1)}, u32[]{:S(2)}, u32[]{:S(2)}) collective-permute-start(bf16[8,64,2560]{2,1,0:T(8,128)(2,1)} %get-tuple-element.88), channel_id=1, source_target_pairs={{0,1},{1,0},{2,3},{3,2},{4,5},{5,4},{6,7},{7,6},{8,9},{9,8},{10,11... | collective-permute-start | bytes 7864328 | tf_op jit(solution)/shard_map/ppermute | solution.py:710
  246.6 16.9 %collective-permute-start.8 = (bf16[8,64,2560]{2,1,0:T(8,128)(2,1)}, bf16[8,64,2560]{2,1,0:T(8,128)(2,1)}, u32[]{:S(2)}, u32[]{:S(2)}) collective-permute-start(bf16[8,64,2560]{2,1,0:T(8,128)(2,1)} %get-tuple-element.85), channel_id=1, source_target_pairs={{0,1},{1,0},{2,3},{3,2},{4,5},{5,4},{6,7},{7,6},{8,9},{9,8},{10,11... | collective-permute-start | bytes 7864328 | tf_op jit(solution)/shard_map/ppermute | solution.py:710
  248.8 9.4 %collective-permute-start.9 = (bf16[2,48,1024]{2,1,0:T(8,128)(2,1)S(1)}, bf16[2,48,1024]{2,1,0:T(8,128)(2,1)S(1)}, u32[]{:S(2)}, u32[]{:S(2)}) collective-permute-start(bf16[2,48,1024]{2,1,0:T(8,128)(2,1)S(1)} %copy-done.11), channel_id=1, source_target_pairs={{0,4},{1,5},{2,6},{3,7},{4,0},{5,1},{6,2},{7,3},{8,12},{9,13},{10,... | collective-permute-start | bytes 589832 | tf_op jit(solution)/shard_map/ppermute | solution.py:710
  259.3 13.5 %collective-permute-start.11 = (bf16[1,48,1024]{2,1,0:T(8,128)(2,1)S(1)}, bf16[1,48,1024]{2,1,0:T(8,128)(2,1)S(1)}, u32[]{:S(2)}, u32[]{:S(2)}) collective-permute-start(bf16[1,48,1024]{2,1,0:T(8,128)(2,1)S(1)} %get-tuple-element.95), channel_id=1, source_target_pairs={{0,8},{1,9},{2,10},{3,11},{4,12},{5,13},{6,14},{7,15},{8,0},{9,1},... | collective-permute-start | bytes 294920 | tf_op jit(solution)/shard_map/ppermute | solution.py:710
  263.5 45.4 %collective-permute-start.14 = (bf16[4,64,2560]{2,1,0:T(8,128)(2,1)}, bf16[4,64,2560]{2,1,0:T(8,128)(2,1)S(1)}, u32[]{:S(2)}, u32[]{:S(2)}) collective-permute-start(bf16[4,64,2560]{2,1,0:T(8,128)(2,1)} %copy-done.7), channel_id=1, source_target_pairs={{0,4},{1,5},{2,6},{3,7},{4,0},{5,1},{6,2},{7,3},{8,12},{9,13},{10,... | collective-permute-start | bytes 3932168 | tf_op jit(solution)/shard_map/ppermute | solution.py:710
  269.0 31.7 %collective-permute-start.12 = (bf16[4,64,2560]{2,1,0:T(8,128)(2,1)}, bf16[4,64,2560]{2,1,0:T(8,128)(2,1)}, u32[]{:S(2)}, u32[]{:S(2)}) collective-permute-start(bf16[4,64,2560]{2,1,0:T(8,128)(2,1)} %get-tuple-element.86.refs_10_), channel_id=1, source_target_pairs={{0,2},{1,3},{2,0},{3,1},{4,6},{5,7},{6,4},{7,5},{8,10},{9,11},{10,... | collective-permute-start | bytes 3932168 | tf_op jit(solution)/shard_map/ppermute | solution.py:710
  292.8 43.3 %all-to-all-start.2 = ((f32[16,1,512]{2,1,0:T(1,128)}), f32[16,1,512]{2,1,0:T(1,128)S(1)}, u32[]{:S(2)}, u32[]{:S(2)}) async-start(f32[16,1,512]{2,1,0:T(1,128)} %reshape.471), calls=%async_computation.2 | async-start | bytes 65536 | tf_op jit(solution)/shard_map/all_to_all | solution.py:965
  303.7 36.0 %collective-permute-start.13 = (bf16[2,64,2560]{2,1,0:T(8,128)(2,1)}, bf16[2,64,2560]{2,1,0:T(8,128)(2,1)S(1)}, u32[]{:S(2)}, u32[]{:S(2)}) collective-permute-start(bf16[2,64,2560]{2,1,0:T(8,128)(2,1)} %get-tuple-element.100.refs_8_), channel_id=1, source_target_pairs={{0,4},{1,5},{2,6},{3,7},{4,0},{5,1},{6,2},{7,3},{8,12},{9,13},{10,... | collective-permute-start | bytes 1966088 | tf_op jit(solution)/shard_map/ppermute | solution.py:710
  309.8 31.5 %collective-permute-start.16 = (bf16[2,64,2560]{2,1,0:T(8,128)(2,1)}, bf16[2,64,2560]{2,1,0:T(8,128)(2,1)S(1)}, u32[]{:S(2)}, u32[]{:S(2)}) collective-permute-start(bf16[2,64,2560]{2,1,0:T(8,128)(2,1)} %get-tuple-element.103.refs_9_), channel_id=1, source_target_pairs={{0,8},{1,9},{2,10},{3,11},{4,12},{5,13},{6,14},{7,15},{8,0},{9,1},... | collective-permute-start | bytes 1966088 | tf_op jit(solution)/shard_map/ppermute | solution.py:710
  338.1 9.2 %collective-permute-start.19 = (bf16[2,64,1024]{2,1,0:T(8,128)(2,1)S(1)}, bf16[2,64,1024]{2,1,0:T(8,128)(2,1)S(1)}, u32[]{:S(2)}, u32[]{:S(2)}) collective-permute-start(bf16[2,64,1024]{2,1,0:T(8,128)(2,1)S(1)} %pad_maximum_fusion.3), channel_id=1, source_target_pairs={{0,2},{1,3},{2,0},{3,1},{4,6},{5,7},{6,4},{7,5},{8,10},{9,11},{10,... | collective-permute-start | bytes 786440 | tf_op jit(solution)/shard_map/ppermute | solution.py:960
  340.6 17.7 %collective-permute-start.15 = (bf16[1,64,2560]{2,1,0:T(8,128)(2,1)S(1)}, bf16[1,64,2560]{2,1,0:T(8,128)(2,1)S(1)}, u32[]{:S(2)}, u32[]{:S(2)}) collective-permute-start(bf16[1,64,2560]{2,1,0:T(8,128)(2,1)S(1)} %get-tuple-element.106.refs_4_), channel_id=1, source_target_pairs={{0,8},{1,9},{2,10},{3,11},{4,12},{5,13},{6,14},{7,15},{8,0},{9,1},... | collective-permute-start | bytes 983048 | tf_op jit(solution)/shard_map/ppermute | solution.py:710
  342.2 11.7 %collective-permute-start.17 = (bf16[1,64,2560]{2,1,0:T(8,128)(2,1)S(1)}, bf16[1,64,2560]{2,1,0:T(8,128)(2,1)S(1)}, u32[]{:S(2)}, u32[]{:S(2)}) collective-permute-start(bf16[1,64,2560]{2,1,0:T(8,128)(2,1)S(1)} %get-tuple-element.109), channel_id=1, source_target_pairs={{0,2},{1,3},{2,0},{3,1},{4,6},{5,7},{6,4},{7,5},{8,10},{9,11},{10,... | collective-permute-start | bytes 983048 | tf_op jit(solution)/shard_map/ppermute | solution.py:710
  (37 other events, 309.8 us)
Sparse Core Ops, SparseCore 0:
  10.7 144.1 all-gather.8
  170.8 59.7 all-gather.10
  232.8 56.2 all-gather.12
